TPU v7x, 512 devices: a whole 4x4x16 slice. The times are simulated.
512 devices in a mesh: sec: 32 (over y_hi, z), tile: 16 (over y_lo, x, core).
Axes of the slice: x: 4, y: 4 (y_hi: 2, y_lo: 2; y = y_hi * 2 + y_lo), z: 16, core: 2. Of those that a mesh axis runs over, the one named last changes fastest.
Arguments:
- image: bfloat16 [32, 4096, 1024], P('sec', 'tile'), may hold values from -6 to 6
- weight: bfloat16 [32, 4096, 1024], P('sec', 'tile'), may hold values from 0.25 to 4
- lens_filter_taps: float32 [32, 16, 25], P('sec', 'tile'), may hold values from -2 to 2
- block_src: int32 [32, 16, 16, 2], P('sec', 'tile'), may hold values from 0 to 15
- block_dst: int32 [32, 16, 16, 2], P('sec', None, 'tile'), may hold values from 0 to 15, as said below
- valid_count: int32 [32, 16, 16], P('sec', 'tile'), may hold values from 1 to 2, as said below
- anchor: bfloat16 [256, 128, 128], P('tile'), may hold values from -6 to 6
Outputs:
- correlation: float32 [32, 512, 128, 128], P('sec', 'tile')
Inputs may be any that keep to these rules, and one draw needn't show every extreme that they name: `block_dst`: every block of every strip receives at least one live slot. `valid_count`: in every section some strip receives 2 live slots from every tile; block_src and block_dst are 0 in slots at or beyond the valid count.
All inputs are finite; a program needn't handle non-finite values.
Results may differ from a plain program's by a relative error of at most 0.02.
Values may be sent and summed in bfloat16 or wider, within the bound.
No kernel may reach another device: no remote copies, remote signals or barrier semaphores. Data moves between devices by JAX's collectives and lax.ppermute only.
A program may use at most 64 MiB of HBM per device.

v0:
```python
import math

import jax
import jax.numpy as jnp
from jax import lax
from jax.sharding import PartitionSpec as P

B = 128
CAP = 2


def extended_2(block, sides, width):
    for axis, dim in sides:
        count = lax.axis_size(axis)
        forward = [(i, i + 1) for i in range(count - 1)]
        backward = [(target, source) for source, target in forward]
        low = lax.ppermute(
            lax.slice_in_dim(block, block.shape[dim] - width, None, axis=dim), axis, forward
        )
        high = lax.ppermute(lax.slice_in_dim(block, 0, width, axis=dim), axis, backward)
        block = jnp.concatenate([low, block, high], axis=dim)
    return block


def from_behind(value, axis, steps):
    count = lax.axis_size(axis)
    first, last = (max(0, -steps), min(count, count - steps))
    return lax.ppermute(value, axis, [(source, source + steps) for source in range(first, last)])


def window_set(strip_blocks, rim_block):
    extended = jnp.concatenate([strip_blocks, rim_block], 0)
    aligned = extended[:-1]
    half_shift = jnp.concatenate([extended[:-1, :, B // 2 :], extended[1:, :, : B // 2]], 2)
    return jnp.stack([aligned, half_shift], 1).reshape(-1, B, B)


def split_table(table):
    high = table.astype(jnp.bfloat16)
    low = (table - high.astype(jnp.float32)).astype(jnp.bfloat16)
    return (high, low)


def right_mult(data, halves):
    first = jnp.einsum("wjk,kl->wjl", data, halves[0], preferred_element_type=jnp.float32)
    return first + jnp.einsum("wjk,kl->wjl", data, halves[1], preferred_element_type=jnp.float32)


def left_mult(halves, data):
    first = jnp.einsum("jk,wkl->wjl", halves[0], data, preferred_element_type=jnp.float32)
    return first + jnp.einsum("jk,wkl->wjl", halves[1], data, preferred_element_type=jnp.float32)


def spectra(windows, tables):
    pair_right, pair_left = (tables[0], tables[1])
    right = right_mult(windows, pair_right).astype(jnp.bfloat16)
    from_cos = left_mult(pair_left, right[:, :, :B])
    from_sin = left_mult(pair_left, right[:, :, B:])
    spec_re = from_cos[:, :B] - from_sin[:, B:]
    spec_im = -(from_cos[:, B:] + from_sin[:, :B])
    return (spec_re, spec_im)


def body(image, weight, lens_filter_taps, block_src, block_dst, valid_count, anchor):
    rows_here = image.shape[1]
    cols_here = image.shape[2]
    strip_count = anchor.shape[0]
    padded = extended_2(image, (("tile", 1),), 2)[0]
    padded = jnp.pad(padded, ((0, 0), (2, 2)))
    kernel_taps = lens_filter_taps[0, 0]
    corrected = jnp.zeros((rows_here, cols_here), jnp.float32)
    for row_off in range(5):
        for col_off in range(5):
            corrected = corrected + kernel_taps[row_off * 5 + col_off] * padded[
                row_off : row_off + rows_here, col_off : col_off + cols_here
            ].astype(jnp.float32)
    weighted = (corrected * weight[0].astype(jnp.float32)).astype(jnp.bfloat16)
    tile_blocks = (
        weighted.reshape(rows_here // B, B, cols_here // B, B)
        .transpose(0, 2, 1, 3)
        .reshape(-1, B, B)
    )
    source_ids = block_src[0, 0]
    is_live = jnp.arange(CAP)[None, :] < valid_count[0, 0][:, None]
    picked = tile_blocks[source_ids]
    outgoing = jnp.where(is_live[:, :, None, None], picked, jnp.zeros_like(picked))
    incoming_blocks = lax.all_to_all(outgoing, "tile", split_axis=0, concat_axis=0, tiled=True)
    dest_ids = block_dst[0, :, 0, :]
    indicator_vector = (dest_ids[..., None] == jnp.arange(strip_count)[None, None, :]).astype(
        jnp.bfloat16
    )
    strip_blocks = jnp.einsum(
        "dbm,dbnh->mnh", indicator_vector, incoming_blocks, preferred_element_type=jnp.float32
    ).astype(jnp.bfloat16)
    own_rim, anchor_border = from_behind((strip_blocks[:1], anchor[:1]), "tile", -1)
    positions = jnp.arange(B, dtype=jnp.int32)
    product = positions[:, None] * positions[None, :] % B
    angle = product.astype(jnp.float32) * (2.0 * math.pi / B)
    cosine = jnp.cos(angle)
    sine_table = jnp.sin(angle)
    tables = (
        split_table(jnp.concatenate([cosine, sine_table], 1)),
        split_table(jnp.concatenate([cosine, sine_table], 0)),
    )
    is_first = lax.axis_index("sec") == 0
    current = spectra(window_set(strip_blocks, own_rim), tables)
    previous_section_blocks, prior_rim = from_behind((strip_blocks, own_rim), "sec", 1)
    previous_section_blocks = jnp.where(is_first, anchor, previous_section_blocks)
    prior_rim = jnp.where(is_first, anchor_border, prior_rim)
    earlier = spectra(window_set(previous_section_blocks, prior_rim), tables)
    cur_re, cur_im = current
    pre_re, pre_im = earlier
    cross_re = cur_re * pre_re + cur_im * pre_im
    cross_im = cur_im * pre_re - cur_re * pre_im
    magnitude = jnp.sqrt(cross_re * cross_re + cross_im * cross_im)
    mean_mag = jnp.mean(magnitude, axis=(1, 2), keepdims=True)
    denominator = magnitude + 0.1 * mean_mag + 1e-06
    whitened = jnp.concatenate([cross_re / denominator, cross_im / denominator], 2).astype(
        jnp.bfloat16
    )
    inverse_right = split_table(
        jnp.concatenate(
            [jnp.concatenate([cosine, sine_table], 1), jnp.concatenate([-sine_table, cosine], 1)], 0
        )
    )
    inverse_left = split_table(jnp.concatenate([cosine, -sine_table], 1))
    rows_both = right_mult(whitened, inverse_right).astype(jnp.bfloat16)
    stacked = jnp.concatenate([rows_both[:, :, :B], rows_both[:, :, B:]], 1)
    result = left_mult(inverse_left, stacked)
    return (result / B)[None]


def solution(mesh):
    in_specs = (
        P("sec", "tile", None),
        P("sec", "tile", None),
        P("sec", "tile", None),
        P("sec", "tile", None, None),
        P("sec", None, "tile", None),
        P("sec", "tile", None),
        P("tile", None, None),
    )
    out_specs = P("sec", "tile", None, None)
    return jax.shard_map(body, mesh=mesh, in_specs=in_specs, out_specs=out_specs, check_vma=False)
```

profile of v0, /device:TPU:24, one launch (start us, length us, event | category | flops | bytes accessed | tf_op | source)
XLA Modules:
  0.0 103.4 jit_solution(4491281840150544237)
XLA Ops:
  0.0 0.8 fusion.90
  0.8 1.9 %collective-permute-start = (bf16[1,2,1024]{2,1,0:T(2,128)(2,1)S(1)}, bf16[1,2,1024]{2,1,0:T(2,128)(2,1)S(1)}, u32[]{:S(2)}, u32[]{:S(2)}) collective-permute-start(bf16[1,2,1024]{2,1,0:T(2,128)(2,1)S(1)} %get-tuple-element.12), channel_id=1, source_target_pairs={{0,1},{1,2},{2,3},{3,4},{4,5},{5,6},{6,7},{7,8},{8,9},{9,10},{10,1... | collective-permute-start | bytes 12296 | tf_op jit(solution)/shard_map/ppermute | solution.py:17
  2.8 5.8 %collective-permute-start.1 = (bf16[1,2,1024]{2,1,0:T(2,128)(2,1)S(1)}, bf16[1,2,1024]{2,1,0:T(2,128)(2,1)S(1)}, u32[]{:S(2)}, u32[]{:S(2)}) collective-permute-start(bf16[1,2,1024]{2,1,0:T(2,128)(2,1)S(1)} %get-tuple-element.13), channel_id=1, source_target_pairs={{1,0},{2,1},{3,2},{4,3},{5,4},{6,5},{7,6},{8,7},{9,8},{10,9},{11,1... | collective-permute-start | bytes 12296 | tf_op jit(solution)/shard_map/ppermute | solution.py:20
  8.5 2.1 %fusion.91 = (f32[1,1,1]{2,1,0:T(1,128)}, f32[1,1,1]{2,1,0:T(1,128)}, f32[1,1,1]{2,1,0:T(1,128)}, f32[1,1,1]{2,1,0:T(1,128)}, f32[1,1,1]{2,1,0:T(1,128)}, /*inde...) fusion(f32[1,1,25]{2,1,0:T(1,128)} %param.9), kind=kLoop, calls=%fused_computation.141 | loop fusion | bytes 152 | tf_op jit(solution)/shard_map/slice | solution.py:74
  10.6 1.6 %fusion.92 = (f32[1,1,1]{2,1,0:T(1,128)}, f32[1,1,1]{2,1,0:T(1,128)}, f32[1,1,1]{2,1,0:T(1,128)}, f32[1,1,1]{2,1,0:T(1,128)}, f32[1,1,1]{2,1,0:T(1,128)}, /*index=5*/f32[1,1,1]{2,1,0:T(1,128)}) fusion(f32[1,1,25]{2,1,0:T(1,128)} %param.9), kind=kLoop, calls=%fused_computation.142 | loop fusion | bytes 48 | tf_op jit(solution)/shard_map/slice | solution.py:74
  12.2 1.1 %constant_dynamic-update-slice_fusion.1 = bf16[1,258,1024]{2,1,0:T(8,128)(2,1)S(1)} fusion(bf16[1,256,1024]{2,1,0:T(8,128)(2,1)} %param.7), kind=kLoop, calls=%fused_computation.124 | loop fusion | bytes 1048576
  13.2 0.7 compare_select_fusion
  13.9 0.1 copy.64
  14.0 0.1 reshape.148
  14.1 0.7 iota_compare_fusion.1
  14.8 0.0 collective-permute-done
  14.9 1.2 %maximum_bitcast_fusion = bf16[260,1024]{1,0:T(8,128)(2,1)S(1)} fusion(bf16[1,2,1024]{2,1,0:T(2,128)(2,1)S(1)} %collective-permute-done.1, bf16[1,256,1024]{2,1,0:T(8,128)(2,1)} %param.7, bf16[1,2,1024]{2,1,0:T(2,128)(2,1)S(1)} %collective-permute-done), kind=kLoop, calls=%fused_computation.67 | loop fusion | flops 1597440 | bytes 1064960 | tf_op jit(solution)/shard_map/squeeze | solution.py:68
  16.1 20.9 %fusion.41 = bf16[32,8,8,128]{3,1,2,0:T(8,128)(2,1)S(1)} fusion(bf16[1,256,1024]{2,1,0:T(8,128)(2,1)S(1)} %copy-done.2, f32[]{:T(128)} %bitcast.33, f32[]{:T(128)} %bitcast.32, bf16[1,258,1024]{2,1,0:T(8,128)(2,1)S(1)} %constant_dynamic-update-slice_fusion, f32[]{:T(128)} %bitcast.30, f32[]{:T(128)} %bitcast.29, f32[]{:T(128)} %bitcast.28, f32[]{:T(128)} %bitcast.27, ...), kind=kLoop, calls=%fused_computation.82 | loop fusion | flops 21757952 | bytes 3158116
  37.0 0.1 copy.97
  37.2 0.1 copy.63
  37.3 0.7 gather_fusion
  38.0 0.1 broadcast_select_fusion
  38.2 0.0 slice-start
  38.2 0.0 copy-start.3
  38.2 2.1 %copy.65 = bf16[16,2,128,128]{3,1,2,0:T(2,128)(2,1)} copy(bf16[16,2,128,128]{3,2,1,0:T(8,128)(2,1)S(1)} %broadcast_select_fusion) | data formatting | bytes 2097152 | tf_op jit(solution)/shard_map/jit(_where)/select_n | solution.py:86
  40.3 3.7 %all-to-all-start = ((bf16[16,2,128,128]{3,1,2,0:T(2,128)(2,1)}), bf16[16,2,128,128]{3,1,2,0:T(2,128)(2,1)S(1)}, u32[]{:S(2)}, u32[]{:S(2)}) async-start(bf16[16,2,128,128]{3,1,2,0:T(2,128)(2,1)} %copy.65), calls=%async_computation | async-start | bytes 2097152 | tf_op jit(solution)/shard_map/all_to_all | solution.py:87
  43.9 0.1 copy.101
  44.0 4.3 %collective-permute-start.4 = (bf16[1,128,128]{2,0,1:T(2,128)(2,1)S(1)}, bf16[1,128,128]{2,0,1:T(2,128)(2,1)S(1)}, u32[]{:S(2)}, u32[]{:S(2)}) collective-permute-start(bf16[1,128,128]{2,0,1:T(2,128)(2,1)S(1)} %copy.101), channel_id=1, source_target_pairs={{1,0},{2,1},{3,2},{4,3},{5,4},{6,5},{7,6},{8,7},{9,8},{10,9},{11,1... | collective-permute-start | bytes 98312 | tf_op jit(solution)/shard_map/ppermute | solution.py:28
  48.3 0.3 fusion.65
  48.6 10.4 %all-to-all-done = bf16[16,2,128,128]{3,1,2,0:T(2,128)(2,1)S(1)} async-done(((bf16[16,2,128,128]{3,1,2,0:T(2,128)(2,1)}), bf16[16,2,128,128]{3,1,2,0:T(2,128)(2,1)S(1)}, u32[]{:S(2)}, u32[]{:S(2)}) %all-to-all-start) | async-done | bytes 1048608 | tf_op jit(solution)/shard_map/all_to_all | solution.py:87
  59.0 0.7 fusion.2
  59.8 3.0 %collective-permute-start.2 = (bf16[1,128,128]{2,0,1:T(2,128)(2,1)S(1)}, bf16[1,128,128]{2,0,1:T(2,128)(2,1)S(1)}, u32[]{:S(2)}, u32[]{:S(2)}) collective-permute-start(bf16[1,128,128]{2,0,1:T(2,128)(2,1)S(1)} %slice.331), channel_id=1, source_target_pairs={{1,0},{2,1},{3,2},{4,3},{5,4},{6,5},{7,6},{8,7},{9,8},{10,9},{11,1... | collective-permute-start | bytes 98312 | tf_op jit(solution)/shard_map/ppermute | solution.py:28
  62.8 0.3 fusion.67
  63.1 0.2 slice.330
  63.3 3.8 %collective-permute-start.3 = (bf16[16,128,128]{2,0,1:T(8,128)(2,1)S(1)}, bf16[16,128,128]{2,0,1:T(8,128)(2,1)S(1)}, u32[]{:S(2)}, u32[]{:S(2)}) collective-permute-start(bf16[16,128,128]{2,0,1:T(8,128)(2,1)S(1)} %fusion.2), channel_id=1, source_target_pairs={{0,16},{16,32},{32,48},{48,64},{64,80},{80,96},{96,112},{112,128},... | collective-permute-start | bytes 1572872 | tf_op jit(solution)/shard_map/ppermute | solution.py:28
  67.1 0.0 collective-permute-done.2
  67.1 0.5 fusion.40
  67.6 0.1 pad_maximum_fusion.6
  67.7 0.3 copy.67
  68.0 0.7 fusion.74
  68.7 0.7 add_convert_fusion.2
  69.4 0.7 fusion.34
  70.2 0.7 fusion.31
  70.9 0.7 add_bitcast_fusion.3
  71.7 0.0 copy-start.1
  71.7 4.1 %collective-permute-start.5 = (bf16[1,128,128]{2,0,1:T(2,128)(2,1)S(1)}, bf16[1,128,128]{2,0,1:T(2,128)(2,1)S(1)}, u32[]{:S(2)}, u32[]{:S(2)}) collective-permute-start(bf16[1,128,128]{2,0,1:T(2,128)(2,1)S(1)} %collective-permute-done.2), channel_id=1, source_target_pairs={{0,16},{16,32},{32,48},{48,64},{64,80},{80,96},{96,112},{112,128},... | collective-permute-start | bytes 98312 | tf_op jit(solution)/shard_map/ppermute | solution.py:28
  75.8 0.7 add_bitcast_fusion.2
  76.6 11.7 %collective-permute-done.5 = bf16[1,128,128]{2,0,1:T(2,128)(2,1)S(1)} collective-permute-done((bf16[1,128,128]{2,0,1:T(2,128)(2,1)S(1)}, bf16[1,128,128]{2,0,1:T(2,128)(2,1)S(1)}, u32[]{:S(2)}, u32[]{:S(2)}) %collective-permute-start.5) | collective-permute-done | bytes 32800 | tf_op jit(solution)/shard_map/ppermute | solution.py:28
  88.2 0.1 broadcast_select_fusion.2
  88.3 0.0 collective-permute-done.3
  88.4 0.3 broadcast_select_fusion.1
  88.7 0.2 slice.336
  88.9 0.5 fusion.38
  89.4 0.1 pad_maximum_fusion.7
  89.5 0.3 copy.74
  89.8 0.7 fusion.72
  90.5 0.7 add_convert_fusion.1
  91.2 0.7 fusion.28
  91.9 0.7 fusion.25
  92.7 0.7 add_bitcast_fusion.1
  93.4 0.7 add_bitcast_fusion
  94.2 2.5 %fusion.3 = (f32[32]{0:T(128)S(1)}, f32[32,128,128]{1,2,0:T(8,128)S(1)}, f32[32,128,128]{1,2,0:T(8,128)S(1)}) fusion(f32[32,256,128]{1,2,0:T(8,128)S(1)} %add_bitcast_fusion, f32[32,256,128]{1,2,0:T(8,128)S(1)} %add_bitcast_fusion.1, f32[32,256,128]{1,2,0:T(8,128)S(1)} %add_bitcast_fusion.2, f32[32,256,128]{1,2,0:T(8,128)S(1)} %add_bitcast_fusion.3), kind=kLoop, calls=%fused_computation.25 | loop fusion | flops 8388576 | bytes 20971648 | tf_op jit(solution)/shard_map/reduce_sum | solution.py:116
  96.7 1.2 %divide_convert_fusion.1 = (bf16[32,128,128]{1,2,0:T(8,128)(2,1)S(1)}, bf16[32,128,128]{1,2,0:T(8,128)(2,1)S(1)}) fusion(f32[32,128,128]{1,2,0:T(8,128)S(1)} %get-tuple-element.6, f32[32,128,128]{1,2,0:T(8,128)S(1)} %get-tuple-element.7, f32[32]{0:T(128)S(1)} %broadcast_multiply_fusion), kind=kLoop, calls=%fused_computation.16 | loop fusion | flops 4718592 | bytes 6291584 | tf_op jit(solution)/shard_map/convert.1
  97.9 0.8 fusion.1
  98.7 0.8 add_convert_fusion
  99.4 0.6 fusion.89
  100.0 0.8 fusion
  100.8 0.8 multiply_bitcast_fusion
  101.6 1.8 %copy.83 = f32[1,32,128,128]{3,2,1,0:T(8,128)} copy(f32[1,32,128,128]{2,3,1,0:T(8,128)S(1)} %multiply_bitcast_fusion) | data formatting | bytes 4194304 | tf_op jit(solution)/shard_map/broadcast_in_dim | solution.py:130
  (16 shorter events, 0.1 us)
Async XLA Ops:
  0.0 16.1 %copy-start = (bf16[1,256,1024]{2,1,0:T(8,128)(2,1)S(1)}, bf16[1,256,1024]{2,1,0:T(8,128)(2,1)}, u32[]{:S(2)}) copy-start(bf16[1,256,1024]{2,1,0:T(8,128)(2,1)} %param.7) | copy-start | bytes 1572868
  0.0 16.1 %copy-start.2 = (bf16[1,256,1024]{2,1,0:T(8,128)(2,1)S(1)}, bf16[1,256,1024]{2,1,0:T(8,128)(2,1)}, u32[]{:S(2)}) copy-start(bf16[1,256,1024]{2,1,0:T(8,128)(2,1)} %param.8) | copy-start | bytes 1572868
  0.8 14.0 %collective-permute-start = (bf16[1,2,1024]{2,1,0:T(2,128)(2,1)S(1)}, bf16[1,2,1024]{2,1,0:T(2,128)(2,1)S(1)}, u32[]{:S(2)}, u32[]{:S(2)}) collective-permute-start(bf16[1,2,1024]{2,1,0:T(2,128)(2,1)S(1)} %get-tuple-element.12), channel_id=1, source_target_pairs={{0,1},{1,2},{2,3},{3,4},{4,5},{5,6},{6,7},{7,8},{8,9},{9,10},{10,1... | collective-permute-start | bytes 12296 | tf_op jit(solution)/shard_map/ppermute | solution.py:17
  2.8 12.1 %collective-permute-start.1 = (bf16[1,2,1024]{2,1,0:T(2,128)(2,1)S(1)}, bf16[1,2,1024]{2,1,0:T(2,128)(2,1)S(1)}, u32[]{:S(2)}, u32[]{:S(2)}) collective-permute-start(bf16[1,2,1024]{2,1,0:T(2,128)(2,1)S(1)} %get-tuple-element.13), channel_id=1, source_target_pairs={{1,0},{2,1},{3,2},{4,3},{5,4},{6,5},{7,6},{8,7},{9,8},{10,9},{11,1... | collective-permute-start | bytes 12296 | tf_op jit(solution)/shard_map/ppermute | solution.py:20
  38.2 5.7 %slice-start = ((bf16[16,128,128]{2,1,0:T(8,128)(2,1)}), bf16[1,128,128]{2,1,0:T(8,128)(2,1)S(1)}, s32[]{:S(2)}) async-start(bf16[16,128,128]{2,1,0:T(8,128)(2,1)} %param.13), calls=%async_computation.1 | async-start | bytes 65536 | tf_op jit(solution)/shard_map/slice | solution.py:95
  38.2 20.8 %copy-start.3 = (s32[1,16,1,2]{1,3,2,0:T(2,128)S(1)}, s32[1,16,1,2]{1,3,2,0:T(2,128)}, u32[]{:S(2)}) copy-start(s32[1,16,1,2]{1,3,2,0:T(2,128)} %param.11) | copy-start | bytes 388
  40.3 18.8 %all-to-all-start = ((bf16[16,2,128,128]{3,1,2,0:T(2,128)(2,1)}), bf16[16,2,128,128]{3,1,2,0:T(2,128)(2,1)S(1)}, u32[]{:S(2)}, u32[]{:S(2)}) async-start(bf16[16,2,128,128]{3,1,2,0:T(2,128)(2,1)} %copy.65), calls=%async_computation | async-start | bytes 2097152 | tf_op jit(solution)/shard_map/all_to_all | solution.py:87
  44.0 32.6 %collective-permute-start.4 = (bf16[1,128,128]{2,0,1:T(2,128)(2,1)S(1)}, bf16[1,128,128]{2,0,1:T(2,128)(2,1)S(1)}, u32[]{:S(2)}, u32[]{:S(2)}) collective-permute-start(bf16[1,128,128]{2,0,1:T(2,128)(2,1)S(1)} %copy.101), channel_id=1, source_target_pairs={{1,0},{2,1},{3,2},{4,3},{5,4},{6,5},{7,6},{8,7},{9,8},{10,9},{11,1... | collective-permute-start | bytes 98312 | tf_op jit(solution)/shard_map/ppermute | solution.py:28
  59.8 7.4 %collective-permute-start.2 = (bf16[1,128,128]{2,0,1:T(2,128)(2,1)S(1)}, bf16[1,128,128]{2,0,1:T(2,128)(2,1)S(1)}, u32[]{:S(2)}, u32[]{:S(2)}) collective-permute-start(bf16[1,128,128]{2,0,1:T(2,128)(2,1)S(1)} %slice.331), channel_id=1, source_target_pairs={{1,0},{2,1},{3,2},{4,3},{5,4},{6,5},{7,6},{8,7},{9,8},{10,9},{11,1... | collective-permute-start | bytes 98312 | tf_op jit(solution)/shard_map/ppermute | solution.py:28
  63.3 25.1 %collective-permute-start.3 = (bf16[16,128,128]{2,0,1:T(8,128)(2,1)S(1)}, bf16[16,128,128]{2,0,1:T(8,128)(2,1)S(1)}, u32[]{:S(2)}, u32[]{:S(2)}) collective-permute-start(bf16[16,128,128]{2,0,1:T(8,128)(2,1)S(1)} %fusion.2), channel_id=1, source_target_pairs={{0,16},{16,32},{32,48},{48,64},{64,80},{80,96},{96,112},{112,128},... | collective-permute-start | bytes 1572872 | tf_op jit(solution)/shard_map/ppermute | solution.py:28
  71.7 16.7 %copy-start.1 = (bf16[16,128,128]{2,1,0:T(8,128)(2,1)S(1)}, bf16[16,128,128]{2,1,0:T(8,128)(2,1)}, u32[]{:S(2)}) copy-start(bf16[16,128,128]{2,1,0:T(8,128)(2,1)} %param.13) | copy-start | bytes 1572868
  71.7 16.6 %collective-permute-start.5 = (bf16[1,128,128]{2,0,1:T(2,128)(2,1)S(1)}, bf16[1,128,128]{2,0,1:T(2,128)(2,1)S(1)}, u32[]{:S(2)}, u32[]{:S(2)}) collective-permute-start(bf16[1,128,128]{2,0,1:T(2,128)(2,1)S(1)} %collective-permute-done.2), channel_id=1, source_target_pairs={{0,16},{16,32},{32,48},{48,64},{64,80},{80,96},{96,112},{112,128},... | collective-permute-start | bytes 98312 | tf_op jit(solution)/shard_map/ppermute | solution.py:28
where the time goes:
time: 104 us; the launch traced here: 103 us
  other arithmetic  29.6 us (28%)
  starting transfers between devices  26.7 us (26%)
  waiting for transfers between devices  22.1 us (21%)
  matrix products  12.4 us (12%)
  local copies, waits for them, and re-layouts  12.2 us (12%)
    unnamed x1, other arithmetic  20.9 us
    ppermute x4, starting transfers between devices, from_behind(): lax.ppermute(value, axis, [(source, source + steps) for source in range(f...  15.3 us
    ppermute x4, waiting for transfers between devices, from_behind(): lax.ppermute(value, axis, [(source, source + steps) for source in range(f...  11.7 us
    all_to_all x1, waiting for transfers between devices, body(): lax.all_to_all(outgoing, 'tile', split_axis=0, concat_axis=0, tiled=True)  10.4 us
    ppermute x1, starting transfers between devices, extended_2(): lax.ppermute(lax.slice_in_dim(block, 0, width, axis=dim), axis, backward)  5.75 us
    dot_general x5, matrix products, left_mult(): jnp.einsum('jk,wkl->wjl', halves[1], data, preferred_element_type=jnp.flo...  3.73 us
    dot_general x5, matrix products, left_mult(): jnp.einsum('jk,wkl->wjl', halves[0], data, preferred_element_type=jnp.flo...  3.72 us
    all_to_all x1, starting transfers between devices, body(): lax.all_to_all(outgoing, 'tile', split_axis=0, concat_axis=0, tiled=True)  3.67 us
  transfers between devices with their start and end apart: 7, of which 2 were waited for; matrix products, arithmetic and copies ran while one was open for 13% of the time, Pallas kernels for 0%

commit v1 on v0

v1 whole, which is shorter than its diff:
```python
import jax
import jax.numpy as jnp
import numpy as np
from jax import lax
from jax.experimental import pallas as pl
from jax.experimental.pallas import tpu as pltpu
from jax.sharding import PartitionSpec as P

B = 128
H = B // 2
EDGE = 16
HALF = 8
F32 = jnp.float32
BF16 = jnp.bfloat16
VMEM_LIMIT = 48 * 2**20


def tables():
    j = np.arange(B)
    angle = (j[:, None] * j[None, :] % B) * (2.0 * np.pi / B)
    c, s = np.cos(angle), np.sin(angle)
    right = np.zeros((2 * B, 2 * B))
    for half, start in ((0, 0), (1, H)):
        right[start : start + B, half * H : half * H + H] = c[:, :H]
        right[start : start + B, B + half * H : B + half * H + H] = s[:, :H]
    left = np.block([[c, -s], [-s, -c]])
    q = np.arange((HALF + 1) * B)
    sign = 1.0 - 2.0 * (q % 2)
    middle = np.zeros(((HALF + 1) * B, B))
    for m in range(HALF):
        middle[:, m] = sign * (q // B == m)
        middle[:, H + m] = sign * ((q - H) // B == m)
    back_left = np.block([[c, -s], [s, c]])
    twice = np.where(j[:H] == 0, 1.0, 2.0)[:, None] / B
    back_right = np.zeros((2 * B, 2 * B))
    imag = -twice * s[:H]
    imag[0] = (1.0 - 2.0 * (j % 2)) / B
    for half in range(2):
        lanes = slice(half * B, half * B + B)
        back_right[half * H : half * H + H, lanes] = twice * c[:H]
        back_right[B + half * H : B + half * H + H, lanes] = imag
    return tuple(np.asarray(t, np.float32).astype(BF16) for t in (right, left, middle, back_left, back_right))


def dot(a, b):
    return jnp.dot(a, b, preferred_element_type=F32)


def shifted(x, off):
    rows = x.shape[0]
    if off == 0:
        return x
    gap = jnp.zeros((rows, abs(off)), x.dtype)
    if off > 0:
        return jnp.concatenate([x[:, off:], gap], 1)
    return jnp.concatenate([gap, x[:, :off]], 1)


def banded(taps_ref, which, valid):
    high, low = [], []
    for b in range(5):
        band = jnp.zeros(which.shape, F32)
        for a in range(5):
            band = jnp.where(which == a, taps_ref[0, 0, 5 * a + b], band)
        if valid is not None:
            band = jnp.where(valid, band, 0.0)
        top = band.astype(BF16)
        high.append(top)
        low.append((band - top.astype(F32)).astype(BF16))
    return jnp.concatenate([jnp.concatenate(high, 1), jnp.concatenate(low, 1)], 0)


def lens_kernel(taps_ref, x_ref, weight_ref, blocks_ref, edge_ref):
    x = x_ref[0]
    rows = x.shape[0]
    i = lax.broadcasted_iota(jnp.int32, (rows, rows), 0)
    j = lax.broadcasted_iota(jnp.int32, (rows, rows), 1)
    bands = banded(taps_ref, j - i + 2, None)
    stack = jnp.concatenate([shifted(x, b - 2) for b in range(5)], 0)
    both = dot(bands, stack)
    corrected = both[:rows] + both[rows:]
    edge_ref[:EDGE] = corrected[:EDGE]
    edge_ref[EDGE:] = corrected[rows - EDGE :]
    weighted = (corrected * weight_ref[0].astype(F32)).astype(BF16)
    across = x.shape[1] // B
    for k in range(blocks_ref.shape[0]):
        r, c = k // across * B, k % across * B
        blocks_ref[k] = weighted[r : r + B, c : c + B]


def pick_kernel(taps_ref, src_ref, count_ref, low_ref, high_ref, edge_ref, wtop_ref, wbot_ref, blocks_ref, out_ref, fix_ref):
    e = lax.broadcasted_iota(jnp.int32, (2 * EDGE, 2 * EDGE), 0)
    k = lax.broadcasted_iota(jnp.int32, (2 * EDGE, 2 * EDGE), 1)
    upper = (e < EDGE) & (k < EDGE)
    lower = (e >= EDGE) & (k >= EDGE)
    which = jnp.where(upper, k - (EDGE - 2) - e, k + (EDGE + 2) - e)
    bands = banded(taps_ref, which, upper | lower)
    rim = jnp.concatenate([low_ref[...], high_ref[...]], 0)
    stack = jnp.concatenate([shifted(rim, b - 2) for b in range(5)], 0)
    both = dot(bands, stack)
    corrected = edge_ref[...] + (both[: 2 * EDGE] + both[2 * EDGE :])
    top = (corrected[:EDGE] * wtop_ref[0].astype(F32)).astype(BF16)
    bottom = (corrected[EDGE:] * wbot_ref[0].astype(F32)).astype(BF16)
    count = blocks_ref.shape[0]
    across = count // 2
    for c in range(across):
        fix_ref[c] = top[:, c * B : c * B + B]
        fix_ref[across + c] = bottom[:, c * B : c * B + B]
    for d in range(out_ref.shape[0]):
        for q in range(out_ref.shape[1]):
            live = q < count_ref[0, 0, d]
            s = src_ref[0, 0, d, q]
            zero = jnp.zeros((), BF16)
            out_ref[d, q] = jnp.where(live, blocks_ref[s], zero)
            at = pl.multiple_of(jnp.where(s < across, 0, B - EDGE), EDGE)
            out_ref[d, q, pl.ds(at, EDGE), :] = jnp.where(live, fix_ref[s], zero)


def strip_kernel(dst_ref, in_ref, a_ref, b_ref, first_ref, acc_ref):
    acc_ref[...] = jnp.zeros_like(acc_ref)
    for d in range(in_ref.shape[0]):
        for q in range(in_ref.shape[1]):
            j = dst_ref[0, d, 0, q]
            acc_ref[j] = acc_ref[j] + in_ref[d, q].astype(F32)
    a_ref[...] = acc_ref[: HALF + 1].astype(BF16)
    b_ref[...] = acc_ref[HALF + 1 :].astype(BF16)
    first_ref[0] = acc_ref[0].astype(BF16)


def forward(blocks, right, left, middle):
    spectra = []
    for m in range(HALF):
        p = dot(jnp.concatenate([blocks[m], blocks[m + 1]], 1), right).astype(BF16)
        spectra.append(dot(left, jnp.concatenate([p[:, :B], p[:, B:]], 0)))
    p = dot(jnp.concatenate(blocks, 1), middle).astype(BF16)
    spectra.append(dot(left[:, :B], p))
    return spectra


def current_kernel(a_ref, b_ref, rim_ref, right_ref, left_ref, middle_ref, out_ref):
    blocks = [a_ref[m] for m in range(HALF + 1)] + [b_ref[m] for m in range(HALF - 1)] + [rim_ref[0]]
    for part in range(2):
        spectra = forward(blocks[part * HALF : part * HALF + HALF + 1], right_ref[...], left_ref[...], middle_ref[...])
        for m, f in enumerate(spectra):
            out_ref[part, m] = f.astype(BF16)


def correlate_chunk(cur_ref, part, blocks, right, left, middle, back_left, back_right, out_ref, cross_ref, mag_ref):
    lane = lax.broadcasted_iota(jnp.int32, (1, B), 1)
    twice = jnp.where(lane % H == 0, 1.0, 2.0)
    sums = []
    for m, f in enumerate(forward(blocks, right, left, middle)):
        c = cur_ref[part, m].astype(F32)
        ar, ai, br, bi = c[:B], c[B:], f[:B], f[B:]
        re = ar * br + ai * bi
        im = ai * br - ar * bi
        square = re * re + im * im
        mag = square * lax.rsqrt(jnp.maximum(square, 1e-30))
        cross_ref[m, :B] = re
        cross_ref[m, B:] = im
        mag_ref[m] = mag
        total = jnp.sum(mag, axis=0, keepdims=True)
        sums.append(total * twice if m < HALF else total)
    row = lax.broadcasted_iota(jnp.int32, (HALF, B), 0)
    lanes = lax.broadcasted_iota(jnp.int32, (HALF, B), 1)
    mine = row == lanes % H
    table = jnp.concatenate(sums[:HALF], 0) + jnp.where(mine, sums[HALF], 0.0)
    aligned = lanes < H
    first = jnp.sum(jnp.where(aligned, table, 0.0), axis=1, keepdims=True)
    second = jnp.sum(jnp.where(aligned, 0.0, table), axis=1, keepdims=True)
    floor = jnp.where(aligned, first, second) * (0.1 / (B * B)) + 1e-6
    floor_middle = jnp.sum(jnp.where(mine, floor, 0.0), axis=0, keepdims=True)
    floor_middle = jnp.where(lane % H < HALF, floor_middle, 1.0)

    def whitened(m, low):
        scale = 1.0 / (mag_ref[m] + low)
        return jnp.concatenate([cross_ref[m, :B] * scale, cross_ref[m, B:] * scale], 0).astype(BF16)

    y_middle = dot(back_left[:B], whitened(HALF, floor_middle))
    is_zero = lane % H == 0
    for m in range(HALF):
        y = dot(back_left, whitened(m, floor[m : m + 1]))
        turned = y_middle if m == 0 else pltpu.roll(y_middle, B - m, 1)
        imag = jnp.where(is_zero, turned, y[B:])
        result = dot(jnp.concatenate([y[:B].astype(BF16), imag.astype(BF16)], 1), back_right)
        out_ref[0, 2 * m] = result[:, :B]
        out_ref[0, 2 * m + 1] = result[:, B:]


def first_half_kernel(cur_ref, a_ref, anchor_ref, right, left, middle, back_left, back_right, out_ref, cross_ref, mag_ref):
    is_first = lax.axis_index("sec") == 0
    blocks = [jnp.where(is_first, anchor_ref[m], a_ref[m]) for m in range(HALF + 1)]
    correlate_chunk(cur_ref, 0, blocks, right[...], left[...], middle[...], back_left[...], back_right[...], out_ref, cross_ref, mag_ref)


def second_half_kernel(
    held_ref, cur_ref, a_ref, b_ref, rim_ref, anchor_ref, border_ref, right, left, middle, back_left, back_right, out_ref, cross_ref, mag_ref
):
    del held_ref
    is_first = lax.axis_index("sec") == 0
    blocks = [jnp.where(is_first, anchor_ref[HALF], a_ref[HALF])]
    blocks += [jnp.where(is_first, anchor_ref[HALF + 1 + m], b_ref[m]) for m in range(HALF - 1)]
    blocks += [jnp.where(is_first, border_ref[0], rim_ref[0])]
    correlate_chunk(cur_ref, 1, blocks, right[...], left[...], middle[...], back_left[...], back_right[...], out_ref, cross_ref, mag_ref)


SMEM = pl.BlockSpec(memory_space=pltpu.SMEM)
VMEM = pl.BlockSpec(memory_space=pltpu.VMEM)
ANY = pl.BlockSpec(memory_space=pl.ANY)


def call(kernel, out_shape, in_specs, out_specs, scratch, flops, moved, args, aliases=None, grid=None):
    extra = {} if grid is None else {"grid": grid}
    return pl.pallas_call(
        kernel,
        out_shape=out_shape,
        in_specs=in_specs,
        out_specs=out_specs,
        scratch_shapes=scratch,
        input_output_aliases=aliases or {},
        compiler_params=pltpu.CompilerParams(vmem_limit_bytes=VMEM_LIMIT),
        cost_estimate=pl.CostEstimate(flops=flops, bytes_accessed=moved, transcendentals=0),
        **extra,
    )(*args)


def body(image, weight, lens_filter_taps, block_src, block_dst, valid_count, anchor):
    rows, cols = image.shape[1:]
    strips = lax.axis_size("tile")
    sections = lax.axis_size("sec")
    slots = block_src.shape[-1]
    shape = jax.ShapeDtypeStruct
    forth = [(i, i + 1) for i in range(strips - 1)]
    back = [(i + 1, i) for i in range(strips - 1)]
    low = lax.ppermute(image[0, rows - EDGE :], "tile", forth)
    high = lax.ppermute(image[0, :EDGE], "tile", back)
    tile_blocks = rows // B * (cols // B)
    blocks, edge = call(
        lens_kernel,
        (shape((tile_blocks, B, B), BF16), shape((2 * EDGE, cols), F32)),
        [SMEM, VMEM, VMEM],
        (VMEM, VMEM),
        [],
        2 * 10 * rows * rows * cols,
        3 * 2 * rows * cols,
        (lens_filter_taps, image, weight),
    )
    edge_of = lambda index: pl.BlockSpec((1, EDGE, cols), lambda i: (0, index, 0))
    whole = lambda *dims: pl.BlockSpec(dims, lambda i: (0,) * len(dims))
    outgoing = call(
        pick_kernel,
        shape((strips, slots, B, B), BF16),
        [
            SMEM,
            SMEM,
            SMEM,
            whole(EDGE, cols),
            whole(EDGE, cols),
            whole(2 * EDGE, cols),
            edge_of(0),
            edge_of(rows // EDGE - 1),
            whole(tile_blocks, B, B),
        ],
        whole(strips, slots, B, B),
        [pltpu.VMEM((tile_blocks, EDGE, B), BF16)],
        2**20,
        4 * 2 * rows * cols,
        (lens_filter_taps, block_src, valid_count, low, high, edge, weight, weight, blocks),
        grid=(1,),
    )
    incoming = lax.all_to_all(outgoing, "tile", split_axis=0, concat_axis=0, tiled=True)
    border = lax.ppermute(anchor[:1], "tile", back)
    count = anchor.shape[0]
    part_a, part_b, first = call(
        strip_kernel,
        (shape((HALF + 1, B, B), BF16), shape((HALF - 1, B, B), BF16), shape((1, B, B), BF16)),
        [SMEM, VMEM],
        (VMEM, VMEM, VMEM),
        [pltpu.VMEM((count, B, B), F32)],
        2**20,
        4 * 2 * rows * cols,
        (block_dst, incoming),
    )
    on = [(i, i + 1) for i in range(sections - 1)]
    prior_a = lax.ppermute(part_a, "sec", on)
    prior_b = lax.ppermute(part_b, "sec", on)
    own_rim = lax.ppermute(first, "tile", back)
    across = [(s * strips + d + 1, (s + 1) * strips + d) for s in range(sections - 1) for d in range(strips - 1)]
    prior_rim = lax.ppermute(first, ("sec", "tile"), across)
    right, left, middle, back_left, back_right = (jnp.asarray(t) for t in tables())
    spectra = call(
        current_kernel,
        shape((2, HALF + 1, 2 * B, B), BF16),
        [VMEM] * 6,
        VMEM,
        [],
        2 * 16 * count * B**3,
        8 * count * B * B,
        (part_a, part_b, own_rim, right, left, middle),
    )
    windows = 2 * count
    scratch = [pltpu.VMEM((HALF + 1, 2 * B, B), F32), pltpu.VMEM((HALF + 1, B, B), F32)]
    half = lambda at: pl.BlockSpec((1, windows // 2, B, B), lambda i: (0, at, 0, 0))
    result = shape((1, windows, B, B), F32)
    t_specs = [whole(2 * B, 2 * B)] * 2 + [whole((HALF + 1) * B, B)] + [whole(2 * B, 2 * B)] * 2
    cur_spec = whole(2, HALF + 1, 2 * B, B)
    held = call(
        first_half_kernel,
        result,
        [cur_spec, whole(HALF + 1, B, B), whole(count, B, B)] + t_specs,
        half(0),
        scratch,
        2 * 16 * count * B**3,
        12 * count * B * B,
        (spectra, prior_a, anchor, right, left, middle, back_left, back_right),
        grid=(1,),
    )
    return call(
        second_half_kernel,
        result,
        [ANY, cur_spec, whole(HALF + 1, B, B), whole(HALF - 1, B, B), whole(1, B, B), whole(count, B, B), whole(1, B, B)] + t_specs,
        half(1),
        scratch,
        2 * 16 * count * B**3,
        12 * count * B * B,
        (held, spectra, prior_a, prior_b, prior_rim, anchor, border, right, left, middle, back_left, back_right),
        aliases={0: 0},
        grid=(1,),
    )


def solution(mesh):
    in_specs = (
        P("sec", "tile", None),
        P("sec", "tile", None),
        P("sec", "tile", None),
        P("sec", "tile", None, None),
        P("sec", None, "tile", None),
        P("sec", "tile", None),
        P("tile", None, None),
    )
    out_specs = P("sec", "tile", None, None)
    return jax.shard_map(body, mesh=mesh, in_specs=in_specs, out_specs=out_specs, check_vma=False)
```

time: 104 us -> 65.5 us (0.63)
  other arithmetic: 29.6 us -> 0 us
  Pallas kernels: 0 us -> 15.9 us
  matrix products: 12.4 us -> 0 us
  local copies, waits for them, and re-layouts: 12.2 us -> 3.73 us
  waiting for transfers between devices: 22.1 us -> 16.7 us
  starting transfers between devices: 26.7 us -> 28.2 us
    unnamed x1 -> x0, other arithmetic: 20.9 us -> none
    pallas_call x0 -> x6, Pallas kernels: none -> 15.9 us  [call(): pl.pallas_call(kernel, out_shape=out_shape, in_specs=in_specs, out_specs=...]
    dot_general x17 -> x0, matrix products: 12.4 us -> none  [the longest x5 3.73 us: left_mult(): jnp.einsum('jk,wkl->wjl', halves[1], data, preferred_element_type=jnp.flo...]
    ppermute x6 -> x7, waiting for transfers between devices: 11.7 us -> 1.7 us  [the longest x1 0.83 us: body(): prior_a = lax.ppermute(part_a, 'sec', on)]
    slice x9 -> x1, local copies, waits for them, and re-layouts: 5.5 us -> 0.01 us  [body(): border = lax.ppermute(anchor[:1], 'tile', back)]
    all_to_all x1, waiting for transfers between devices: 10.4 us -> 15 us  [body(): lax.all_to_all(outgoing, 'tile', split_axis=0, concat_axis=0, tiled=True)]
    reduce_sum x1 -> x0, other arithmetic: 2.49 us -> none  [body(): mean_mag = jnp.mean(magnitude, axis=(1, 2), keepdims=True)]
    another operation x5 -> x0, other arithmetic: 2.41 us -> none  [the longest x4 1.22 us: window_set(): return jnp.stack([aligned, half_shift], 1).reshape(-1, B, B)]
  transfers between devices with their start and end apart: 7 -> 8, of which waited for: 2 -> 4; matrix products, arithmetic and copies ran while one was open for 13% -> 0% of each run, Pallas kernels for 0% -> 13%
where the time goes in v1:
time: 65.5 us; the launch traced here: 64.8 us
  starting transfers between devices  28.2 us (43%)
  waiting for transfers between devices  16.7 us (25%)
  Pallas kernels  15.9 us (24%)
  local copies, waits for them, and re-layouts  3.73 us (6%)
    pallas_call x6, Pallas kernels, call(): pl.pallas_call(kernel, out_shape=out_shape, in_specs=in_specs, out_specs=...  15.9 us
    all_to_all x1, waiting for transfers between devices, body(): lax.all_to_all(outgoing, 'tile', split_axis=0, concat_axis=0, tiled=True)  15 us
    all_to_all x1, starting transfers between devices, body(): lax.all_to_all(outgoing, 'tile', split_axis=0, concat_axis=0, tiled=True)  5.54 us
    ppermute x1, starting transfers between devices, body(): high = lax.ppermute(image[0, :EDGE], 'tile', back)  4.27 us
    ppermute x1, starting transfers between devices, body(): prior_rim = lax.ppermute(first, ('sec', 'tile'), across)  4 us
    ppermute x1, starting transfers between devices, body(): prior_a = lax.ppermute(part_a, 'sec', on)  3.97 us
    ppermute x1, starting transfers between devices, body(): prior_b = lax.ppermute(part_b, 'sec', on)  3.82 us
    unnamed x30, local copies, waits for them, and re-layouts  2.95 us
  transfers between devices with their start and end apart: 8, of which 4 were waited for; matrix products, arithmetic and copies ran while one was open for 0% of the time, Pallas kernels for 13%

profile of v1, /device:TPU:24, one launch (start us, length us, event | category | flops | bytes accessed | tf_op | source)
XLA Modules:
  0.0 64.8 jit_solution(14396550008448144464)
XLA Ops:
  0.0 0.8 %slice_bitcast_fusion = (bf16[16,1024]{1,0:T(8,128)(2,1)S(1)}, bf16[16,1024]{1,0:T(8,128)(2,1)S(1)}) fusion(bf16[1,256,1024]{2,1,0:T(8,128)(2,1)} %x_ref.1), kind=kLoop, calls=%fused_computation | loop fusion | bytes 131072 | tf_op jit(solution)/shard_map/squeeze | solution.py:236
  0.8 4.3 %collective-permute-start.1 = (bf16[16,1024]{1,0:T(8,128)(2,1)S(1)}, bf16[16,1024]{1,0:T(8,128)(2,1)S(1)}, u32[]{:S(2)}, u32[]{:S(2)}) collective-permute-start(bf16[16,1024]{1,0:T(8,128)(2,1)S(1)} %get-tuple-element.15), channel_id=1, source_target_pairs={{1,0},{2,1},{3,2},{4,3},{5,4},{6,5},{7,6},{8,7},{9,8},{10,9},{11,1... | collective-permute-start | bytes 98312 | tf_op jit(solution)/shard_map/ppermute | solution.py:236
  5.1 1.9 %collective-permute-start = (bf16[16,1024]{1,0:T(8,128)(2,1)S(1)}, bf16[16,1024]{1,0:T(8,128)(2,1)S(1)}, u32[]{:S(2)}, u32[]{:S(2)}) collective-permute-start(bf16[16,1024]{1,0:T(8,128)(2,1)S(1)} %get-tuple-element.16), channel_id=1, source_target_pairs={{0,1},{1,2},{2,3},{3,4},{4,5},{5,6},{6,7},{7,8},{8,9},{9,10},{10,1... | collective-permute-start | bytes 98312 | tf_op jit(solution)/shard_map/ppermute | solution.py:235
  7.0 0.0 copy-start.1
  7.0 1.0 %copy-done.1 = bf16[1,256,1024]{2,1,0:T(8,128)(2,1)S(1)} copy-done((bf16[1,256,1024]{2,1,0:T(8,128)(2,1)S(1)}, bf16[1,256,1024]{2,1,0:T(8,128)(2,1)}, u32[]{:S(2)}) %copy-start.1) | copy-done | bytes 524312
  8.0 0.0 copy-start.8
  8.0 1.0 %copy-done.8 = bf16[1,256,1024]{2,1,0:T(8,128)(2,1)S(1)} copy-done((bf16[1,256,1024]{2,1,0:T(8,128)(2,1)S(1)}, bf16[1,256,1024]{2,1,0:T(8,128)(2,1)}, u32[]{:S(2)}) %copy-start.8) | copy-done | bytes 524312
  9.1 0.0 copy-start.9
  9.1 0.7 %copy-done.9 = f32[1,1,25]{2,1,0:T(1,128)S(1)} copy-done((f32[1,1,25]{2,1,0:T(1,128)S(1)}, f32[1,1,25]{2,1,0:T(1,128)}, u32[]{:S(2)}) %copy-start.9) | copy-done | bytes 124
  9.7 0.0 copy-start.12
  9.7 0.0 copy-start.2
  9.7 0.0 copy-start.10
  9.7 0.0 copy-start.11
  9.7 2.2 %shard_map.118 = (bf16[16,128,128]{2,1,0:T(8,128)(2,1)S(1)}, f32[32,1024]{1,0:T(8,128)S(1)}) custom-call(f32[1,1,25]{2,1,0:T(1,128)S(1)} %copy-done.9, bf16[1,256,1024]{2,1,0:T(8,128)(2,1)S(1)} %copy-done.8, bf16[1,256,1024]{2,1,0:T(8,128)(2,1)S(1)} %copy-done.1), custom_call_target="tpu_custom_call" | custom-call | flops 1342177280 | bytes 1572864 | tf_op jit(solution)/shard_map/pallas_call | solution.py:214
  12.0 0.0 copy-done.12
  12.0 0.1 copy.14.src_ref
  12.1 0.0 collective-permute-done.1.high_ref
  12.1 0.3 collective-permute-done.low_ref
  12.4 0.0 copy-done.2
  12.4 0.0 copy-done.10
  12.4 0.0 copy-done.11
  12.4 0.0 copy-start.13
  12.4 2.2 %shard_map.119 = bf16[16,2,128,128]{3,2,1,0:T(8,128)(2,1)} custom-call(f32[1,1,25]{2,1,0:T(1,128)S(1)} %copy-done.10, s32[1,1,16,2]{3,2,1,0:T(8,128)S(1)} %copy.14.src_ref, s32[1,1,16]{2,1,0:T(1,128)S(1)} %copy-done.11, bf16[16,1024]{1,0:T(8,128)(2,1)S(1)} %collective-permute-done.low_ref, bf16[16,1024]{1,0:T(8,128)(2,1)S(1)} %collective-permute-done.1.high_ref, ...), custom_call_target="tpu_custom_call" | custom-call | flops 1048576 | bytes 2097152 | tf_op jit(solution)/shard_map/pallas_call | solution.py:214
  14.6 0.0 copy-start
  14.6 0.0 copy-start.3
  14.6 0.0 copy-start.4
  14.6 0.0 copy-start.5
  14.6 5.5 %all-to-all-start = ((bf16[16,2,128,128]{3,2,1,0:T(8,128)(2,1)}), bf16[16,2,128,128]{3,2,1,0:T(8,128)(2,1)S(1)}, u32[]{:S(2)}, u32[]{:S(2)}) async-start(bf16[16,2,128,128]{3,2,1,0:T(8,128)(2,1)} %shard_map.119), calls=%async_computation | async-start | bytes 2097152 | tf_op jit(solution)/shard_map/all_to_all | solution.py:271
  20.2 0.0 copy-done.13
  20.2 0.1 copy.15.dst_ref
  20.2 15.0 %all-to-all-done.in_ref = bf16[16,2,128,128]{3,2,1,0:T(8,128)(2,1)S(1)} async-done(((bf16[16,2,128,128]{3,2,1,0:T(8,128)(2,1)}), bf16[16,2,128,128]{3,2,1,0:T(8,128)(2,1)S(1)}, u32[]{:S(2)}, u32[]{:S(2)}) %all-to-all-start) | async-done | bytes 1048608 | tf_op jit(solution)/shard_map/all_to_all | solution.py:271
  35.3 1.0 %shard_map.120 = (bf16[9,128,128]{2,1,0:T(8,128)(2,1)S(1)}, bf16[7,128,128]{2,1,0:T(8,128)(2,1)S(1)}, bf16[1,128,128]{2,1,0:T(8,128)(2,1)S(1)}) custom-call(s32[1,16,1,2]{3,2,1,0:T(1,128)S(1)} %copy.15.dst_ref, bf16[16,2,128,128]{3,2,1,0:T(8,128)(2,1)S(1)} %all-to-all-done.in_ref), custom_call_target="tpu_custom_call" | custom-call | flops 1048576 | bytes 2097152 | tf_op jit(solution)/shard_map/pallas_call | solution.py:214
  36.3 0.0 copy-start.6
  36.3 0.0 copy-start.7
  36.3 4.0 %collective-permute-start.3 = (bf16[9,128,128]{2,1,0:T(8,128)(2,1)S(1)}, bf16[9,128,128]{2,1,0:T(8,128)(2,1)S(1)}, u32[]{:S(2)}, u32[]{:S(2)}) collective-permute-start(bf16[9,128,128]{2,1,0:T(8,128)(2,1)S(1)} %get-tuple-element.12.a_ref), channel_id=1, source_target_pairs={{0,16},{16,32},{32,48},{48,64},{64,80},{80,96},{96,112},{112,128},... | collective-permute-start | bytes 884744 | tf_op jit(solution)/shard_map/ppermute | solution.py:285
  40.3 2.7 %collective-permute-start.2 = (bf16[1,128,128]{2,1,0:T(8,128)(2,1)S(1)}, bf16[1,128,128]{2,1,0:T(8,128)(2,1)S(1)}, u32[]{:S(2)}, u32[]{:S(2)}) collective-permute-start(bf16[1,128,128]{2,1,0:T(8,128)(2,1)S(1)} %get-tuple-element.14), channel_id=1, source_target_pairs={{1,0},{2,1},{3,2},{4,3},{5,4},{6,5},{7,6},{8,7},{9,8},{10,9},{11,1... | collective-permute-start | bytes 98312 | tf_op jit(solution)/shard_map/ppermute | solution.py:287
  43.0 3.8 %collective-permute-start.4 = (bf16[7,128,128]{2,1,0:T(8,128)(2,1)S(1)}, bf16[7,128,128]{2,1,0:T(8,128)(2,1)S(1)}, u32[]{:S(2)}, u32[]{:S(2)}) collective-permute-start(bf16[7,128,128]{2,1,0:T(8,128)(2,1)S(1)} %get-tuple-element.13.b_ref), channel_id=1, source_target_pairs={{0,16},{16,32},{32,48},{48,64},{64,80},{80,96},{96,112},{112,128},... | collective-permute-start | bytes 688136 | tf_op jit(solution)/shard_map/ppermute | solution.py:286
  46.9 0.0 copy-done
  46.9 1.9 %collective-permute-start.6 = (bf16[1,128,128]{2,1,0:T(8,128)(2,1)S(1)}, bf16[1,128,128]{2,1,0:T(8,128)(2,1)S(1)}, u32[]{:S(2)}, u32[]{:S(2)}) collective-permute-start(bf16[1,128,128]{2,1,0:T(8,128)(2,1)S(1)} %slice.11), channel_id=1, source_target_pairs={{1,0},{2,1},{3,2},{4,3},{5,4},{6,5},{7,6},{8,7},{9,8},{10,9},{11,1... | collective-permute-start | bytes 98312 | tf_op jit(solution)/shard_map/ppermute | solution.py:272
  48.8 4.0 %collective-permute-start.5 = (bf16[1,128,128]{2,1,0:T(8,128)(2,1)S(1)}, bf16[1,128,128]{2,1,0:T(8,128)(2,1)S(1)}, u32[]{:S(2)}, u32[]{:S(2)}) collective-permute-start(bf16[1,128,128]{2,1,0:T(8,128)(2,1)S(1)} %get-tuple-element.14), channel_id=1, source_target_pairs={{1,16},{2,17},{3,18},{4,19},{5,20},{6,21},{7,22},{8,23},{9,24},{10... | collective-permute-start | bytes 98312 | tf_op jit(solution)/shard_map/ppermute | solution.py:289
  52.8 0.0 collective-permute-done.2.rim_ref
  52.8 0.0 copy-done.3
  52.8 0.0 copy-done.4
  52.9 0.0 copy-done.5
  52.9 2.4 %shard_map.121.cur_ref = bf16[2,9,256,128]{3,2,1,0:T(8,128)(2,1)S(1)} custom-call(bf16[9,128,128]{2,1,0:T(8,128)(2,1)S(1)} %get-tuple-element.12.a_ref, bf16[7,128,128]{2,1,0:T(8,128)(2,1)S(1)} %get-tuple-element.13.b_ref, bf16[1,128,128]{2,1,0:T(8,128)(2,1)S(1)} %collective-permute-done.2.rim_ref, bf16[256,256]{1,0:T(8,128)(2,1)S(1)} %copy-done.5, ...), custom_call_target="tpu_custom_call" | custom-call | flops 1073741824 | bytes 2097152 | tf_op jit(solution)/shard_map/pallas_call | solution.py:214
  55.2 0.8 %collective-permute-done.3.a_ref = bf16[9,128,128]{2,1,0:T(8,128)(2,1)S(1)} collective-permute-done((bf16[9,128,128]{2,1,0:T(8,128)(2,1)S(1)}, bf16[9,128,128]{2,1,0:T(8,128)(2,1)S(1)}, u32[]{:S(2)}, u32[]{:S(2)}) %collective-permute-start.3) | collective-permute-done | bytes 294944 | tf_op jit(solution)/shard_map/ppermute | solution.py:285
  56.1 0.0 copy-done.6
  56.1 0.0 copy-done.7
  56.1 4.1 %shard_map.122.held_ref = f32[1,32,128,128]{3,2,1,0:T(8,128)} custom-call(bf16[2,9,256,128]{3,2,1,0:T(8,128)(2,1)S(1)} %shard_map.121.cur_ref, bf16[9,128,128]{2,1,0:T(8,128)(2,1)S(1)} %collective-permute-done.3.a_ref, bf16[16,128,128]{2,1,0:T(8,128)(2,1)S(1)} %copy-done, bf16[256,256]{1,0:T(8,128)(2,1)S(1)} %copy-done.5, bf16[256,256]{1,0:T(8,128)(2,1)S(1)} %copy-done.4, ...), custom_call_target="tpu_custom_call" | custom-call | flops 1073741824 | bytes 3145728 | tf_op jit(solution)/shard_map/pallas_call | solution.py:214
  60.1 0.0 collective-permute-done.6.border_ref
  60.1 0.0 collective-permute-done.5.rim_ref
  60.2 0.6 collective-permute-done.4.b_ref
  60.7 4.1 %shard_map.123 = f32[1,32,128,128]{3,2,1,0:T(8,128)} custom-call(f32[1,32,128,128]{3,2,1,0:T(8,128)} %shard_map.122.held_ref, bf16[2,9,256,128]{3,2,1,0:T(8,128)(2,1)S(1)} %shard_map.121.cur_ref, bf16[9,128,128]{2,1,0:T(8,128)(2,1)S(1)} %collective-permute-done.3.a_ref, ...), custom_call_target="tpu_custom_call", output_to_operand_aliasing={{}: (0, {})} | custom-call | flops 1073741824 | bytes 3145728 | tf_op jit(solution)/shard_map/pallas_call | solution.py:214
  (1 shorter events, 0.0 us)
Async XLA Ops:
  0.8 11.3 %collective-permute-start.1 = (bf16[16,1024]{1,0:T(8,128)(2,1)S(1)}, bf16[16,1024]{1,0:T(8,128)(2,1)S(1)}, u32[]{:S(2)}, u32[]{:S(2)}) collective-permute-start(bf16[16,1024]{1,0:T(8,128)(2,1)S(1)} %get-tuple-element.15), channel_id=1, source_target_pairs={{1,0},{2,1},{3,2},{4,3},{5,4},{6,5},{7,6},{8,7},{9,8},{10,9},{11,1... | collective-permute-start | bytes 98312 | tf_op jit(solution)/shard_map/ppermute | solution.py:236
  5.1 7.3 %collective-permute-start = (bf16[16,1024]{1,0:T(8,128)(2,1)S(1)}, bf16[16,1024]{1,0:T(8,128)(2,1)S(1)}, u32[]{:S(2)}, u32[]{:S(2)}) collective-permute-start(bf16[16,1024]{1,0:T(8,128)(2,1)S(1)} %get-tuple-element.16), channel_id=1, source_target_pairs={{0,1},{1,2},{2,3},{3,4},{4,5},{5,6},{6,7},{7,8},{8,9},{9,10},{10,1... | collective-permute-start | bytes 98312 | tf_op jit(solution)/shard_map/ppermute | solution.py:235
  7.0 1.0 %copy-start.1 = (bf16[1,256,1024]{2,1,0:T(8,128)(2,1)S(1)}, bf16[1,256,1024]{2,1,0:T(8,128)(2,1)}, u32[]{:S(2)}) copy-start(bf16[1,256,1024]{2,1,0:T(8,128)(2,1)} %wbot_ref.1) | copy-start | bytes 1572868
  8.0 1.0 %copy-start.8 = (bf16[1,256,1024]{2,1,0:T(8,128)(2,1)S(1)}, bf16[1,256,1024]{2,1,0:T(8,128)(2,1)}, u32[]{:S(2)}) copy-start(bf16[1,256,1024]{2,1,0:T(8,128)(2,1)} %x_ref.1) | copy-start | bytes 1572868
  9.1 0.7 %copy-start.9 = (f32[1,1,25]{2,1,0:T(1,128)S(1)}, f32[1,1,25]{2,1,0:T(1,128)}, u32[]{:S(2)}) copy-start(f32[1,1,25]{2,1,0:T(1,128)} %taps_ref.3) | copy-start | bytes 304
  9.7 2.3 %copy-start.12 = (s32[1,1,16,2]{2,3,1,0:T(2,128)S(1)}, s32[1,1,16,2]{2,3,1,0:T(2,128)}, u32[]{:S(2)}) copy-start(s32[1,1,16,2]{2,3,1,0:T(2,128)} %param.15) | copy-start | bytes 388
  9.7 2.7 %copy-start.2 = (bf16[1,256,1024]{2,1,0:T(8,128)(2,1)S(1)}, bf16[1,256,1024]{2,1,0:T(8,128)(2,1)}, u32[]{:S(2)}) copy-start(bf16[1,256,1024]{2,1,0:T(8,128)(2,1)} %wbot_ref.1) | copy-start | bytes 1572868
  9.7 2.7 %copy-start.10 = (f32[1,1,25]{2,1,0:T(1,128)S(1)}, f32[1,1,25]{2,1,0:T(1,128)}, u32[]{:S(2)}) copy-start(f32[1,1,25]{2,1,0:T(1,128)} %taps_ref.3) | copy-start | bytes 304
  9.7 2.7 %copy-start.11 = (s32[1,1,16]{2,1,0:T(1,128)S(1)}, s32[1,1,16]{2,1,0:T(1,128)}, u32[]{:S(2)}) copy-start(s32[1,1,16]{2,1,0:T(1,128)} %count_ref.1) | copy-start | bytes 196
  12.4 7.7 %copy-start.13 = (s32[1,16,1,2]{1,3,2,0:T(2,128)S(1)}, s32[1,16,1,2]{1,3,2,0:T(2,128)}, u32[]{:S(2)}) copy-start(s32[1,16,1,2]{1,3,2,0:T(2,128)} %param.16) | copy-start | bytes 388
  14.6 32.3 %copy-start = (bf16[16,128,128]{2,1,0:T(8,128)(2,1)S(1)}, bf16[16,128,128]{2,1,0:T(8,128)(2,1)}, u32[]{:S(2)}) copy-start(bf16[16,128,128]{2,1,0:T(8,128)(2,1)} %anchor_ref.3) | copy-start | bytes 1572868
  14.6 38.2 %copy-start.3 = (bf16[1152,128]{1,0:T(8,128)(2,1)S(1)}, bf16[1152,128]{1,0:T(8,128)(2,1)}, u32[]{:S(2)}) copy-start(bf16[1152,128]{1,0:T(8,128)(2,1)} %constant.12.clone.middle_ref.middle) | copy-start | bytes 884740
  14.6 38.2 %copy-start.4 = (bf16[256,256]{1,0:T(8,128)(2,1)S(1)}, bf16[256,256]{1,0:T(8,128)(2,1)}, u32[]{:S(2)}) copy-start(bf16[256,256]{1,0:T(8,128)(2,1)} %constant.11.clone.left_ref.left) | copy-start | bytes 393220
  14.6 38.2 %copy-start.5 = (bf16[256,256]{1,0:T(8,128)(2,1)S(1)}, bf16[256,256]{1,0:T(8,128)(2,1)}, u32[]{:S(2)}) copy-start(bf16[256,256]{1,0:T(8,128)(2,1)} %constant.10.clone.right_ref.right) | copy-start | bytes 393220
  14.6 20.7 %all-to-all-start = ((bf16[16,2,128,128]{3,2,1,0:T(8,128)(2,1)}), bf16[16,2,128,128]{3,2,1,0:T(8,128)(2,1)S(1)}, u32[]{:S(2)}, u32[]{:S(2)}) async-start(bf16[16,2,128,128]{3,2,1,0:T(8,128)(2,1)} %shard_map.119), calls=%async_computation | async-start | bytes 2097152 | tf_op jit(solution)/shard_map/all_to_all | solution.py:271
  36.3 19.8 %copy-start.6 = (bf16[256,256]{1,0:T(8,128)(2,1)S(1)}, bf16[256,256]{1,0:T(8,128)(2,1)}, u32[]{:S(2)}) copy-start(bf16[256,256]{1,0:T(8,128)(2,1)} %constant.14.clone.back_right) | copy-start | bytes 393220
  36.3 19.8 %copy-start.7 = (bf16[256,256]{1,0:T(8,128)(2,1)S(1)}, bf16[256,256]{1,0:T(8,128)(2,1)}, u32[]{:S(2)}) copy-start(bf16[256,256]{1,0:T(8,128)(2,1)} %constant.13.clone.back_left) | copy-start | bytes 393220
  36.3 19.8 %collective-permute-start.3 = (bf16[9,128,128]{2,1,0:T(8,128)(2,1)S(1)}, bf16[9,128,128]{2,1,0:T(8,128)(2,1)S(1)}, u32[]{:S(2)}, u32[]{:S(2)}) collective-permute-start(bf16[9,128,128]{2,1,0:T(8,128)(2,1)S(1)} %get-tuple-element.12.a_ref), channel_id=1, source_target_pairs={{0,16},{16,32},{32,48},{48,64},{64,80},{80,96},{96,112},{112,128},... | collective-permute-start | bytes 884744 | tf_op jit(solution)/shard_map/ppermute | solution.py:285
  40.3 12.5 %collective-permute-start.2 = (bf16[1,128,128]{2,1,0:T(8,128)(2,1)S(1)}, bf16[1,128,128]{2,1,0:T(8,128)(2,1)S(1)}, u32[]{:S(2)}, u32[]{:S(2)}) collective-permute-start(bf16[1,128,128]{2,1,0:T(8,128)(2,1)S(1)} %get-tuple-element.14), channel_id=1, source_target_pairs={{1,0},{2,1},{3,2},{4,3},{5,4},{6,5},{7,6},{8,7},{9,8},{10,9},{11,1... | collective-permute-start | bytes 98312 | tf_op jit(solution)/shard_map/ppermute | solution.py:287
  43.0 17.7 %collective-permute-start.4 = (bf16[7,128,128]{2,1,0:T(8,128)(2,1)S(1)}, bf16[7,128,128]{2,1,0:T(8,128)(2,1)S(1)}, u32[]{:S(2)}, u32[]{:S(2)}) collective-permute-start(bf16[7,128,128]{2,1,0:T(8,128)(2,1)S(1)} %get-tuple-element.13.b_ref), channel_id=1, source_target_pairs={{0,16},{16,32},{32,48},{48,64},{64,80},{80,96},{96,112},{112,128},... | collective-permute-start | bytes 688136 | tf_op jit(solution)/shard_map/ppermute | solution.py:286
  46.9 13.3 %collective-permute-start.6 = (bf16[1,128,128]{2,1,0:T(8,128)(2,1)S(1)}, bf16[1,128,128]{2,1,0:T(8,128)(2,1)S(1)}, u32[]{:S(2)}, u32[]{:S(2)}) collective-permute-start(bf16[1,128,128]{2,1,0:T(8,128)(2,1)S(1)} %slice.11), channel_id=1, source_target_pairs={{1,0},{2,1},{3,2},{4,3},{5,4},{6,5},{7,6},{8,7},{9,8},{10,9},{11,1... | collective-permute-start | bytes 98312 | tf_op jit(solution)/shard_map/ppermute | solution.py:272
  48.8 11.3 %collective-permute-start.5 = (bf16[1,128,128]{2,1,0:T(8,128)(2,1)S(1)}, bf16[1,128,128]{2,1,0:T(8,128)(2,1)S(1)}, u32[]{:S(2)}, u32[]{:S(2)}) collective-permute-start(bf16[1,128,128]{2,1,0:T(8,128)(2,1)S(1)} %get-tuple-element.14), channel_id=1, source_target_pairs={{1,16},{2,17},{3,18},{4,19},{5,20},{6,21},{7,22},{8,23},{9,24},{10... | collective-permute-start | bytes 98312 | tf_op jit(solution)/shard_map/ppermute | solution.py:289

commit v2 on v1

v2 whole, which is shorter than its diff:
```python
import jax
import jax.numpy as jnp
import numpy as np
from jax import lax
from jax.experimental import pallas as pl
from jax.experimental.pallas import tpu as pltpu
from jax.sharding import PartitionSpec as P

B = 128
H = B // 2
EDGE = 16
HALF = 8
F32 = jnp.float32
BF16 = jnp.bfloat16
VMEM_LIMIT = 48 * 2**20
PREPARE_VMEM_LIMIT = 54912 * 2**10


def tables():
    j = np.arange(B)
    angle = (j[:, None] * j[None, :] % B) * (2.0 * np.pi / B)
    c, s = np.cos(angle), np.sin(angle)
    right = np.zeros((2 * B, 2 * B))
    for half, start in ((0, 0), (1, H)):
        right[start : start + B, half * H : half * H + H] = c[:, :H]
        right[start : start + B, B + half * H : B + half * H + H] = s[:, :H]
    left = np.block([[c, -s], [-s, -c]])
    q = np.arange((HALF + 1) * B)
    sign = 1.0 - 2.0 * (q % 2)
    middle = np.zeros(((HALF + 1) * B, B))
    for m in range(HALF):
        middle[:, m] = sign * (q // B == m)
        middle[:, H + m] = sign * ((q - H) // B == m)
    back_left = np.block([[c, -s], [s, c]])
    twice = np.where(j[:H] == 0, 1.0, 2.0)[:, None] / B
    back_right = np.zeros((2 * B, 2 * B))
    imag = -twice * s[:H]
    imag[0] = (1.0 - 2.0 * (j % 2)) / B
    for half in range(2):
        lanes = slice(half * B, half * B + B)
        back_right[half * H : half * H + H, lanes] = twice * c[:H]
        back_right[B + half * H : B + half * H + H, lanes] = imag
    return tuple(np.asarray(t, np.float32).astype(BF16) for t in (right, left, middle, back_left, back_right))


def dot(a, b):
    return jnp.dot(a, b, preferred_element_type=F32)


def shifted(x, off):
    rows = x.shape[0]
    if off == 0:
        return x
    gap = jnp.zeros((rows, abs(off)), x.dtype)
    if off > 0:
        return jnp.concatenate([x[:, off:], gap], 1)
    return jnp.concatenate([gap, x[:, :off]], 1)


def banded(taps_ref, which, valid):
    high, low = [], []
    for b in range(5):
        band = jnp.zeros(which.shape, F32)
        for a in range(5):
            band = jnp.where(which == a, taps_ref[0, 0, 5 * a + b], band)
        if valid is not None:
            band = jnp.where(valid, band, 0.0)
        top = band.astype(BF16)
        high.append(top)
        low.append((band - top.astype(F32)).astype(BF16))
    return jnp.concatenate([jnp.concatenate(high, 1), jnp.concatenate(low, 1)], 0)


def prepare_kernel(image, last, head, sems):
    rows = image.shape[1]
    pairs = ((image.at[0, pl.ds(rows - EDGE, EDGE)], last), (image.at[0, pl.ds(0, EDGE)], head))
    copies = [pltpu.make_async_copy(whence, where, sems.at[n]) for n, (whence, where) in enumerate(pairs)]
    for copy in copies:
        copy.start()
    for copy in copies:
        copy.wait()


def front_kernel(
    taps_ref, src_ref, count_ref, low_ref, high_ref, image_ref, weight_ref, anchor, out, first, blocks_ref, keep_sem, out_sems
):
    keep_first = pltpu.make_async_copy(anchor.at[pl.ds(0, 1)], first, keep_sem)
    keep_first.start()
    x_ref = image_ref.at[0]
    rows, cols = x_ref.shape
    across = cols // B
    count = rows // B * across
    blocks_ref[count] = jnp.zeros((B, B), BF16)
    i = lax.broadcasted_iota(jnp.int32, (rows, rows), 0)
    j = lax.broadcasted_iota(jnp.int32, (rows, rows), 1)
    bands = banded(taps_ref, j - i + 2, None)
    e = lax.broadcasted_iota(jnp.int32, (2 * EDGE, 2 * EDGE), 0)
    k = lax.broadcasted_iota(jnp.int32, (2 * EDGE, 2 * EDGE), 1)
    upper = (e < EDGE) & (k < EDGE)
    lower = (e >= EDGE) & (k >= EDGE)
    which = jnp.where(upper, k - (EDGE - 2) - e, k + (EDGE + 2) - e)
    rim = jnp.concatenate([low_ref[...], high_ref[...]], 0)
    rims = jnp.concatenate([shifted(rim, b - 2) for b in range(5)], 0)
    edge = dot(banded(taps_ref, which, upper | lower), rims)
    edge = edge[: 2 * EDGE] + edge[2 * EDGE :]
    x = x_ref[...]
    stack = jnp.concatenate([shifted(x, b - 2) for b in range(5)], 0)
    both = dot(bands, stack)
    corrected = both[:rows] + both[rows:]
    corrected = jnp.concatenate(
        [corrected[:EDGE] + edge[:EDGE], corrected[EDGE : rows - EDGE], corrected[rows - EDGE :] + edge[EDGE:]], 0
    )
    weighted = (corrected * weight_ref[0].astype(F32)).astype(BF16)
    for k in range(count):
        r, c = k // across * B, k % across * B
        blocks_ref[k] = weighted[r : r + B, c : c + B]
    sends = []
    for d in range(out.shape[0]):
        for q in range(out.shape[1]):
            at = jnp.where(q < count_ref[0, 0, d], src_ref[0, 0, d, q], count)
            sends.append(pltpu.make_async_copy(blocks_ref.at[at], out.at[d, q], out_sems.at[d, q]))
            sends[-1].start()
    keep_first.wait()
    for send in sends:
        send.wait()


def strip_kernel(dst_ref, in_ref, a_ref, b_ref, first_ref, acc_ref):
    acc_ref[...] = jnp.zeros_like(acc_ref)
    for d in range(in_ref.shape[0]):
        for q in range(in_ref.shape[1]):
            j = dst_ref[0, d, 0, q]
            acc_ref[j] = acc_ref[j] + in_ref[d, q].astype(F32)
    a_ref[...] = acc_ref[: HALF + 1].astype(BF16)
    b_ref[: HALF - 1] = acc_ref[HALF + 1 :].astype(BF16)
    b_ref[HALF - 1] = jnp.zeros((B, B), BF16)
    first_ref[0] = acc_ref[0].astype(BF16)


def forward(blocks, right, left, middle):
    pairs = jnp.concatenate([jnp.concatenate([blocks[m], blocks[m + 1]], 1) for m in range(HALF)], 0)
    p = dot(pairs, right).astype(BF16)
    re = [p[m * B : m * B + B, :B] for m in range(HALF)]
    im = [p[m * B : m * B + B, B:] for m in range(HALF)]
    spectra = dot(left, jnp.concatenate([jnp.concatenate(re, 1), jnp.concatenate(im, 1)], 0))
    p = dot(jnp.concatenate(blocks, 1), middle).astype(BF16)
    return spectra, dot(left[:, :B], p)


def current_kernel(a_ref, b_ref, right_ref, left_ref, middle_ref, out_ref):
    blocks = [a_ref[m] for m in range(HALF + 1)] + [b_ref[m] for m in range(HALF)]
    for part in range(2):
        spectra, rest = forward(blocks[part * HALF : part * HALF + HALF + 1], right_ref[...], left_ref[...], middle_ref[...])
        out_ref[part, :, : HALF * B] = spectra.astype(BF16)
        out_ref[part, :, HALF * B :] = rest.astype(BF16)


def correlate_chunk(cur_ref, part, blocks, right, left, middle, back_left, back_right, out_ref, cross_ref, mag_ref):
    lane = lax.broadcasted_iota(jnp.int32, (1, B), 1)
    twice = jnp.where(lane % H == 0, 1.0, 2.0)
    sums = []
    spectra, rest = forward(blocks, right, left, middle)
    for m in range(HALF + 1):
        f = spectra[:, m * B : m * B + B] if m < HALF else rest
        c = cur_ref[part, :, m * B : m * B + B].astype(F32)
        ar, ai, br, bi = c[:B], c[B:], f[:B], f[B:]
        re = ar * br + ai * bi
        im = ai * br - ar * bi
        square = re * re + im * im
        mag = square * lax.rsqrt(jnp.maximum(square, 1e-30))
        cross_ref[m, :B] = re
        cross_ref[m, B:] = im
        mag_ref[m] = mag
        total = jnp.sum(mag, axis=0, keepdims=True)
        sums.append(total * twice if m < HALF else total)
    row = lax.broadcasted_iota(jnp.int32, (HALF, B), 0)
    lanes = lax.broadcasted_iota(jnp.int32, (HALF, B), 1)
    mine = row == lanes % H
    table = jnp.concatenate(sums[:HALF], 0) + jnp.where(mine, sums[HALF], 0.0)
    aligned = lanes < H
    first = jnp.sum(jnp.where(aligned, table, 0.0), axis=1, keepdims=True)
    second = jnp.sum(jnp.where(aligned, 0.0, table), axis=1, keepdims=True)
    floor = jnp.where(aligned, first, second) * (0.1 / (B * B)) + 1e-6
    floor_middle = jnp.sum(jnp.where(mine, floor, 0.0), axis=0, keepdims=True)
    floor_middle = jnp.where(lane % H < HALF, floor_middle, 1.0)

    def whitened(m, low):
        scale = 1.0 / (mag_ref[m] + low)
        return jnp.concatenate([cross_ref[m, :B] * scale, cross_ref[m, B:] * scale], 0).astype(BF16)

    y_middle = dot(back_left[:B], whitened(HALF, floor_middle))
    y = dot(back_left, jnp.concatenate([whitened(m, floor[m : m + 1]) for m in range(HALF)], 1))
    is_zero = lane % H == 0
    both = []
    for m in range(HALF):
        turned = y_middle if m == 0 else pltpu.roll(y_middle, B - m, 1)
        imag = jnp.where(is_zero, turned, y[B:, m * B : m * B + B])
        both.append(jnp.concatenate([y[:B, m * B : m * B + B].astype(BF16), imag.astype(BF16)], 1))
    result = dot(jnp.concatenate(both, 0), back_right)
    for m in range(HALF):
        out_ref[0, 2 * m] = result[m * B : m * B + B, :B]
        out_ref[0, 2 * m + 1] = result[m * B : m * B + B, B:]


def first_half_kernel(cur_ref, a_ref, anchor_ref, right, left, middle, back_left, back_right, out_ref, cross_ref, mag_ref):
    is_first = lax.axis_index("sec") == 0
    blocks = [jnp.where(is_first, anchor_ref[m], a_ref[m]) for m in range(HALF + 1)]
    correlate_chunk(cur_ref, 0, blocks, right[...], left[...], middle[...], back_left[...], back_right[...], out_ref, cross_ref, mag_ref)


def second_half_kernel(
    held_ref, cur_ref, a_ref, b_ref, anchor_ref, border_ref, right, left, middle, back_left, back_right, out_ref, cross_ref, mag_ref
):
    del held_ref
    is_first = lax.axis_index("sec") == 0
    blocks = [jnp.where(is_first, anchor_ref[HALF], a_ref[HALF])]
    blocks += [jnp.where(is_first, anchor_ref[HALF + 1 + m], b_ref[m]) for m in range(HALF - 1)]
    blocks += [jnp.where(is_first, border_ref[0], b_ref[HALF - 1])]
    correlate_chunk(cur_ref, 1, blocks, right[...], left[...], middle[...], back_left[...], back_right[...], out_ref, cross_ref, mag_ref)


SMEM = pl.BlockSpec(memory_space=pltpu.SMEM)
VMEM = pl.BlockSpec(memory_space=pltpu.VMEM)
ANY = pl.BlockSpec(memory_space=pl.ANY)
HBM = pl.BlockSpec(memory_space=pltpu.HBM)


def call(kernel, out_shape, in_specs, out_specs, scratch, flops, moved, args, aliases=None, grid=None, limit=VMEM_LIMIT):
    extra = {} if grid is None else {"grid": grid}
    return pl.pallas_call(
        kernel,
        out_shape=out_shape,
        in_specs=in_specs,
        out_specs=out_specs,
        scratch_shapes=scratch,
        input_output_aliases=aliases or {},
        compiler_params=pltpu.CompilerParams(vmem_limit_bytes=limit),
        cost_estimate=pl.CostEstimate(flops=flops, bytes_accessed=moved, transcendentals=0),
        **extra,
    )(*args)


def body(image, weight, lens_filter_taps, block_src, block_dst, valid_count, anchor):
    rows, cols = image.shape[1:]
    strips = lax.axis_size("tile")
    sections = lax.axis_size("sec")
    slots = block_src.shape[-1]
    count = anchor.shape[0]
    shape = jax.ShapeDtypeStruct
    whole = lambda *dims: pl.BlockSpec(dims, lambda i: (0,) * len(dims))
    forth = [(i, i + 1) for i in range(strips - 1)]
    back = [(i + 1, i) for i in range(strips - 1)]
    last, head = call(
        prepare_kernel,
        (shape((EDGE, cols), BF16), shape((EDGE, cols), BF16)),
        [HBM],
        (VMEM,) * 2,
        [pltpu.SemaphoreType.DMA((2,))],
        2**33,
        2**17,
        (image,),
        limit=PREPARE_VMEM_LIMIT,
    )
    low = lax.ppermute(last, "tile", forth)
    high = lax.ppermute(head, "tile", back)
    tile_blocks = rows // B * (cols // B)
    outgoing, anchor_first = call(
        front_kernel,
        (shape((strips, slots, B, B), BF16), shape((1, B, B), BF16)),
        [SMEM] * 3 + [VMEM] * 4 + [HBM],
        (HBM, HBM),
        [
            pltpu.VMEM((tile_blocks + 1, B, B), BF16),
            pltpu.SemaphoreType.DMA,
            pltpu.SemaphoreType.DMA((strips, slots)),
        ],
        2 * 10 * rows * rows * cols,
        4 * 2 * rows * cols,
        (lens_filter_taps, block_src, valid_count, low, high, image, weight, anchor),
    )
    incoming = lax.all_to_all(outgoing, "tile", split_axis=0, concat_axis=0, tiled=True)
    border = lax.ppermute(anchor_first, "tile", back)
    incoming, border = lax.optimization_barrier((incoming, border))
    part_a, part_b, first = call(
        strip_kernel,
        (shape((HALF + 1, B, B), BF16), shape((HALF, B, B), BF16), shape((1, B, B), BF16)),
        [SMEM, VMEM],
        (VMEM, VMEM, VMEM),
        [pltpu.VMEM((count, B, B), F32)],
        2**20,
        4 * 2 * rows * cols,
        (block_dst, incoming),
    )
    on = [(i, i + 1) for i in range(sections - 1)]
    prior_a = lax.ppermute(part_a, "sec", on)
    own_rim = lax.ppermute(first, "tile", back)
    part_b = lax.dynamic_update_slice(part_b, own_rim, (HALF - 1, 0, 0))
    prior_b = lax.ppermute(part_b, "sec", on)
    right, left, middle, back_left, back_right = (jnp.asarray(t) for t in tables())
    spectra = call(
        current_kernel,
        shape((2, 2 * B, (HALF + 1) * B), BF16),
        [VMEM] * 5,
        VMEM,
        [],
        2 * 16 * count * B**3,
        8 * count * B * B,
        (part_a, part_b, right, left, middle),
    )
    windows = 2 * count
    scratch = [pltpu.VMEM((HALF + 1, 2 * B, B), F32), pltpu.VMEM((HALF + 1, B, B), F32)]
    half = lambda at: pl.BlockSpec((1, windows // 2, B, B), lambda i: (0, at, 0, 0))
    result = shape((1, windows, B, B), F32)
    held = call(
        first_half_kernel,
        result,
        [VMEM] * 8,
        half(0),
        scratch,
        2 * 16 * count * B**3,
        12 * count * B * B,
        (spectra, prior_a, anchor, right, left, middle, back_left, back_right),
        grid=(1,),
    )
    return call(
        second_half_kernel,
        result,
        [ANY] + [VMEM] * 10,
        half(1),
        scratch,
        2 * 16 * count * B**3,
        12 * count * B * B,
        (held, spectra, prior_a, prior_b, anchor, border, right, left, middle, back_left, back_right),
        aliases={0: 0},
        grid=(1,),
    )


def solution(mesh):
    in_specs = (
        P("sec", "tile", None),
        P("sec", "tile", None),
        P("sec", "tile", None),
        P("sec", "tile", None, None),
        P("sec", None, "tile", None),
        P("sec", "tile", None),
        P("tile", None, None),
    )
    out_specs = P("sec", "tile", None, None)
    return jax.shard_map(body, mesh=mesh, in_specs=in_specs, out_specs=out_specs, check_vma=False)
```

time: 65.5 us -> 66.3 us (1.012)
  waiting for transfers between devices: 16.7 us -> 24.5 us
  Pallas kernels: 15.9 us -> 12 us
  local copies, waits for them, and re-layouts: 3.73 us -> 0.24 us
  starting transfers between devices: 28.2 us -> 29 us
    all_to_all x1, waiting for transfers between devices: 15 us -> 2.57 us  [body(): lax.all_to_all(outgoing, 'tile', split_axis=0, concat_axis=0, tiled=True)]
    ppermute x1, waiting for transfers between devices: 0.83 us -> 10.9 us  [body(): prior_a = lax.ppermute(part_a, 'sec', on)]
    ppermute x4 -> x3, waiting for transfers between devices: 0.32 us -> 9.59 us  [the longest x1 8.11 us: body(): border = lax.ppermute(anchor_first, 'tile', back)]
    pallas_call x6, Pallas kernels: 15.9 us -> 12 us  [call(): pl.pallas_call(kernel, out_shape=out_shape, in_specs=in_specs, out_specs=...]
    unnamed x30 -> x26, local copies, waits for them, and re-layouts: 2.95 us -> 0.23 us
    ppermute x1, waiting for transfers between devices: 0.56 us -> 1.4 us  [body(): prior_b = lax.ppermute(part_b, 'sec', on)]
    squeeze x1 -> x0, local copies, waits for them, and re-layouts: 0.78 us -> none  [body(): high = lax.ppermute(image[0, :EDGE], 'tile', back)]
    ppermute x1, starting transfers between devices: 2.74 us -> 3.51 us  [body(): own_rim = lax.ppermute(first, 'tile', back)]
  transfers between devices with their start and end apart: 8 -> 7, of which waited for: 4 -> 5; matrix products, arithmetic and copies ran while one was open for 0% -> 0% of each run, Pallas kernels for 13% -> 6%
where the time goes in v2:
time: 66.3 us; the launch traced here: 65.9 us
  starting transfers between devices  29 us (44%)
  waiting for transfers between devices  24.5 us (37%)
  Pallas kernels  12 us (18%)
    pallas_call x6, Pallas kernels, call(): pl.pallas_call(kernel, out_shape=out_shape, in_specs=in_specs, out_specs=...  12 us
    ppermute x1, waiting for transfers between devices, body(): prior_a = lax.ppermute(part_a, 'sec', on)  10.9 us
    ppermute x1, waiting for transfers between devices, body(): border = lax.ppermute(anchor_first, 'tile', back)  8.11 us
    all_to_all x1, starting transfers between devices, body(): lax.all_to_all(outgoing, 'tile', split_axis=0, concat_axis=0, tiled=True)  5.86 us
    ppermute x1, starting transfers between devices, body(): high = lax.ppermute(head, 'tile', back)  5.75 us
    ppermute x1, starting transfers between devices, body(): border = lax.ppermute(anchor_first, 'tile', back)  4.32 us
    ppermute x1, starting transfers between devices, body(): prior_a = lax.ppermute(part_a, 'sec', on)  3.83 us
    ppermute x1, starting transfers between devices, body(): prior_b = lax.ppermute(part_b, 'sec', on)  3.82 us
  transfers between devices with their start and end apart: 7, of which 5 were waited for; matrix products, arithmetic and copies ran while one was open for 0% of the time, Pallas kernels for 6%

profile of v2, /device:TPU:24, one launch (start us, length us, event | category | flops | bytes accessed | tf_op | source)
XLA Modules:
  0.0 65.9 jit_solution(795504033879403953)
XLA Ops:
  0.0 0.0 copy-start.6
  0.0 0.0 copy-start.10
  0.0 0.0 copy-start
  0.0 0.0 copy-start.9
  0.0 0.0 copy-start.8
  0.0 0.0 copy-start.7
  0.0 0.9 %shard_map.118 = (bf16[16,1024]{1,0:T(8,128)(2,1)S(1)}, bf16[16,1024]{1,0:T(8,128)(2,1)S(1)}) custom-call(bf16[1,256,1024]{2,1,0:T(8,128)(2,1)} %image_ref.1), custom_call_target="tpu_custom_call" | custom-call | flops 8589934592 | bytes 131072 | tf_op jit(solution)/shard_map/pallas_call | solution.py:230
  1.0 1.9 %collective-permute-start = (bf16[16,1024]{1,0:T(8,128)(2,1)S(1)}, bf16[16,1024]{1,0:T(8,128)(2,1)S(1)}, u32[]{:S(2)}, u32[]{:S(2)}) collective-permute-start(bf16[16,1024]{1,0:T(8,128)(2,1)S(1)} %get-tuple-element.14), channel_id=1, source_target_pairs={{0,1},{1,2},{2,3},{3,4},{4,5},{5,6},{6,7},{7,8},{8,9},{9,10},{10,1... | collective-permute-start | bytes 98312 | tf_op jit(solution)/shard_map/ppermute | solution.py:264
  2.9 5.8 %collective-permute-start.1 = (bf16[16,1024]{1,0:T(8,128)(2,1)S(1)}, bf16[16,1024]{1,0:T(8,128)(2,1)S(1)}, u32[]{:S(2)}, u32[]{:S(2)}) collective-permute-start(bf16[16,1024]{1,0:T(8,128)(2,1)S(1)} %get-tuple-element.15), channel_id=1, source_target_pairs={{1,0},{2,1},{3,2},{4,3},{5,4},{6,5},{7,6},{8,7},{9,8},{10,9},{11,1... | collective-permute-start | bytes 98312 | tf_op jit(solution)/shard_map/ppermute | solution.py:265
  8.6 0.0 copy-done.10
  8.6 0.1 copy.14.src_ref
  8.7 0.0 collective-permute-done.low_ref
  8.7 1.5 %collective-permute-done.1.high_ref = bf16[16,1024]{1,0:T(8,128)(2,1)S(1)} collective-permute-done((bf16[16,1024]{1,0:T(8,128)(2,1)S(1)}, bf16[16,1024]{1,0:T(8,128)(2,1)S(1)}, u32[]{:S(2)}, u32[]{:S(2)}) %collective-permute-start.1) | collective-permute-done | bytes 32800 | tf_op jit(solution)/shard_map/ppermute | solution.py:265
  10.2 0.0 copy-done.6
  10.2 0.0 copy-done
  10.2 0.0 copy-done.9
  10.2 0.0 copy-done.8
  10.2 0.0 copy-done.7
  10.2 3.7 %shard_map.119 = (bf16[16,2,128,128]{3,2,1,0:T(8,128)(2,1)}, bf16[1,128,128]{2,1,0:T(8,128)(2,1)S(1)}) custom-call(f32[1,1,25]{2,1,0:T(1,128)S(1)} %copy-done.8, s32[1,1,16,2]{3,2,1,0:T(8,128)S(1)} %copy.14.src_ref, s32[1,1,16]{2,1,0:T(1,128)S(1)} %copy-done.9, bf16[16,1024]{1,0:T(8,128)(2,1)S(1)} %collective-permute-done.low_ref, ...), custom_call_target="tpu_custom_call" | custom-call | flops 1342177280 | bytes 2097152 | tf_op jit(solution)/shard_map/pallas_call | solution.py:230
  14.0 0.0 copy-start.11
  14.0 0.0 copy-start.1
  14.0 0.0 copy-start.2
  14.0 0.0 copy-start.3
  14.0 5.9 %all-to-all-start = ((bf16[16,2,128,128]{3,2,1,0:T(8,128)(2,1)}), bf16[16,2,128,128]{3,2,1,0:T(8,128)(2,1)S(1)}, u32[]{:S(2)}, u32[]{:S(2)}) async-start(bf16[16,2,128,128]{3,2,1,0:T(8,128)(2,1)} %get-tuple-element.16), calls=%async_computation | async-start | bytes 2097152 | tf_op jit(solution)/shard_map/all_to_all | solution.py:281
  19.9 4.3 %collective-permute-start.2 = (bf16[1,128,128]{2,1,0:T(8,128)(2,1)S(1)}, bf16[1,128,128]{2,1,0:T(8,128)(2,1)S(1)}, u32[]{:S(2)}, u32[]{:S(2)}) collective-permute-start(bf16[1,128,128]{2,1,0:T(8,128)(2,1)S(1)} %get-tuple-element.17), channel_id=1, source_target_pairs={{1,0},{2,1},{3,2},{4,3},{5,4},{6,5},{7,6},{8,7},{9,8},{10,9},{11,1... | collective-permute-start | bytes 98312 | tf_op jit(solution)/shard_map/ppermute | solution.py:282
  24.2 0.0 copy-done.11
  24.2 0.1 copy.15.dst_ref
  24.3 8.1 %collective-permute-done.2.border_ref = bf16[1,128,128]{2,1,0:T(8,128)(2,1)S(1)} collective-permute-done((bf16[1,128,128]{2,1,0:T(8,128)(2,1)S(1)}, bf16[1,128,128]{2,1,0:T(8,128)(2,1)S(1)}, u32[]{:S(2)}, u32[]{:S(2)}) %collective-permute-start.2) | collective-permute-done | bytes 32800 | tf_op jit(solution)/shard_map/ppermute | solution.py:282
  32.4 2.6 %all-to-all-done.in_ref = bf16[16,2,128,128]{3,2,1,0:T(8,128)(2,1)S(1)} async-done(((bf16[16,2,128,128]{3,2,1,0:T(8,128)(2,1)}), bf16[16,2,128,128]{3,2,1,0:T(8,128)(2,1)S(1)}, u32[]{:S(2)}, u32[]{:S(2)}) %all-to-all-start) | async-done | bytes 1048608 | tf_op jit(solution)/shard_map/all_to_all | solution.py:281
  35.0 1.0 %shard_map.120 = (bf16[9,128,128]{2,1,0:T(8,128)(2,1)S(1)}, bf16[8,128,128]{2,1,0:T(8,128)(2,1)S(1)}, bf16[1,128,128]{2,1,0:T(8,128)(2,1)S(1)}) custom-call(s32[1,16,1,2]{3,2,1,0:T(1,128)S(1)} %copy.15.dst_ref, bf16[16,2,128,128]{3,2,1,0:T(8,128)(2,1)S(1)} %all-to-all-done.in_ref), custom_call_target="tpu_custom_call" | custom-call | flops 1048576 | bytes 2097152 | tf_op jit(solution)/shard_map/pallas_call | solution.py:230
  36.0 0.0 copy-start.4
  36.0 0.0 copy-start.5
  36.0 3.5 %collective-permute-start.3 = (bf16[1,128,128]{2,1,0:T(8,128)(2,1)S(1)}, bf16[1,128,128]{2,1,0:T(8,128)(2,1)S(1)}, u32[]{:S(2)}, u32[]{:S(2)}) collective-permute-start(bf16[1,128,128]{2,1,0:T(8,128)(2,1)S(1)} %get-tuple-element.21), channel_id=1, source_target_pairs={{1,0},{2,1},{3,2},{4,3},{5,4},{6,5},{7,6},{8,7},{9,8},{10,9},{11,1... | collective-permute-start | bytes 98312 | tf_op jit(solution)/shard_map/ppermute | solution.py:296
  39.6 3.8 %collective-permute-start.4 = (bf16[9,128,128]{2,1,0:T(8,128)(2,1)S(1)}, bf16[9,128,128]{2,1,0:T(8,128)(2,1)S(1)}, u32[]{:S(2)}, u32[]{:S(2)}) collective-permute-start(bf16[9,128,128]{2,1,0:T(8,128)(2,1)S(1)} %get-tuple-element.19.a_ref), channel_id=1, source_target_pairs={{0,16},{16,32},{32,48},{48,64},{64,80},{80,96},{96,112},{112,128},... | collective-permute-start | bytes 884744 | tf_op jit(solution)/shard_map/ppermute | solution.py:295
  43.4 0.0 collective-permute-done.3
  43.4 3.8 %collective-permute-start.5 = (bf16[8,128,128]{2,1,0:T(8,128)(2,1)S(1)}, bf16[8,128,128]{2,1,0:T(8,128)(2,1)S(1)}, u32[]{:S(2)}, u32[]{:S(2)}) collective-permute-start(bf16[8,128,128]{2,1,0:T(8,128)(2,1)S(1)} %constant_dynamic-update-slice_fusion.b_ref), channel_id=1, source_target_pairs={{0,16},{16,32},{32,48},{48,64},{64,80},{80,96},{96,112},{112,128},... | collective-permute-start | bytes 786440 | tf_op jit(solution)/shard_map/ppermute | solution.py:298
  47.3 0.0 copy-done.1
  47.3 0.0 copy-done.2
  47.3 0.0 copy-done.3
  47.3 1.3 %shard_map.121.cur_ref = bf16[2,256,1152]{2,1,0:T(8,128)(2,1)S(1)} custom-call(bf16[9,128,128]{2,1,0:T(8,128)(2,1)S(1)} %get-tuple-element.19.a_ref, bf16[8,128,128]{2,1,0:T(8,128)(2,1)S(1)} %constant_dynamic-update-slice_fusion.b_ref, bf16[256,256]{1,0:T(8,128)(2,1)S(1)} %copy-done.3, bf16[256,256]{1,0:T(8,128)(2,1)S(1)} %copy-done.2, ...), custom_call_target="tpu_custom_call" | custom-call | flops 1073741824 | bytes 2097152 | tf_op jit(solution)/shard_map/pallas_call | solution.py:230
  48.6 10.9 %collective-permute-done.4.a_ref = bf16[9,128,128]{2,1,0:T(8,128)(2,1)S(1)} collective-permute-done((bf16[9,128,128]{2,1,0:T(8,128)(2,1)S(1)}, bf16[9,128,128]{2,1,0:T(8,128)(2,1)S(1)}, u32[]{:S(2)}, u32[]{:S(2)}) %collective-permute-start.4) | collective-permute-done | bytes 294944 | tf_op jit(solution)/shard_map/ppermute | solution.py:295
  59.6 0.0 copy-done.4
  59.6 0.0 copy-done.5
  59.6 2.5 %shard_map.122.held_ref = f32[1,32,128,128]{3,2,1,0:T(8,128)} custom-call(bf16[2,256,1152]{2,1,0:T(8,128)(2,1)S(1)} %shard_map.121.cur_ref, bf16[9,128,128]{2,1,0:T(8,128)(2,1)S(1)} %collective-permute-done.4.a_ref, bf16[16,128,128]{2,1,0:T(8,128)(2,1)S(1)} %copy-done, bf16[256,256]{1,0:T(8,128)(2,1)S(1)} %copy-done.3, bf16[256,256]{1,0:T(8,128)(2,1)S(1)} %copy-done.2, ...), custom_call_target="tpu_custom_call" | custom-call | flops 1073741824 | bytes 3145728 | tf_op jit(solution)/shard_map/pallas_call | solution.py:230
  62.1 1.4 %collective-permute-done.5.b_ref = bf16[8,128,128]{2,1,0:T(8,128)(2,1)S(1)} collective-permute-done((bf16[8,128,128]{2,1,0:T(8,128)(2,1)S(1)}, bf16[8,128,128]{2,1,0:T(8,128)(2,1)S(1)}, u32[]{:S(2)}, u32[]{:S(2)}) %collective-permute-start.5) | collective-permute-done | bytes 262176 | tf_op jit(solution)/shard_map/ppermute | solution.py:298
  63.5 2.5 %shard_map.123 = f32[1,32,128,128]{3,2,1,0:T(8,128)} custom-call(f32[1,32,128,128]{3,2,1,0:T(8,128)} %shard_map.122.held_ref, bf16[2,256,1152]{2,1,0:T(8,128)(2,1)S(1)} %shard_map.121.cur_ref, bf16[9,128,128]{2,1,0:T(8,128)(2,1)S(1)} %collective-permute-done.4.a_ref, ...), custom_call_target="tpu_custom_call", output_to_operand_aliasing={{}: (0, {})} | custom-call | flops 1073741824 | bytes 3145728 | tf_op jit(solution)/shard_map/pallas_call | solution.py:230
  (1 shorter events, 0.0 us)
Async XLA Ops:
  0.0 10.2 %copy-start.6 = (bf16[1,256,1024]{2,1,0:T(8,128)(2,1)S(1)}, bf16[1,256,1024]{2,1,0:T(8,128)(2,1)}, u32[]{:S(2)}) copy-start(bf16[1,256,1024]{2,1,0:T(8,128)(2,1)} %image_ref.1) | copy-start | bytes 1572868
  0.0 8.6 %copy-start.10 = (s32[1,1,16,2]{2,3,1,0:T(2,128)S(1)}, s32[1,1,16,2]{2,3,1,0:T(2,128)}, u32[]{:S(2)}) copy-start(s32[1,1,16,2]{2,3,1,0:T(2,128)} %param.15) | copy-start | bytes 388
  0.0 10.2 %copy-start = (bf16[16,128,128]{2,1,0:T(8,128)(2,1)S(1)}, bf16[16,128,128]{2,1,0:T(8,128)(2,1)}, u32[]{:S(2)}) copy-start(bf16[16,128,128]{2,1,0:T(8,128)(2,1)} %anchor_ref.3) | copy-start | bytes 1572868
  0.0 10.2 %copy-start.9 = (s32[1,1,16]{2,1,0:T(1,128)S(1)}, s32[1,1,16]{2,1,0:T(1,128)}, u32[]{:S(2)}) copy-start(s32[1,1,16]{2,1,0:T(1,128)} %count_ref.1) | copy-start | bytes 196
  0.0 10.2 %copy-start.8 = (f32[1,1,25]{2,1,0:T(1,128)S(1)}, f32[1,1,25]{2,1,0:T(1,128)}, u32[]{:S(2)}) copy-start(f32[1,1,25]{2,1,0:T(1,128)} %taps_ref.1) | copy-start | bytes 304
  0.0 10.2 %copy-start.7 = (bf16[1,256,1024]{2,1,0:T(8,128)(2,1)S(1)}, bf16[1,256,1024]{2,1,0:T(8,128)(2,1)}, u32[]{:S(2)}) copy-start(bf16[1,256,1024]{2,1,0:T(8,128)(2,1)} %weight_ref.1) | copy-start | bytes 1572868
  1.0 7.8 %collective-permute-start = (bf16[16,1024]{1,0:T(8,128)(2,1)S(1)}, bf16[16,1024]{1,0:T(8,128)(2,1)S(1)}, u32[]{:S(2)}, u32[]{:S(2)}) collective-permute-start(bf16[16,1024]{1,0:T(8,128)(2,1)S(1)} %get-tuple-element.14), channel_id=1, source_target_pairs={{0,1},{1,2},{2,3},{3,4},{4,5},{5,6},{6,7},{7,8},{8,9},{9,10},{10,1... | collective-permute-start | bytes 98312 | tf_op jit(solution)/shard_map/ppermute | solution.py:264
  2.9 7.3 %collective-permute-start.1 = (bf16[16,1024]{1,0:T(8,128)(2,1)S(1)}, bf16[16,1024]{1,0:T(8,128)(2,1)S(1)}, u32[]{:S(2)}, u32[]{:S(2)}) collective-permute-start(bf16[16,1024]{1,0:T(8,128)(2,1)S(1)} %get-tuple-element.15), channel_id=1, source_target_pairs={{1,0},{2,1},{3,2},{4,3},{5,4},{6,5},{7,6},{8,7},{9,8},{10,9},{11,1... | collective-permute-start | bytes 98312 | tf_op jit(solution)/shard_map/ppermute | solution.py:265
  14.0 10.2 %copy-start.11 = (s32[1,16,1,2]{1,3,2,0:T(2,128)S(1)}, s32[1,16,1,2]{1,3,2,0:T(2,128)}, u32[]{:S(2)}) copy-start(s32[1,16,1,2]{1,3,2,0:T(2,128)} %param.16) | copy-start | bytes 388
  14.0 33.3 %copy-start.1 = (bf16[1152,128]{1,0:T(8,128)(2,1)S(1)}, bf16[1152,128]{1,0:T(8,128)(2,1)}, u32[]{:S(2)}) copy-start(bf16[1152,128]{1,0:T(8,128)(2,1)} %constant.16.clone.middle_ref.middle) | copy-start | bytes 884740
  14.0 33.3 %copy-start.2 = (bf16[256,256]{1,0:T(8,128)(2,1)S(1)}, bf16[256,256]{1,0:T(8,128)(2,1)}, u32[]{:S(2)}) copy-start(bf16[256,256]{1,0:T(8,128)(2,1)} %constant.15.clone.left_ref.left) | copy-start | bytes 393220
  14.0 33.3 %copy-start.3 = (bf16[256,256]{1,0:T(8,128)(2,1)S(1)}, bf16[256,256]{1,0:T(8,128)(2,1)}, u32[]{:S(2)}) copy-start(bf16[256,256]{1,0:T(8,128)(2,1)} %constant.14.clone.right_ref.right) | copy-start | bytes 393220
  14.0 21.0 %all-to-all-start = ((bf16[16,2,128,128]{3,2,1,0:T(8,128)(2,1)}), bf16[16,2,128,128]{3,2,1,0:T(8,128)(2,1)S(1)}, u32[]{:S(2)}, u32[]{:S(2)}) async-start(bf16[16,2,128,128]{3,2,1,0:T(8,128)(2,1)} %get-tuple-element.16), calls=%async_computation | async-start | bytes 2097152 | tf_op jit(solution)/shard_map/all_to_all | solution.py:281
  19.9 12.5 %collective-permute-start.2 = (bf16[1,128,128]{2,1,0:T(8,128)(2,1)S(1)}, bf16[1,128,128]{2,1,0:T(8,128)(2,1)S(1)}, u32[]{:S(2)}, u32[]{:S(2)}) collective-permute-start(bf16[1,128,128]{2,1,0:T(8,128)(2,1)S(1)} %get-tuple-element.17), channel_id=1, source_target_pairs={{1,0},{2,1},{3,2},{4,3},{5,4},{6,5},{7,6},{8,7},{9,8},{10,9},{11,1... | collective-permute-start | bytes 98312 | tf_op jit(solution)/shard_map/ppermute | solution.py:282
  36.0 23.5 %copy-start.4 = (bf16[256,256]{1,0:T(8,128)(2,1)S(1)}, bf16[256,256]{1,0:T(8,128)(2,1)}, u32[]{:S(2)}) copy-start(bf16[256,256]{1,0:T(8,128)(2,1)} %constant.18.clone.back_right) | copy-start | bytes 393220
  36.0 23.5 %copy-start.5 = (bf16[256,256]{1,0:T(8,128)(2,1)S(1)}, bf16[256,256]{1,0:T(8,128)(2,1)}, u32[]{:S(2)}) copy-start(bf16[256,256]{1,0:T(8,128)(2,1)} %constant.17.clone.back_left) | copy-start | bytes 393220
  36.0 7.4 %collective-permute-start.3 = (bf16[1,128,128]{2,1,0:T(8,128)(2,1)S(1)}, bf16[1,128,128]{2,1,0:T(8,128)(2,1)S(1)}, u32[]{:S(2)}, u32[]{:S(2)}) collective-permute-start(bf16[1,128,128]{2,1,0:T(8,128)(2,1)S(1)} %get-tuple-element.21), channel_id=1, source_target_pairs={{1,0},{2,1},{3,2},{4,3},{5,4},{6,5},{7,6},{8,7},{9,8},{10,9},{11,1... | collective-permute-start | bytes 98312 | tf_op jit(solution)/shard_map/ppermute | solution.py:296
  39.6 20.0 %collective-permute-start.4 = (bf16[9,128,128]{2,1,0:T(8,128)(2,1)S(1)}, bf16[9,128,128]{2,1,0:T(8,128)(2,1)S(1)}, u32[]{:S(2)}, u32[]{:S(2)}) collective-permute-start(bf16[9,128,128]{2,1,0:T(8,128)(2,1)S(1)} %get-tuple-element.19.a_ref), channel_id=1, source_target_pairs={{0,16},{16,32},{32,48},{48,64},{64,80},{80,96},{96,112},{112,128},... | collective-permute-start | bytes 884744 | tf_op jit(solution)/shard_map/ppermute | solution.py:295
  43.4 20.0 %collective-permute-start.5 = (bf16[8,128,128]{2,1,0:T(8,128)(2,1)S(1)}, bf16[8,128,128]{2,1,0:T(8,128)(2,1)S(1)}, u32[]{:S(2)}, u32[]{:S(2)}) collective-permute-start(bf16[8,128,128]{2,1,0:T(8,128)(2,1)S(1)} %constant_dynamic-update-slice_fusion.b_ref), channel_id=1, source_target_pairs={{0,16},{16,32},{32,48},{48,64},{64,80},{80,96},{96,112},{112,128},... | collective-permute-start | bytes 786440 | tf_op jit(solution)/shard_map/ppermute | solution.py:298

commit v3 on v2

v3 whole, which is shorter than its diff:
```python
import jax
import jax.numpy as jnp
import numpy as np
from jax import lax
from jax.experimental import pallas as pl
from jax.experimental.pallas import tpu as pltpu
from jax.sharding import PartitionSpec as P

B = 128
H = B // 2
EDGE = 16
EARLY = 8
PAIRS = 9
F32 = jnp.float32
BF16 = jnp.bfloat16
VMEM_LIMIT = 48 * 2**20
PREPARE_VMEM_LIMIT = 54912 * 2**10


def tables():
    j = np.arange(B)
    angle = (j[:, None] * j[None, :] % B) * (2.0 * np.pi / B)
    c, s = np.cos(angle), np.sin(angle)
    right = np.zeros((2 * B, 2 * B))
    for half, start in ((0, 0), (1, H)):
        right[start : start + B, half * H : half * H + H] = c[:, :H]
        right[start : start + B, B + half * H : B + half * H + H] = s[:, :H]
    left = np.block([[c, -s], [-s, -c]])
    q = np.arange((PAIRS + 1) * B)
    sign = 1.0 - 2.0 * (q % 2)
    middle = np.zeros(((PAIRS + 1) * B, B))
    for m in range(PAIRS):
        middle[:, m] = sign * (q // B == m)
        middle[:, H + m] = sign * ((q - H) // B == m)
    back_left = np.block([[c, -s], [s, c]])
    twice = np.where(j[:H] == 0, 1.0, 2.0)[:, None] / B
    back_right = np.zeros((2 * B, 2 * B))
    imag = -twice * s[:H]
    imag[0] = (1.0 - 2.0 * (j % 2)) / B
    for half in range(2):
        lanes = slice(half * B, half * B + B)
        back_right[half * H : half * H + H, lanes] = twice * c[:H]
        back_right[B + half * H : B + half * H + H, lanes] = imag
    return tuple(np.asarray(t, np.float32).astype(BF16) for t in (right, left, middle, back_left, back_right))


def dot(a, b):
    return jnp.dot(a, b, preferred_element_type=F32)


def shifted(x, off):
    rows = x.shape[0]
    if off == 0:
        return x
    gap = jnp.zeros((rows, abs(off)), x.dtype)
    if off > 0:
        return jnp.concatenate([x[:, off:], gap], 1)
    return jnp.concatenate([gap, x[:, :off]], 1)


def banded(taps_ref, which, valid):
    high, low = [], []
    for b in range(5):
        band = jnp.zeros(which.shape, F32)
        for a in range(5):
            band = jnp.where(which == a, taps_ref[0, 0, 5 * a + b], band)
        if valid is not None:
            band = jnp.where(valid, band, 0.0)
        top = band.astype(BF16)
        high.append(top)
        low.append((band - top.astype(F32)).astype(BF16))
    return jnp.concatenate([jnp.concatenate(high, 1), jnp.concatenate(low, 1)], 0)


def prepare_kernel(image, last, head, sems):
    rows = image.shape[1]
    pairs = ((image.at[0, pl.ds(rows - EDGE, EDGE)], last), (image.at[0, pl.ds(0, EDGE)], head))
    copies = [pltpu.make_async_copy(whence, where, sems.at[n]) for n, (whence, where) in enumerate(pairs)]
    for copy in copies:
        copy.start()
    for copy in copies:
        copy.wait()


def lens_kernel(taps_ref, image_ref, weight_ref, blocks_ref, edge_ref):
    x = image_ref[0]
    rows, cols = x.shape
    across = cols // B
    i = lax.broadcasted_iota(jnp.int32, (rows, rows), 0)
    j = lax.broadcasted_iota(jnp.int32, (rows, rows), 1)
    bands = banded(taps_ref, j - i + 2, None)
    stack = jnp.concatenate([shifted(x, b - 2) for b in range(5)], 0)
    both = dot(bands, stack)
    corrected = both[:rows] + both[rows:]
    edge_ref[:EDGE] = corrected[:EDGE]
    edge_ref[EDGE:] = corrected[rows - EDGE :]
    weighted = (corrected * weight_ref[0].astype(F32)).astype(BF16)
    for k in range(rows // B * across):
        r, c = k // across * B, k % across * B
        blocks_ref[k] = weighted[r : r + B, c : c + B]


def pick_kernel(
    taps_ref, src_ref, count_ref, low_ref, high_ref, edge_ref, weight_ref, blocks_ref, anchor_ref, out, first_ref, fixed_ref, out_sems
):
    rows, cols = weight_ref.shape[1:]
    across = cols // B
    count = rows // B * across
    for k in range(count):
        fixed_ref[k] = blocks_ref[k]
    fixed_ref[count] = jnp.zeros((B, B), BF16)
    first_ref[0] = anchor_ref[0]
    e = lax.broadcasted_iota(jnp.int32, (2 * EDGE, 2 * EDGE), 0)
    k = lax.broadcasted_iota(jnp.int32, (2 * EDGE, 2 * EDGE), 1)
    upper = (e < EDGE) & (k < EDGE)
    lower = (e >= EDGE) & (k >= EDGE)
    which = jnp.where(upper, k - (EDGE - 2) - e, k + (EDGE + 2) - e)
    rim = jnp.concatenate([low_ref[...], high_ref[...]], 0)
    rims = jnp.concatenate([shifted(rim, b - 2) for b in range(5)], 0)
    both = dot(banded(taps_ref, which, upper | lower), rims)
    corrected = edge_ref[...] + (both[: 2 * EDGE] + both[2 * EDGE :])
    top = (corrected[:EDGE] * weight_ref[0, :EDGE].astype(F32)).astype(BF16)
    bottom = (corrected[EDGE:] * weight_ref[0, rows - EDGE :].astype(F32)).astype(BF16)
    for c in range(across):
        fixed_ref[c, :EDGE] = top[:, c * B : c * B + B]
        fixed_ref[count - across + c, B - EDGE :] = bottom[:, c * B : c * B + B]
    sends = []
    for d in range(out.shape[0]):
        for q in range(out.shape[1]):
            at = jnp.where(q < count_ref[0, 0, d], src_ref[0, 0, d, q], count)
            sends.append(pltpu.make_async_copy(fixed_ref.at[at], out.at[d, q], out_sems.at[d, q]))
            sends[-1].start()
    for send in sends:
        send.wait()


def strip_kernel(dst_ref, in_ref, a_ref, rest_ref, acc_ref):
    acc_ref[...] = jnp.zeros_like(acc_ref)
    for d in range(in_ref.shape[0]):
        for q in range(in_ref.shape[1]):
            j = dst_ref[0, d, 0, q]
            acc_ref[j] = acc_ref[j] + in_ref[d, q].astype(F32)
    a_ref[...] = acc_ref[:EARLY].astype(BF16)
    rest_ref[...] = acc_ref[EARLY:]


def rest_kernel(a_ref, rest_ref, b_ref, first_ref):
    count = rest_ref.shape[0]
    b_ref[:count] = rest_ref[...].astype(BF16)
    b_ref[count] = jnp.zeros((B, B), BF16)
    first_ref[0] = a_ref[0]


def forward(blocks, right, left, middle):
    pairs = len(blocks) - 1
    both = jnp.concatenate([jnp.concatenate([blocks[m], blocks[m + 1]], 1) for m in range(pairs)], 0)
    p = dot(both, right).astype(BF16)
    re = [p[m * B : m * B + B, :B] for m in range(pairs)]
    im = [p[m * B : m * B + B, B:] for m in range(pairs)]
    spectra = dot(left, jnp.concatenate([jnp.concatenate(re, 1), jnp.concatenate(im, 1)], 0))
    p = dot(jnp.concatenate(blocks, 1), middle[: (pairs + 1) * B]).astype(BF16)
    return spectra, dot(left[:, :B], p)


def spectra_out(blocks, right_ref, left_ref, middle_ref, out_ref):
    spectra, rest = forward(blocks, right_ref[...], left_ref[...], middle_ref[...])
    out_ref[:, : spectra.shape[1]] = spectra.astype(BF16)
    out_ref[:, spectra.shape[1] :] = rest.astype(BF16)


def early_kernel(a_ref, *refs):
    spectra_out([a_ref[m] for m in range(EARLY)], *refs)


def late_kernel(a_ref, b_ref, *refs):
    spectra_out([a_ref[EARLY - 1]] + [b_ref[m] for m in range(b_ref.shape[0])], *refs)


def correlate_chunk(cur_ref, blocks, tables, out, at, cross_ref, mag_ref, result_ref, sems):
    right, left, middle, back_left, back_right = (table[...] for table in tables)
    pairs = len(blocks) - 1
    lane = lax.broadcasted_iota(jnp.int32, (1, B), 1)
    twice = jnp.where(lane % H == 0, 1.0, 2.0)
    sums = []
    spectra, rest = forward(blocks, right, left, middle)
    for m in range(pairs + 1):
        f = spectra[:, m * B : m * B + B] if m < pairs else rest
        c = cur_ref[:, m * B : m * B + B].astype(F32)
        ar, ai, br, bi = c[:B], c[B:], f[:B], f[B:]
        re = ar * br + ai * bi
        im = ai * br - ar * bi
        square = re * re + im * im
        mag = square * lax.rsqrt(jnp.maximum(square, 1e-30))
        cross_ref[m, :B] = re
        cross_ref[m, B:] = im
        mag_ref[m] = mag
        total = jnp.sum(mag, axis=0, keepdims=True)
        sums.append(total * twice if m < pairs else total)
    row = lax.broadcasted_iota(jnp.int32, (pairs, B), 0)
    lanes = lax.broadcasted_iota(jnp.int32, (pairs, B), 1)
    mine = row == lanes % H
    table = jnp.concatenate(sums[:pairs], 0) + jnp.where(mine, sums[pairs], 0.0)
    aligned = lanes < H
    first = jnp.sum(jnp.where(aligned, table, 0.0), axis=1, keepdims=True)
    second = jnp.sum(jnp.where(aligned, 0.0, table), axis=1, keepdims=True)
    floor = jnp.where(aligned, first, second) * (0.1 / (B * B)) + 1e-6
    floor_middle = jnp.sum(jnp.where(mine, floor, 0.0), axis=0, keepdims=True)
    floor_middle = jnp.where(lane % H < pairs, floor_middle, 1.0)

    def whitened(m, low):
        scale = 1.0 / (mag_ref[m] + low)
        return jnp.concatenate([cross_ref[m, :B] * scale, cross_ref[m, B:] * scale], 0).astype(BF16)

    y_middle = dot(back_left[:B], whitened(pairs, floor_middle))
    y = dot(back_left, jnp.concatenate([whitened(m, floor[m : m + 1]) for m in range(pairs)], 1))
    is_zero = lane % H == 0
    both = []
    for m in range(pairs):
        turned = y_middle if m == 0 else pltpu.roll(y_middle, B - m, 1)
        imag = jnp.where(is_zero, turned, y[B:, m * B : m * B + B])
        both.append(jnp.concatenate([y[:B, m * B : m * B + B].astype(BF16), imag.astype(BF16)], 1))
    result = dot(jnp.concatenate(both, 0), back_right)
    sends = []
    for m in range(pairs):
        result_ref[2 * m] = result[m * B : m * B + B, :B]
        result_ref[2 * m + 1] = result[m * B : m * B + B, B:]
        sends.append(
            pltpu.make_async_copy(result_ref.at[pl.ds(2 * m, 2)], out.at[0, pl.ds(2 * (at + m), 2)], sems.at[m])
        )
        sends[-1].start()
    for send in sends:
        send.wait()


def prior_block(anchor, direct, relayed):
    sec = lax.axis_index("sec")
    chosen = jnp.where(sec == lax.axis_size("sec") // 2, relayed, direct)
    return jnp.where(sec == 0, anchor, chosen)


def correlate_early(cur_ref, a_ref, relay_ref, anchor_ref, *refs):
    blocks = [prior_block(anchor_ref[m], a_ref[m], relay_ref[m]) for m in range(EARLY)]
    correlate_chunk(cur_ref, blocks, refs[:5], refs[5], 0, *refs[6:])


def correlate_late(held, cur_ref, a_ref, relay_ref, b_ref, anchor_ref, border_ref, *refs):
    del held
    is_first = lax.axis_index("sec") == 0
    rest = b_ref.shape[0] - 1
    blocks = [prior_block(anchor_ref[EARLY - 1], a_ref[EARLY - 1], relay_ref[EARLY - 1])]
    blocks += [jnp.where(is_first, anchor_ref[EARLY + m], b_ref[m]) for m in range(rest)]
    blocks += [jnp.where(is_first, border_ref[0], b_ref[rest])]
    correlate_chunk(cur_ref, blocks, refs[:5], refs[5], EARLY - 1, *refs[6:])


SMEM = pl.BlockSpec(memory_space=pltpu.SMEM)
VMEM = pl.BlockSpec(memory_space=pltpu.VMEM)
ANY = pl.BlockSpec(memory_space=pl.ANY)
HBM = pl.BlockSpec(memory_space=pltpu.HBM)


def call(kernel, out_shape, in_specs, out_specs, scratch, flops, moved, args, aliases=None, grid=None, limit=VMEM_LIMIT):
    extra = {} if grid is None else {"grid": grid}
    return pl.pallas_call(
        kernel,
        out_shape=out_shape,
        in_specs=in_specs,
        out_specs=out_specs,
        scratch_shapes=scratch,
        input_output_aliases=aliases or {},
        compiler_params=pltpu.CompilerParams(vmem_limit_bytes=limit),
        cost_estimate=pl.CostEstimate(flops=flops, bytes_accessed=moved, transcendentals=0),
        **extra,
    )(*args)


def body(image, weight, lens_filter_taps, block_src, block_dst, valid_count, anchor):
    rows, cols = image.shape[1:]
    strips = lax.axis_size("tile")
    sections = lax.axis_size("sec")
    slots = block_src.shape[-1]
    count = anchor.shape[0]
    shape = jax.ShapeDtypeStruct
    whole = lambda *dims: pl.BlockSpec(dims, lambda i: (0,) * len(dims))
    forth = [(i, i + 1) for i in range(strips - 1)]
    back = [(i + 1, i) for i in range(strips - 1)]
    last, head = call(
        prepare_kernel,
        (shape((EDGE, cols), BF16), shape((EDGE, cols), BF16)),
        [HBM],
        (VMEM,) * 2,
        [pltpu.SemaphoreType.DMA((2,))],
        2**33,
        2**17,
        (image,),
        limit=PREPARE_VMEM_LIMIT,
    )
    low = lax.ppermute(last, "tile", forth)
    high = lax.ppermute(head, "tile", back)
    tile_blocks = rows // B * (cols // B)
    blocks, edge = call(
        lens_kernel,
        (shape((tile_blocks, B, B), BF16), shape((2 * EDGE, cols), F32)),
        [SMEM, VMEM, VMEM],
        (VMEM, VMEM),
        [],
        2 * 10 * rows * rows * cols,
        3 * 2 * rows * cols,
        (lens_filter_taps, image, weight),
    )
    outgoing, anchor_first = call(
        pick_kernel,
        (shape((strips, slots, B, B), BF16), shape((1, B, B), BF16)),
        [SMEM] * 3 + [VMEM] * 6,
        (HBM, VMEM),
        [pltpu.VMEM((tile_blocks + 1, B, B), BF16), pltpu.SemaphoreType.DMA((strips, slots))],
        2**20,
        4 * 2 * rows * cols,
        (lens_filter_taps, block_src, valid_count, low, high, edge, weight, blocks, anchor),
    )
    incoming = lax.all_to_all(outgoing, "tile", split_axis=0, concat_axis=0, tiled=True)
    border = lax.ppermute(anchor_first, "tile", back)
    incoming, border = lax.optimization_barrier((incoming, border))
    part_a, rest = call(
        strip_kernel,
        (shape((EARLY, B, B), BF16), shape((count - EARLY, B, B), F32)),
        [SMEM, VMEM],
        (VMEM, VMEM),
        [pltpu.VMEM((count, B, B), F32)],
        2**20,
        4 * 2 * rows * cols,
        (block_dst, incoming),
    )
    part_b, first = call(
        rest_kernel,
        (shape((count - EARLY + 1, B, B), BF16), shape((1, B, B), BF16)),
        [VMEM] * 2,
        (VMEM, VMEM),
        [],
        2**18,
        6 * EARLY * B * B,
        (part_a, rest),
    )
    turn, side = sections // 2, strips // 2
    by_relay, forward_on = [], []
    for s in range(sections - 1):
        for d in range(strips):
            here, there = s * strips + d, (s + 1) * strips + d
            if s + 1 == turn:
                relay = there + side if d < side else d - side
                by_relay.append((here, relay))
                forward_on.append((relay, there))
            else:
                by_relay.append((here, there))
    on = [(i, i + 1) for i in range(sections - 1)]
    prior_a = lax.ppermute(part_a, ("sec", "tile"), by_relay)
    own_rim = lax.ppermute(first, "tile", back)
    part_b = lax.dynamic_update_slice(part_b, own_rim, (count - EARLY, 0, 0))
    prior_b = lax.ppermute(part_b, "sec", on)
    right, left, middle, back_left, back_right = (jnp.asarray(t) for t in tables())
    early, late = EARLY - 1, count - EARLY + 1
    current = lambda kernel, pairs, *parts: call(
        kernel,
        shape((2 * B, (pairs + 1) * B), BF16),
        [VMEM] * (len(parts) + 3),
        VMEM,
        [],
        2**10,
        2**10,
        (*parts, right, left, middle),
    )
    spectra_a = current(early_kernel, early, part_a)
    spectra_b = current(late_kernel, late, part_a, part_b)
    prior_a, spectra_b = lax.optimization_barrier((prior_a, spectra_b))
    relayed_a = lax.ppermute(prior_a, ("sec", "tile"), forward_on)
    result = shape((1, 2 * count, B, B), F32)
    scratch = lambda pairs: [
        pltpu.VMEM((pairs + 1, 2 * B, B), F32),
        pltpu.VMEM((pairs + 1, B, B), F32),
        pltpu.VMEM((2 * pairs, B, B), F32),
        pltpu.SemaphoreType.DMA((pairs,)),
    ]
    held = call(
        correlate_early,
        result,
        [VMEM] * 9,
        HBM,
        scratch(early),
        2**10,
        2**10,
        (spectra_a, prior_a, relayed_a, anchor, right, left, middle, back_left, back_right),
    )
    return call(
        correlate_late,
        result,
        [HBM] + [VMEM] * 11,
        HBM,
        scratch(late),
        2**30,
        2**22,
        (held, spectra_b, prior_a, relayed_a, prior_b, anchor, border, right, left, middle, back_left, back_right),
        aliases={0: 0},
    )


def solution(mesh):
    in_specs = (
        P("sec", "tile", None),
        P("sec", "tile", None),
        P("sec", "tile", None),
        P("sec", "tile", None, None),
        P("sec", None, "tile", None),
        P("sec", "tile", None),
        P("tile", None, None),
    )
    out_specs = P("sec", "tile", None, None)
    return jax.shard_map(body, mesh=mesh, in_specs=in_specs, out_specs=out_specs, check_vma=False)
```

time: 66.3 us -> 72.4 us (1.092)
  waiting for transfers between devices: 24.5 us -> 28.3 us
  Pallas kernels: 12 us -> 12.9 us
  starting transfers between devices: 29 us -> 29.9 us
    ppermute x1 -> x2, waiting for transfers between devices: 10.9 us -> 16 us  [the longest x1 11.1 us: body(): relayed_a = lax.ppermute(prior_a, ('sec', 'tile'), forward_on)]
    ppermute x1 -> x2, starting transfers between devices: 3.83 us -> 5.87 us  [the longest x1 3.96 us: body(): prior_a = lax.ppermute(part_a, ('sec', 'tile'), by_relay)]
    ppermute x1, waiting for transfers between devices: 0.01 us -> 1.58 us  [body(): own_rim = lax.ppermute(first, 'tile', back)]
    ppermute x1, waiting for transfers between devices: 1.48 us -> 0.01 us  [body(): high = lax.ppermute(head, 'tile', back)]
    ppermute x1, waiting for transfers between devices: 1.4 us -> 0.01 us  [body(): prior_b = lax.ppermute(part_b, 'sec', on)]
    pallas_call x6 -> x9, Pallas kernels: 12 us -> 12.9 us  [call(): pl.pallas_call(kernel, out_shape=out_shape, in_specs=in_specs, out_specs=...]
    all_to_all x1, starting transfers between devices: 5.86 us -> 5.03 us  [body(): lax.all_to_all(outgoing, 'tile', split_axis=0, concat_axis=0, tiled=True)]
  transfers between devices with their start and end apart: 7 -> 8, of which waited for: 5 -> 5; matrix products, arithmetic and copies ran while one was open for 0% -> 0% of each run, Pallas kernels for 6% -> 9%
where the time goes in v3:
time: 72.4 us; the launch traced here: 71.7 us
  starting transfers between devices  29.9 us (41%)
  waiting for transfers between devices  28.3 us (39%)
  Pallas kernels  12.9 us (18%)
    pallas_call x9, Pallas kernels, call(): pl.pallas_call(kernel, out_shape=out_shape, in_specs=in_specs, out_specs=...  12.9 us
    ppermute x1, waiting for transfers between devices, body(): relayed_a = lax.ppermute(prior_a, ('sec', 'tile'), forward_on)  11.1 us
    ppermute x1, waiting for transfers between devices, body(): border = lax.ppermute(anchor_first, 'tile', back)  8.11 us
    ppermute x1, starting transfers between devices, body(): high = lax.ppermute(head, 'tile', back)  5.88 us
    all_to_all x1, starting transfers between devices, body(): lax.all_to_all(outgoing, 'tile', split_axis=0, concat_axis=0, tiled=True)  5.03 us
    ppermute x1, waiting for transfers between devices, body(): prior_a = lax.ppermute(part_a, ('sec', 'tile'), by_relay)  4.97 us
    ppermute x1, starting transfers between devices, body(): border = lax.ppermute(anchor_first, 'tile', back)  4.32 us
    ppermute x1, starting transfers between devices, body(): prior_a = lax.ppermute(part_a, ('sec', 'tile'), by_relay)  3.96 us
  transfers between devices with their start and end apart: 8, of which 5 were waited for; matrix products, arithmetic and copies ran while one was open for 0% of the time, Pallas kernels for 9%

profile of v3, /device:TPU:24, one launch (start us, length us, event | category | flops | bytes accessed | tf_op | source)
XLA Modules:
  0.0 71.7 jit_solution(11656160992416036131)
XLA Ops:
  0.0 0.0 copy-start.9
  0.0 0.0 copy-start.7
  0.0 0.0 copy-start.6
  0.0 0.9 %shard_map.118 = (bf16[16,1024]{1,0:T(8,128)(2,1)S(1)}, bf16[16,1024]{1,0:T(8,128)(2,1)S(1)}) custom-call(bf16[1,256,1024]{2,1,0:T(8,128)(2,1)} %image_ref.1), custom_call_target="tpu_custom_call" | custom-call | flops 8589934592 | bytes 131072 | tf_op jit(solution)/shard_map/pallas_call | solution.py:264
  0.9 1.9 %collective-permute-start = (bf16[16,1024]{1,0:T(8,128)(2,1)S(1)}, bf16[16,1024]{1,0:T(8,128)(2,1)S(1)}, u32[]{:S(2)}, u32[]{:S(2)}) collective-permute-start(bf16[16,1024]{1,0:T(8,128)(2,1)S(1)} %get-tuple-element.19), channel_id=1, source_target_pairs={{0,1},{1,2},{2,3},{3,4},{4,5},{5,6},{6,7},{7,8},{8,9},{9,10},{10,1... | collective-permute-start | bytes 98312 | tf_op jit(solution)/shard_map/ppermute | solution.py:298
  2.8 0.0 copy-start.10
  2.8 0.0 copy-start.1
  2.9 0.0 copy-start.8
  2.9 5.9 %collective-permute-start.1 = (bf16[16,1024]{1,0:T(8,128)(2,1)S(1)}, bf16[16,1024]{1,0:T(8,128)(2,1)S(1)}, u32[]{:S(2)}, u32[]{:S(2)}) collective-permute-start(bf16[16,1024]{1,0:T(8,128)(2,1)S(1)} %get-tuple-element.20), channel_id=1, source_target_pairs={{1,0},{2,1},{3,2},{4,3},{5,4},{6,5},{7,6},{8,7},{9,8},{10,9},{11,1... | collective-permute-start | bytes 98312 | tf_op jit(solution)/shard_map/ppermute | solution.py:299
  8.8 0.0 copy-done.9
  8.8 0.0 copy-done.7
  8.8 0.0 copy-done.6
  8.8 2.2 %shard_map.119 = (bf16[16,128,128]{2,1,0:T(8,128)(2,1)S(1)}, f32[32,1024]{1,0:T(8,128)S(1)}) custom-call(f32[1,1,25]{2,1,0:T(1,128)S(1)} %copy-done.7, bf16[1,256,1024]{2,1,0:T(8,128)(2,1)S(1)} %copy-done.9, bf16[1,256,1024]{2,1,0:T(8,128)(2,1)S(1)} %copy-done.6), custom_call_target="tpu_custom_call" | custom-call | flops 1342177280 | bytes 1572864 | tf_op jit(solution)/shard_map/pallas_call | solution.py:264
  11.0 0.0 copy-done.10
  11.0 0.0 copy-start.11
  11.0 0.1 copy.14.src_ref
  11.1 0.0 collective-permute-done.low_ref
  11.1 0.0 collective-permute-done.1.high_ref
  11.1 0.0 copy-done.1
  11.1 0.0 copy-done.8
  11.2 2.2 %shard_map.120 = (bf16[16,2,128,128]{3,2,1,0:T(8,128)(2,1)}, bf16[1,128,128]{2,1,0:T(8,128)(2,1)S(1)}) custom-call(f32[1,1,25]{2,1,0:T(1,128)S(1)} %copy-done.7, s32[1,1,16,2]{3,2,1,0:T(8,128)S(1)} %copy.14.src_ref, s32[1,1,16]{2,1,0:T(1,128)S(1)} %copy-done.8, bf16[16,1024]{1,0:T(8,128)(2,1)S(1)} %collective-permute-done.low_ref, ...), custom_call_target="tpu_custom_call" | custom-call | flops 1048576 | bytes 2097152 | tf_op jit(solution)/shard_map/pallas_call | solution.py:264
  13.4 0.0 copy-start
  13.4 0.0 copy-start.2
  13.4 0.0 copy-start.3
  13.4 5.0 %all-to-all-start = ((bf16[16,2,128,128]{3,2,1,0:T(8,128)(2,1)}), bf16[16,2,128,128]{3,2,1,0:T(8,128)(2,1)S(1)}, u32[]{:S(2)}, u32[]{:S(2)}) async-start(bf16[16,2,128,128]{3,2,1,0:T(8,128)(2,1)} %get-tuple-element.23), calls=%async_computation | async-start | bytes 2097152 | tf_op jit(solution)/shard_map/all_to_all | solution.py:321
  18.4 4.3 %collective-permute-start.2 = (bf16[1,128,128]{2,1,0:T(8,128)(2,1)S(1)}, bf16[1,128,128]{2,1,0:T(8,128)(2,1)S(1)}, u32[]{:S(2)}, u32[]{:S(2)}) collective-permute-start(bf16[1,128,128]{2,1,0:T(8,128)(2,1)S(1)} %get-tuple-element.24), channel_id=1, source_target_pairs={{1,0},{2,1},{3,2},{4,3},{5,4},{6,5},{7,6},{8,7},{9,8},{10,9},{11,1... | collective-permute-start | bytes 98312 | tf_op jit(solution)/shard_map/ppermute | solution.py:322
  22.7 0.0 copy-done.11
  22.8 0.1 copy.15.dst_ref
  22.8 8.1 %collective-permute-done.2.border_ref = bf16[1,128,128]{2,1,0:T(8,128)(2,1)S(1)} collective-permute-done((bf16[1,128,128]{2,1,0:T(8,128)(2,1)S(1)}, bf16[1,128,128]{2,1,0:T(8,128)(2,1)S(1)}, u32[]{:S(2)}, u32[]{:S(2)}) %collective-permute-start.2) | collective-permute-done | bytes 32800 | tf_op jit(solution)/shard_map/ppermute | solution.py:322
  31.0 2.6 %all-to-all-done.in_ref = bf16[16,2,128,128]{3,2,1,0:T(8,128)(2,1)S(1)} async-done(((bf16[16,2,128,128]{3,2,1,0:T(8,128)(2,1)}), bf16[16,2,128,128]{3,2,1,0:T(8,128)(2,1)S(1)}, u32[]{:S(2)}, u32[]{:S(2)}) %all-to-all-start) | async-done | bytes 1048608 | tf_op jit(solution)/shard_map/all_to_all | solution.py:321
  33.5 1.0 %shard_map.121 = (bf16[8,128,128]{2,1,0:T(8,128)(2,1)S(1)}, f32[8,128,128]{2,1,0:T(8,128)S(1)}) custom-call(s32[1,16,1,2]{3,2,1,0:T(1,128)S(1)} %copy.15.dst_ref, bf16[16,2,128,128]{3,2,1,0:T(8,128)(2,1)S(1)} %all-to-all-done.in_ref), custom_call_target="tpu_custom_call" | custom-call | flops 1048576 | bytes 2097152 | tf_op jit(solution)/shard_map/pallas_call | solution.py:264
  34.5 0.0 copy-start.4
  34.6 0.0 copy-start.5
  34.6 4.0 %collective-permute-start.3 = (bf16[8,128,128]{2,1,0:T(8,128)(2,1)S(1)}, bf16[8,128,128]{2,1,0:T(8,128)(2,1)S(1)}, u32[]{:S(2)}, u32[]{:S(2)}) collective-permute-start(bf16[8,128,128]{2,1,0:T(8,128)(2,1)S(1)} %get-tuple-element.26.a_ref), channel_id=1, source_target_pairs={{0,16},{1,17},{2,18},{3,19},{4,20},{5,21},{6,22},{7,23},{8,24},{9,... | collective-permute-start | bytes 786440 | tf_op jit(solution)/shard_map/ppermute | solution.py:356
  38.6 3.1 %collective-permute-start.4 = (bf16[1,128,128]{2,1,0:T(8,128)(2,1)S(1)}, bf16[1,128,128]{2,1,0:T(8,128)(2,1)S(1)}, u32[]{:S(2)}, u32[]{:S(2)}) collective-permute-start(bf16[1,128,128]{2,1,0:T(8,128)(2,1)S(1)} %get-tuple-element.29), channel_id=1, source_target_pairs={{1,0},{2,1},{3,2},{4,3},{5,4},{6,5},{7,6},{8,7},{9,8},{10,9},{11,1... | collective-permute-start | bytes 98312 | tf_op jit(solution)/shard_map/ppermute | solution.py:357
  41.7 1.6 %collective-permute-done.4 = bf16[1,128,128]{2,1,0:T(8,128)(2,1)S(1)} collective-permute-done((bf16[1,128,128]{2,1,0:T(8,128)(2,1)S(1)}, bf16[1,128,128]{2,1,0:T(8,128)(2,1)S(1)}, u32[]{:S(2)}, u32[]{:S(2)}) %collective-permute-start.4) | collective-permute-done | bytes 32800 | tf_op jit(solution)/shard_map/ppermute | solution.py:357
  43.3 3.8 %collective-permute-start.6 = (bf16[9,128,128]{2,1,0:T(8,128)(2,1)S(1)}, bf16[9,128,128]{2,1,0:T(8,128)(2,1)S(1)}, u32[]{:S(2)}, u32[]{:S(2)}) collective-permute-start(bf16[9,128,128]{2,1,0:T(8,128)(2,1)S(1)} %constant_dynamic-update-slice_fusion.b_ref), channel_id=1, source_target_pairs={{0,16},{16,32},{32,48},{48,64},{64,80},{80,96},{96,112},{112,128},... | collective-permute-start | bytes 884744 | tf_op jit(solution)/shard_map/ppermute | solution.py:359
  47.1 0.0 copy-done
  47.1 0.0 copy-done.2
  47.1 0.0 copy-done.3
  47.1 0.9 %shard_map.124.cur_ref = bf16[256,1280]{1,0:T(8,128)(2,1)S(1)} custom-call(bf16[8,128,128]{2,1,0:T(8,128)(2,1)S(1)} %get-tuple-element.26.a_ref, bf16[9,128,128]{2,1,0:T(8,128)(2,1)S(1)} %constant_dynamic-update-slice_fusion.b_ref, bf16[256,256]{1,0:T(8,128)(2,1)S(1)} %copy-done.3, bf16[256,256]{1,0:T(8,128)(2,1)S(1)} %copy-done.2, bf16[1280,128]{1,0:T(8,128)(2,1)S(1)} %copy-done), custom_call_target="tpu_custom_call" | custom-call | flops 1024 | bytes 1024 | tf_op jit(solution)/shard_map/pallas_call | solution.py:264
  48.1 5.0 %collective-permute-done.3.a_ref = bf16[8,128,128]{2,1,0:T(8,128)(2,1)S(1)} collective-permute-done((bf16[8,128,128]{2,1,0:T(8,128)(2,1)S(1)}, bf16[8,128,128]{2,1,0:T(8,128)(2,1)S(1)}, u32[]{:S(2)}, u32[]{:S(2)}) %collective-permute-start.3) | collective-permute-done | bytes 262176 | tf_op jit(solution)/shard_map/ppermute | solution.py:356
  53.0 1.9 %collective-permute-start.5 = (bf16[8,128,128]{2,1,0:T(8,128)(2,1)S(1)}, bf16[8,128,128]{2,1,0:T(8,128)(2,1)S(1)}, u32[]{:S(2)}, u32[]{:S(2)}) collective-permute-start(bf16[8,128,128]{2,1,0:T(8,128)(2,1)S(1)} %collective-permute-done.3.a_ref), channel_id=1, source_target_pairs={{264,256},{265,257},{266,258},{267,259},{268,260},{269,261},{270,2... | collective-permute-start | bytes 786440 | tf_op jit(solution)/shard_map/ppermute | solution.py:375
  54.9 0.8 %shard_map.122.cur_ref = bf16[256,1024]{1,0:T(8,128)(2,1)S(1)} custom-call(bf16[8,128,128]{2,1,0:T(8,128)(2,1)S(1)} %get-tuple-element.26.a_ref, bf16[256,256]{1,0:T(8,128)(2,1)S(1)} %copy-done.3, bf16[256,256]{1,0:T(8,128)(2,1)S(1)} %copy-done.2, bf16[1280,128]{1,0:T(8,128)(2,1)S(1)} %copy-done), custom_call_target="tpu_custom_call" | custom-call | flops 1024 | bytes 1024 | tf_op jit(solution)/shard_map/pallas_call | solution.py:264
  55.8 11.1 %collective-permute-done.5.relay_ref = bf16[8,128,128]{2,1,0:T(8,128)(2,1)S(1)} collective-permute-done((bf16[8,128,128]{2,1,0:T(8,128)(2,1)S(1)}, bf16[8,128,128]{2,1,0:T(8,128)(2,1)S(1)}, u32[]{:S(2)}, u32[]{:S(2)}) %collective-permute-start.5) | collective-permute-done | bytes 262176 | tf_op jit(solution)/shard_map/ppermute | solution.py:375
  66.8 0.0 copy-done.4
  66.8 0.0 copy-done.5
  66.8 2.3 %shard_map.125.held = f32[1,32,128,128]{3,2,1,0:T(8,128)} custom-call(bf16[256,1024]{1,0:T(8,128)(2,1)S(1)} %shard_map.122.cur_ref, bf16[8,128,128]{2,1,0:T(8,128)(2,1)S(1)} %collective-permute-done.3.a_ref, bf16[8,128,128]{2,1,0:T(8,128)(2,1)S(1)} %collective-permute-done.5.relay_ref, bf16[16,128,128]{2,1,0:T(8,128)(2,1)S(1)} %copy-done.1, ...), custom_call_target="tpu_custom_call" | custom-call | flops 1024 | bytes 1024 | tf_op jit(solution)/shard_map/pallas_call | solution.py:264
  69.1 0.0 collective-permute-done.6.b_ref
  69.1 2.6 %shard_map.126 = f32[1,32,128,128]{3,2,1,0:T(8,128)} custom-call(f32[1,32,128,128]{3,2,1,0:T(8,128)} %shard_map.125.held, bf16[256,1280]{1,0:T(8,128)(2,1)S(1)} %shard_map.124.cur_ref, bf16[8,128,128]{2,1,0:T(8,128)(2,1)S(1)} %collective-permute-done.3.a_ref, ...), custom_call_target="tpu_custom_call", output_to_operand_aliasing={{}: (0, {})} | custom-call | flops 1073741824 | bytes 4194304 | tf_op jit(solution)/shard_map/pallas_call | solution.py:264
  (2 shorter events, 0.0 us)
Async XLA Ops:
  0.0 8.8 %copy-start.9 = (bf16[1,256,1024]{2,1,0:T(8,128)(2,1)S(1)}, bf16[1,256,1024]{2,1,0:T(8,128)(2,1)}, u32[]{:S(2)}) copy-start(bf16[1,256,1024]{2,1,0:T(8,128)(2,1)} %image_ref.1) | copy-start | bytes 1572868
  0.0 8.8 %copy-start.7 = (f32[1,1,25]{2,1,0:T(1,128)S(1)}, f32[1,1,25]{2,1,0:T(1,128)}, u32[]{:S(2)}) copy-start(f32[1,1,25]{2,1,0:T(1,128)} %taps_ref.3) | copy-start | bytes 304
  0.0 8.8 %copy-start.6 = (bf16[1,256,1024]{2,1,0:T(8,128)(2,1)S(1)}, bf16[1,256,1024]{2,1,0:T(8,128)(2,1)}, u32[]{:S(2)}) copy-start(bf16[1,256,1024]{2,1,0:T(8,128)(2,1)} %weight_ref.3) | copy-start | bytes 1572868
  0.9 10.2 %collective-permute-start = (bf16[16,1024]{1,0:T(8,128)(2,1)S(1)}, bf16[16,1024]{1,0:T(8,128)(2,1)S(1)}, u32[]{:S(2)}, u32[]{:S(2)}) collective-permute-start(bf16[16,1024]{1,0:T(8,128)(2,1)S(1)} %get-tuple-element.19), channel_id=1, source_target_pairs={{0,1},{1,2},{2,3},{3,4},{4,5},{5,6},{6,7},{7,8},{8,9},{9,10},{10,1... | collective-permute-start | bytes 98312 | tf_op jit(solution)/shard_map/ppermute | solution.py:298
  2.8 8.2 %copy-start.10 = (s32[1,1,16,2]{2,3,1,0:T(2,128)S(1)}, s32[1,1,16,2]{2,3,1,0:T(2,128)}, u32[]{:S(2)}) copy-start(s32[1,1,16,2]{2,3,1,0:T(2,128)} %param.15) | copy-start | bytes 388
  2.8 8.3 %copy-start.1 = (bf16[16,128,128]{2,1,0:T(8,128)(2,1)S(1)}, bf16[16,128,128]{2,1,0:T(8,128)(2,1)}, u32[]{:S(2)}) copy-start(bf16[16,128,128]{2,1,0:T(8,128)(2,1)} %anchor_ref.5) | copy-start | bytes 1572868
  2.9 8.3 %copy-start.8 = (s32[1,1,16]{2,1,0:T(1,128)S(1)}, s32[1,1,16]{2,1,0:T(1,128)}, u32[]{:S(2)}) copy-start(s32[1,1,16]{2,1,0:T(1,128)} %count_ref.1) | copy-start | bytes 196
  2.9 8.3 %collective-permute-start.1 = (bf16[16,1024]{1,0:T(8,128)(2,1)S(1)}, bf16[16,1024]{1,0:T(8,128)(2,1)S(1)}, u32[]{:S(2)}, u32[]{:S(2)}) collective-permute-start(bf16[16,1024]{1,0:T(8,128)(2,1)S(1)} %get-tuple-element.20), channel_id=1, source_target_pairs={{1,0},{2,1},{3,2},{4,3},{5,4},{6,5},{7,6},{8,7},{9,8},{10,9},{11,1... | collective-permute-start | bytes 98312 | tf_op jit(solution)/shard_map/ppermute | solution.py:299
  11.0 11.7 %copy-start.11 = (s32[1,16,1,2]{1,3,2,0:T(2,128)S(1)}, s32[1,16,1,2]{1,3,2,0:T(2,128)}, u32[]{:S(2)}) copy-start(s32[1,16,1,2]{1,3,2,0:T(2,128)} %param.16) | copy-start | bytes 388
  13.4 33.7 %copy-start = (bf16[1280,128]{1,0:T(8,128)(2,1)S(1)}, bf16[1280,128]{1,0:T(8,128)(2,1)}, u32[]{:S(2)}) copy-start(bf16[1280,128]{1,0:T(8,128)(2,1)} %constant.16.clone.refs_2_) | copy-start | bytes 983044
  13.4 33.7 %copy-start.2 = (bf16[256,256]{1,0:T(8,128)(2,1)S(1)}, bf16[256,256]{1,0:T(8,128)(2,1)}, u32[]{:S(2)}) copy-start(bf16[256,256]{1,0:T(8,128)(2,1)} %constant.15.clone.refs_1_) | copy-start | bytes 393220
  13.4 33.7 %copy-start.3 = (bf16[256,256]{1,0:T(8,128)(2,1)S(1)}, bf16[256,256]{1,0:T(8,128)(2,1)}, u32[]{:S(2)}) copy-start(bf16[256,256]{1,0:T(8,128)(2,1)} %constant.14.clone.refs_0_) | copy-start | bytes 393220
  13.4 20.1 %all-to-all-start = ((bf16[16,2,128,128]{3,2,1,0:T(8,128)(2,1)}), bf16[16,2,128,128]{3,2,1,0:T(8,128)(2,1)S(1)}, u32[]{:S(2)}, u32[]{:S(2)}) async-start(bf16[16,2,128,128]{3,2,1,0:T(8,128)(2,1)} %get-tuple-element.23), calls=%async_computation | async-start | bytes 2097152 | tf_op jit(solution)/shard_map/all_to_all | solution.py:321
  18.4 12.5 %collective-permute-start.2 = (bf16[1,128,128]{2,1,0:T(8,128)(2,1)S(1)}, bf16[1,128,128]{2,1,0:T(8,128)(2,1)S(1)}, u32[]{:S(2)}, u32[]{:S(2)}) collective-permute-start(bf16[1,128,128]{2,1,0:T(8,128)(2,1)S(1)} %get-tuple-element.24), channel_id=1, source_target_pairs={{1,0},{2,1},{3,2},{4,3},{5,4},{6,5},{7,6},{8,7},{9,8},{10,9},{11,1... | collective-permute-start | bytes 98312 | tf_op jit(solution)/shard_map/ppermute | solution.py:322
  34.5 32.3 %copy-start.4 = (bf16[256,256]{1,0:T(8,128)(2,1)S(1)}, bf16[256,256]{1,0:T(8,128)(2,1)}, u32[]{:S(2)}) copy-start(bf16[256,256]{1,0:T(8,128)(2,1)} %constant.18.clone.refs_4_) | copy-start | bytes 393220
  34.6 32.3 %copy-start.5 = (bf16[256,256]{1,0:T(8,128)(2,1)S(1)}, bf16[256,256]{1,0:T(8,128)(2,1)}, u32[]{:S(2)}) copy-start(bf16[256,256]{1,0:T(8,128)(2,1)} %constant.17.clone.refs_3_) | copy-start | bytes 393220
  34.6 18.5 %collective-permute-start.3 = (bf16[8,128,128]{2,1,0:T(8,128)(2,1)S(1)}, bf16[8,128,128]{2,1,0:T(8,128)(2,1)S(1)}, u32[]{:S(2)}, u32[]{:S(2)}) collective-permute-start(bf16[8,128,128]{2,1,0:T(8,128)(2,1)S(1)} %get-tuple-element.26.a_ref), channel_id=1, source_target_pairs={{0,16},{1,17},{2,18},{3,19},{4,20},{5,21},{6,22},{7,23},{8,24},{9,... | collective-permute-start | bytes 786440 | tf_op jit(solution)/shard_map/ppermute | solution.py:356
  38.6 4.7 %collective-permute-start.4 = (bf16[1,128,128]{2,1,0:T(8,128)(2,1)S(1)}, bf16[1,128,128]{2,1,0:T(8,128)(2,1)S(1)}, u32[]{:S(2)}, u32[]{:S(2)}) collective-permute-start(bf16[1,128,128]{2,1,0:T(8,128)(2,1)S(1)} %get-tuple-element.29), channel_id=1, source_target_pairs={{1,0},{2,1},{3,2},{4,3},{5,4},{6,5},{7,6},{8,7},{9,8},{10,9},{11,1... | collective-permute-start | bytes 98312 | tf_op jit(solution)/shard_map/ppermute | solution.py:357
  43.3 25.9 %collective-permute-start.6 = (bf16[9,128,128]{2,1,0:T(8,128)(2,1)S(1)}, bf16[9,128,128]{2,1,0:T(8,128)(2,1)S(1)}, u32[]{:S(2)}, u32[]{:S(2)}) collective-permute-start(bf16[9,128,128]{2,1,0:T(8,128)(2,1)S(1)} %constant_dynamic-update-slice_fusion.b_ref), channel_id=1, source_target_pairs={{0,16},{16,32},{32,48},{48,64},{64,80},{80,96},{96,112},{112,128},... | collective-permute-start | bytes 884744 | tf_op jit(solution)/shard_map/ppermute | solution.py:359
  53.0 13.8 %collective-permute-start.5 = (bf16[8,128,128]{2,1,0:T(8,128)(2,1)S(1)}, bf16[8,128,128]{2,1,0:T(8,128)(2,1)S(1)}, u32[]{:S(2)}, u32[]{:S(2)}) collective-permute-start(bf16[8,128,128]{2,1,0:T(8,128)(2,1)S(1)} %collective-permute-done.3.a_ref), channel_id=1, source_target_pairs={{264,256},{265,257},{266,258},{267,259},{268,260},{269,261},{270,2... | collective-permute-start | bytes 786440 | tf_op jit(solution)/shard_map/ppermute | solution.py:375

commit v4 on v3

--- a/solution.py
+++ b/solution.py
@@ -9,8 +9,8 @@
 B = 128
 H = B // 2
 EDGE = 16
-EARLY = 8
-PAIRS = 9
+EARLY = 11
+PAIRS = 10
 F32 = jnp.float32
 BF16 = jnp.bfloat16
 VMEM_LIMIT = 48 * 2**20
@@ -232,22 +232,17 @@
         send.wait()
 
 
-def prior_block(anchor, direct, relayed):
-    sec = lax.axis_index("sec")
-    chosen = jnp.where(sec == lax.axis_size("sec") // 2, relayed, direct)
-    return jnp.where(sec == 0, anchor, chosen)
-
-
-def correlate_early(cur_ref, a_ref, relay_ref, anchor_ref, *refs):
-    blocks = [prior_block(anchor_ref[m], a_ref[m], relay_ref[m]) for m in range(EARLY)]
+def correlate_early(cur_ref, a_ref, anchor_ref, *refs):
+    is_first = lax.axis_index("sec") == 0
+    blocks = [jnp.where(is_first, anchor_ref[m], a_ref[m]) for m in range(EARLY)]
     correlate_chunk(cur_ref, blocks, refs[:5], refs[5], 0, *refs[6:])
 
 
-def correlate_late(held, cur_ref, a_ref, relay_ref, b_ref, anchor_ref, border_ref, *refs):
+def correlate_late(held, cur_ref, a_ref, b_ref, anchor_ref, border_ref, *refs):
     del held
     is_first = lax.axis_index("sec") == 0
     rest = b_ref.shape[0] - 1
-    blocks = [prior_block(anchor_ref[EARLY - 1], a_ref[EARLY - 1], relay_ref[EARLY - 1])]
+    blocks = [jnp.where(is_first, anchor_ref[EARLY - 1], a_ref[EARLY - 1])]
     blocks += [jnp.where(is_first, anchor_ref[EARLY + m], b_ref[m]) for m in range(rest)]
     blocks += [jnp.where(is_first, border_ref[0], b_ref[rest])]
     correlate_chunk(cur_ref, blocks, refs[:5], refs[5], EARLY - 1, *refs[6:])
@@ -341,19 +336,8 @@
         6 * EARLY * B * B,
         (part_a, rest),
     )
-    turn, side = sections // 2, strips // 2
-    by_relay, forward_on = [], []
-    for s in range(sections - 1):
-        for d in range(strips):
-            here, there = s * strips + d, (s + 1) * strips + d
-            if s + 1 == turn:
-                relay = there + side if d < side else d - side
-                by_relay.append((here, relay))
-                forward_on.append((relay, there))
-            else:
-                by_relay.append((here, there))
     on = [(i, i + 1) for i in range(sections - 1)]
-    prior_a = lax.ppermute(part_a, ("sec", "tile"), by_relay)
+    prior_a = lax.ppermute(part_a, "sec", on)
     own_rim = lax.ppermute(first, "tile", back)
     part_b = lax.dynamic_update_slice(part_b, own_rim, (count - EARLY, 0, 0))
     prior_b = lax.ppermute(part_b, "sec", on)
@@ -371,8 +355,6 @@
     )
     spectra_a = current(early_kernel, early, part_a)
     spectra_b = current(late_kernel, late, part_a, part_b)
-    prior_a, spectra_b = lax.optimization_barrier((prior_a, spectra_b))
-    relayed_a = lax.ppermute(prior_a, ("sec", "tile"), forward_on)
     result = shape((1, 2 * count, B, B), F32)
     scratch = lambda pairs: [
         pltpu.VMEM((pairs + 1, 2 * B, B), F32),
@@ -383,22 +365,22 @@
     held = call(
         correlate_early,
         result,
-        [VMEM] * 9,
+        [VMEM] * 8,
         HBM,
         scratch(early),
         2**10,
         2**10,
-        (spectra_a, prior_a, relayed_a, anchor, right, left, middle, back_left, back_right),
+        (spectra_a, prior_a, anchor, right, left, middle, back_left, back_right),
     )
     return call(
         correlate_late,
         result,
-        [HBM] + [VMEM] * 11,
+        [HBM] + [VMEM] * 10,
         HBM,
         scratch(late),
         2**30,
         2**22,
-        (held, spectra_b, prior_a, relayed_a, prior_b, anchor, border, right, left, middle, back_left, back_right),
+        (held, spectra_b, prior_a, prior_b, anchor, border, right, left, middle, back_left, back_right),
         aliases={0: 0},
     )
 

time: 72.4 us -> 62.1 us (0.86)
  waiting for transfers between devices: 28.3 us -> 20.2 us
  starting transfers between devices: 29.9 us -> 28 us
    ppermute x2 -> x1, waiting for transfers between devices: 16 us -> 6.49 us  [body(): prior_a = lax.ppermute(part_a, 'sec', on)]
    ppermute x2 -> x1, starting transfers between devices: 5.87 us -> 3.96 us  [body(): prior_a = lax.ppermute(part_a, 'sec', on)]
    ppermute x1, waiting for transfers between devices: 0.01 us -> 1.46 us  [body(): prior_b = lax.ppermute(part_b, 'sec', on)]
  transfers between devices with their start and end apart: 8 -> 7, of which waited for: 5 -> 5; matrix products, arithmetic and copies ran while one was open for 0% -> 0% of each run, Pallas kernels for 9% -> 11%
where the time goes in v4:
time: 62.1 us; the launch traced here: 61.5 us
  starting transfers between devices  28 us (45%)
  waiting for transfers between devices  20.2 us (33%)
  Pallas kernels  12.8 us (21%)
    pallas_call x9, Pallas kernels, call(): pl.pallas_call(kernel, out_shape=out_shape, in_specs=in_specs, out_specs=...  12.8 us
    ppermute x1, waiting for transfers between devices, body(): border = lax.ppermute(anchor_first, 'tile', back)  8.11 us
    ppermute x1, waiting for transfers between devices, body(): prior_a = lax.ppermute(part_a, 'sec', on)  6.49 us
    ppermute x1, starting transfers between devices, body(): high = lax.ppermute(head, 'tile', back)  5.88 us
    all_to_all x1, starting transfers between devices, body(): lax.all_to_all(outgoing, 'tile', split_axis=0, concat_axis=0, tiled=True)  5.03 us
    ppermute x1, starting transfers between devices, body(): border = lax.ppermute(anchor_first, 'tile', back)  4.32 us
    ppermute x1, starting transfers between devices, body(): prior_a = lax.ppermute(part_a, 'sec', on)  3.96 us
    ppermute x1, starting transfers between devices, body(): prior_b = lax.ppermute(part_b, 'sec', on)  3.82 us
  transfers between devices with their start and end apart: 7, of which 5 were waited for; matrix products, arithmetic and copies ran while one was open for 0% of the time, Pallas kernels for 11%

profile of v4, /device:TPU:24, one launch (start us, length us, event | category | flops | bytes accessed | tf_op | source)
XLA Modules:
  0.0 61.5 jit_solution(14472713662219058155)
XLA Ops:
  0.0 0.0 copy-start.9
  0.0 0.0 copy-start.7
  0.0 0.0 copy-start.4
  0.0 0.9 %shard_map.118 = (bf16[16,1024]{1,0:T(8,128)(2,1)S(1)}, bf16[16,1024]{1,0:T(8,128)(2,1)S(1)}) custom-call(bf16[1,256,1024]{2,1,0:T(8,128)(2,1)} %image_ref.1), custom_call_target="tpu_custom_call" | custom-call | flops 8589934592 | bytes 131072 | tf_op jit(solution)/shard_map/pallas_call | solution.py:259
  0.9 1.9 %collective-permute-start = (bf16[16,1024]{1,0:T(8,128)(2,1)S(1)}, bf16[16,1024]{1,0:T(8,128)(2,1)S(1)}, u32[]{:S(2)}, u32[]{:S(2)}) collective-permute-start(bf16[16,1024]{1,0:T(8,128)(2,1)S(1)} %get-tuple-element.17), channel_id=1, source_target_pairs={{0,1},{1,2},{2,3},{3,4},{4,5},{5,6},{6,7},{7,8},{8,9},{9,10},{10,1... | collective-permute-start | bytes 98312 | tf_op jit(solution)/shard_map/ppermute | solution.py:293
  2.8 0.0 copy-start.10
  2.8 0.0 copy-start.1
  2.9 0.0 copy-start.8
  2.9 5.9 %collective-permute-start.1 = (bf16[16,1024]{1,0:T(8,128)(2,1)S(1)}, bf16[16,1024]{1,0:T(8,128)(2,1)S(1)}, u32[]{:S(2)}, u32[]{:S(2)}) collective-permute-start(bf16[16,1024]{1,0:T(8,128)(2,1)S(1)} %get-tuple-element.18), channel_id=1, source_target_pairs={{1,0},{2,1},{3,2},{4,3},{5,4},{6,5},{7,6},{8,7},{9,8},{10,9},{11,1... | collective-permute-start | bytes 98312 | tf_op jit(solution)/shard_map/ppermute | solution.py:294
  8.8 0.0 copy-done.9
  8.8 0.0 copy-done.7
  8.8 0.0 copy-done.4
  8.8 2.2 %shard_map.119 = (bf16[16,128,128]{2,1,0:T(8,128)(2,1)S(1)}, f32[32,1024]{1,0:T(8,128)S(1)}) custom-call(f32[1,1,25]{2,1,0:T(1,128)S(1)} %copy-done.7, bf16[1,256,1024]{2,1,0:T(8,128)(2,1)S(1)} %copy-done.9, bf16[1,256,1024]{2,1,0:T(8,128)(2,1)S(1)} %copy-done.4), custom_call_target="tpu_custom_call" | custom-call | flops 1342177280 | bytes 1572864 | tf_op jit(solution)/shard_map/pallas_call | solution.py:259
  11.0 0.0 copy-done.10
  11.0 0.0 copy-start.11
  11.0 0.1 copy.14.src_ref
  11.1 0.0 collective-permute-done.low_ref
  11.1 0.0 collective-permute-done.1.high_ref
  11.1 0.0 copy-done.1
  11.1 0.0 copy-done.8
  11.2 2.2 %shard_map.120 = (bf16[16,2,128,128]{3,2,1,0:T(8,128)(2,1)}, bf16[1,128,128]{2,1,0:T(8,128)(2,1)S(1)}) custom-call(f32[1,1,25]{2,1,0:T(1,128)S(1)} %copy-done.7, s32[1,1,16,2]{3,2,1,0:T(8,128)S(1)} %copy.14.src_ref, s32[1,1,16]{2,1,0:T(1,128)S(1)} %copy-done.8, bf16[16,1024]{1,0:T(8,128)(2,1)S(1)} %collective-permute-done.low_ref, ...), custom_call_target="tpu_custom_call" | custom-call | flops 1048576 | bytes 2097152 | tf_op jit(solution)/shard_map/pallas_call | solution.py:259
  13.4 0.0 copy-start
  13.4 0.0 copy-start.2
  13.4 0.0 copy-start.3
  13.4 5.0 %all-to-all-start = ((bf16[16,2,128,128]{3,2,1,0:T(8,128)(2,1)}), bf16[16,2,128,128]{3,2,1,0:T(8,128)(2,1)S(1)}, u32[]{:S(2)}, u32[]{:S(2)}) async-start(bf16[16,2,128,128]{3,2,1,0:T(8,128)(2,1)} %get-tuple-element.21), calls=%async_computation | async-start | bytes 2097152 | tf_op jit(solution)/shard_map/all_to_all | solution.py:316
  18.4 4.3 %collective-permute-start.2 = (bf16[1,128,128]{2,1,0:T(8,128)(2,1)S(1)}, bf16[1,128,128]{2,1,0:T(8,128)(2,1)S(1)}, u32[]{:S(2)}, u32[]{:S(2)}) collective-permute-start(bf16[1,128,128]{2,1,0:T(8,128)(2,1)S(1)} %get-tuple-element.22), channel_id=1, source_target_pairs={{1,0},{2,1},{3,2},{4,3},{5,4},{6,5},{7,6},{8,7},{9,8},{10,9},{11,1... | collective-permute-start | bytes 98312 | tf_op jit(solution)/shard_map/ppermute | solution.py:317
  22.7 0.0 copy-done.11
  22.8 0.1 copy.15.dst_ref
  22.8 8.1 %collective-permute-done.2.border_ref = bf16[1,128,128]{2,1,0:T(8,128)(2,1)S(1)} collective-permute-done((bf16[1,128,128]{2,1,0:T(8,128)(2,1)S(1)}, bf16[1,128,128]{2,1,0:T(8,128)(2,1)S(1)}, u32[]{:S(2)}, u32[]{:S(2)}) %collective-permute-start.2) | collective-permute-done | bytes 32800 | tf_op jit(solution)/shard_map/ppermute | solution.py:317
  31.0 2.6 %all-to-all-done.in_ref = bf16[16,2,128,128]{3,2,1,0:T(8,128)(2,1)S(1)} async-done(((bf16[16,2,128,128]{3,2,1,0:T(8,128)(2,1)}), bf16[16,2,128,128]{3,2,1,0:T(8,128)(2,1)S(1)}, u32[]{:S(2)}, u32[]{:S(2)}) %all-to-all-start) | async-done | bytes 1048608 | tf_op jit(solution)/shard_map/all_to_all | solution.py:316
  33.5 1.0 %shard_map.121 = (bf16[11,128,128]{2,1,0:T(8,128)(2,1)S(1)}, f32[5,128,128]{2,1,0:T(8,128)S(1)}) custom-call(s32[1,16,1,2]{3,2,1,0:T(1,128)S(1)} %copy.15.dst_ref, bf16[16,2,128,128]{3,2,1,0:T(8,128)(2,1)S(1)} %all-to-all-done.in_ref), custom_call_target="tpu_custom_call" | custom-call | flops 1048576 | bytes 2097152 | tf_op jit(solution)/shard_map/pallas_call | solution.py:259
  34.5 0.0 copy-start.5
  34.5 0.0 copy-start.6
  34.6 4.0 %collective-permute-start.3 = (bf16[11,128,128]{2,1,0:T(8,128)(2,1)S(1)}, bf16[11,128,128]{2,1,0:T(8,128)(2,1)S(1)}, u32[]{:S(2)}, u32[]{:S(2)}) collective-permute-start(bf16[11,128,128]{2,1,0:T(8,128)(2,1)S(1)} %get-tuple-element.24.a_ref), channel_id=1, source_target_pairs={{0,16},{16,32},{32,48},{48,64},{64,80},{80,96},{96,112},{112,128},... | collective-permute-start | bytes 1081352 | tf_op jit(solution)/shard_map/ppermute | solution.py:340
  38.6 3.1 %collective-permute-start.4 = (bf16[1,128,128]{2,1,0:T(8,128)(2,1)S(1)}, bf16[1,128,128]{2,1,0:T(8,128)(2,1)S(1)}, u32[]{:S(2)}, u32[]{:S(2)}) collective-permute-start(bf16[1,128,128]{2,1,0:T(8,128)(2,1)S(1)} %get-tuple-element.27), channel_id=1, source_target_pairs={{1,0},{2,1},{3,2},{4,3},{5,4},{6,5},{7,6},{8,7},{9,8},{10,9},{11,1... | collective-permute-start | bytes 98312 | tf_op jit(solution)/shard_map/ppermute | solution.py:341
  41.7 1.6 %collective-permute-done.4 = bf16[1,128,128]{2,1,0:T(8,128)(2,1)S(1)} collective-permute-done((bf16[1,128,128]{2,1,0:T(8,128)(2,1)S(1)}, bf16[1,128,128]{2,1,0:T(8,128)(2,1)S(1)}, u32[]{:S(2)}, u32[]{:S(2)}) %collective-permute-start.4) | collective-permute-done | bytes 32800 | tf_op jit(solution)/shard_map/ppermute | solution.py:341
  43.3 3.8 %collective-permute-start.5 = (bf16[6,128,128]{2,1,0:T(8,128)(2,1)S(1)}, bf16[6,128,128]{2,1,0:T(8,128)(2,1)S(1)}, u32[]{:S(2)}, u32[]{:S(2)}) collective-permute-start(bf16[6,128,128]{2,1,0:T(8,128)(2,1)S(1)} %constant_dynamic-update-slice_fusion.b_ref), channel_id=1, source_target_pairs={{0,16},{16,32},{32,48},{48,64},{64,80},{80,96},{96,112},{112,128},... | collective-permute-start | bytes 589832 | tf_op jit(solution)/shard_map/ppermute | solution.py:343
  47.1 0.0 copy-done
  47.1 0.0 copy-done.2
  47.1 0.0 copy-done.3
  47.1 0.9 %shard_map.122.cur_ref = bf16[256,1408]{1,0:T(8,128)(2,1)S(1)} custom-call(bf16[11,128,128]{2,1,0:T(8,128)(2,1)S(1)} %get-tuple-element.24.a_ref, bf16[256,256]{1,0:T(8,128)(2,1)S(1)} %copy-done.3, bf16[256,256]{1,0:T(8,128)(2,1)S(1)} %copy-done.2, bf16[1408,128]{1,0:T(8,128)(2,1)S(1)} %copy-done), custom_call_target="tpu_custom_call" | custom-call | flops 1024 | bytes 1024 | tf_op jit(solution)/shard_map/pallas_call | solution.py:259
  48.0 0.8 %shard_map.125.cur_ref = bf16[256,896]{1,0:T(8,128)(2,1)S(1)} custom-call(bf16[11,128,128]{2,1,0:T(8,128)(2,1)S(1)} %get-tuple-element.24.a_ref, bf16[6,128,128]{2,1,0:T(8,128)(2,1)S(1)} %constant_dynamic-update-slice_fusion.b_ref, bf16[256,256]{1,0:T(8,128)(2,1)S(1)} %copy-done.3, bf16[256,256]{1,0:T(8,128)(2,1)S(1)} %copy-done.2, bf16[1408,128]{1,0:T(8,128)(2,1)S(1)} %copy-done), custom_call_target="tpu_custom_call" | custom-call | flops 1024 | bytes 1024 | tf_op jit(solution)/shard_map/pallas_call | solution.py:259
  48.8 6.5 %collective-permute-done.3.a_ref = bf16[11,128,128]{2,1,0:T(8,128)(2,1)S(1)} collective-permute-done((bf16[11,128,128]{2,1,0:T(8,128)(2,1)S(1)}, bf16[11,128,128]{2,1,0:T(8,128)(2,1)S(1)}, u32[]{:S(2)}, u32[]{:S(2)}) %collective-permute-start.3) | collective-permute-done | bytes 360480 | tf_op jit(solution)/shard_map/ppermute | solution.py:340
  55.3 0.0 copy-done.5
  55.3 0.0 copy-done.6
  55.3 2.6 %shard_map.123.held = f32[1,32,128,128]{3,2,1,0:T(8,128)} custom-call(bf16[256,1408]{1,0:T(8,128)(2,1)S(1)} %shard_map.122.cur_ref, bf16[11,128,128]{2,1,0:T(8,128)(2,1)S(1)} %collective-permute-done.3.a_ref, bf16[16,128,128]{2,1,0:T(8,128)(2,1)S(1)} %copy-done.1, bf16[256,256]{1,0:T(8,128)(2,1)S(1)} %copy-done.3, bf16[256,256]{1,0:T(8,128)(2,1)S(1)} %copy-done.2, ...), custom_call_target="tpu_custom_call" | custom-call | flops 1024 | bytes 1024 | tf_op jit(solution)/shard_map/pallas_call | solution.py:259
  57.9 1.5 %collective-permute-done.5.b_ref = bf16[6,128,128]{2,1,0:T(8,128)(2,1)S(1)} collective-permute-done((bf16[6,128,128]{2,1,0:T(8,128)(2,1)S(1)}, bf16[6,128,128]{2,1,0:T(8,128)(2,1)S(1)}, u32[]{:S(2)}, u32[]{:S(2)}) %collective-permute-start.5) | collective-permute-done | bytes 196640 | tf_op jit(solution)/shard_map/ppermute | solution.py:343
  59.3 2.2 %shard_map.126 = f32[1,32,128,128]{3,2,1,0:T(8,128)} custom-call(f32[1,32,128,128]{3,2,1,0:T(8,128)} %shard_map.123.held, bf16[256,896]{1,0:T(8,128)(2,1)S(1)} %shard_map.125.cur_ref, bf16[11,128,128]{2,1,0:T(8,128)(2,1)S(1)} %collective-permute-done.3.a_ref, bf16[6,128,128]{2,1,0:T(8,128)(2,1)S(1)} %collective-permute-done.5.b_ref, ...), custom_call_target="tpu_custom_call", output_to_operand_aliasing={{}: (0, {})} | custom-call | flops 1073741824 | bytes 4194304 | tf_op jit(solution)/shard_map/pallas_call | solution.py:259
  (2 shorter events, 0.0 us)
Async XLA Ops:
  0.0 8.8 %copy-start.9 = (bf16[1,256,1024]{2,1,0:T(8,128)(2,1)S(1)}, bf16[1,256,1024]{2,1,0:T(8,128)(2,1)}, u32[]{:S(2)}) copy-start(bf16[1,256,1024]{2,1,0:T(8,128)(2,1)} %image_ref.1) | copy-start | bytes 1572868
  0.0 8.8 %copy-start.7 = (f32[1,1,25]{2,1,0:T(1,128)S(1)}, f32[1,1,25]{2,1,0:T(1,128)}, u32[]{:S(2)}) copy-start(f32[1,1,25]{2,1,0:T(1,128)} %taps_ref.3) | copy-start | bytes 304
  0.0 8.8 %copy-start.4 = (bf16[1,256,1024]{2,1,0:T(8,128)(2,1)S(1)}, bf16[1,256,1024]{2,1,0:T(8,128)(2,1)}, u32[]{:S(2)}) copy-start(bf16[1,256,1024]{2,1,0:T(8,128)(2,1)} %weight_ref.3) | copy-start | bytes 1572868
  0.9 10.2 %collective-permute-start = (bf16[16,1024]{1,0:T(8,128)(2,1)S(1)}, bf16[16,1024]{1,0:T(8,128)(2,1)S(1)}, u32[]{:S(2)}, u32[]{:S(2)}) collective-permute-start(bf16[16,1024]{1,0:T(8,128)(2,1)S(1)} %get-tuple-element.17), channel_id=1, source_target_pairs={{0,1},{1,2},{2,3},{3,4},{4,5},{5,6},{6,7},{7,8},{8,9},{9,10},{10,1... | collective-permute-start | bytes 98312 | tf_op jit(solution)/shard_map/ppermute | solution.py:293
  2.8 8.2 %copy-start.10 = (s32[1,1,16,2]{2,3,1,0:T(2,128)S(1)}, s32[1,1,16,2]{2,3,1,0:T(2,128)}, u32[]{:S(2)}) copy-start(s32[1,1,16,2]{2,3,1,0:T(2,128)} %param.15) | copy-start | bytes 388
  2.8 8.3 %copy-start.1 = (bf16[16,128,128]{2,1,0:T(8,128)(2,1)S(1)}, bf16[16,128,128]{2,1,0:T(8,128)(2,1)}, u32[]{:S(2)}) copy-start(bf16[16,128,128]{2,1,0:T(8,128)(2,1)} %anchor_ref.5) | copy-start | bytes 1572868
  2.9 8.3 %copy-start.8 = (s32[1,1,16]{2,1,0:T(1,128)S(1)}, s32[1,1,16]{2,1,0:T(1,128)}, u32[]{:S(2)}) copy-start(s32[1,1,16]{2,1,0:T(1,128)} %count_ref.1) | copy-start | bytes 196
  2.9 8.3 %collective-permute-start.1 = (bf16[16,1024]{1,0:T(8,128)(2,1)S(1)}, bf16[16,1024]{1,0:T(8,128)(2,1)S(1)}, u32[]{:S(2)}, u32[]{:S(2)}) collective-permute-start(bf16[16,1024]{1,0:T(8,128)(2,1)S(1)} %get-tuple-element.18), channel_id=1, source_target_pairs={{1,0},{2,1},{3,2},{4,3},{5,4},{6,5},{7,6},{8,7},{9,8},{10,9},{11,1... | collective-permute-start | bytes 98312 | tf_op jit(solution)/shard_map/ppermute | solution.py:294
  11.0 11.7 %copy-start.11 = (s32[1,16,1,2]{1,3,2,0:T(2,128)S(1)}, s32[1,16,1,2]{1,3,2,0:T(2,128)}, u32[]{:S(2)}) copy-start(s32[1,16,1,2]{1,3,2,0:T(2,128)} %param.16) | copy-start | bytes 388
  13.4 33.7 %copy-start = (bf16[1408,128]{1,0:T(8,128)(2,1)S(1)}, bf16[1408,128]{1,0:T(8,128)(2,1)}, u32[]{:S(2)}) copy-start(bf16[1408,128]{1,0:T(8,128)(2,1)} %constant.16.clone.refs_2_) | copy-start | bytes 1081348
  13.4 33.7 %copy-start.2 = (bf16[256,256]{1,0:T(8,128)(2,1)S(1)}, bf16[256,256]{1,0:T(8,128)(2,1)}, u32[]{:S(2)}) copy-start(bf16[256,256]{1,0:T(8,128)(2,1)} %constant.15.clone.refs_1_) | copy-start | bytes 393220
  13.4 33.7 %copy-start.3 = (bf16[256,256]{1,0:T(8,128)(2,1)S(1)}, bf16[256,256]{1,0:T(8,128)(2,1)}, u32[]{:S(2)}) copy-start(bf16[256,256]{1,0:T(8,128)(2,1)} %constant.14.clone.refs_0_) | copy-start | bytes 393220
  13.4 20.1 %all-to-all-start = ((bf16[16,2,128,128]{3,2,1,0:T(8,128)(2,1)}), bf16[16,2,128,128]{3,2,1,0:T(8,128)(2,1)S(1)}, u32[]{:S(2)}, u32[]{:S(2)}) async-start(bf16[16,2,128,128]{3,2,1,0:T(8,128)(2,1)} %get-tuple-element.21), calls=%async_computation | async-start | bytes 2097152 | tf_op jit(solution)/shard_map/all_to_all | solution.py:316
  18.4 12.5 %collective-permute-start.2 = (bf16[1,128,128]{2,1,0:T(8,128)(2,1)S(1)}, bf16[1,128,128]{2,1,0:T(8,128)(2,1)S(1)}, u32[]{:S(2)}, u32[]{:S(2)}) collective-permute-start(bf16[1,128,128]{2,1,0:T(8,128)(2,1)S(1)} %get-tuple-element.22), channel_id=1, source_target_pairs={{1,0},{2,1},{3,2},{4,3},{5,4},{6,5},{7,6},{8,7},{9,8},{10,9},{11,1... | collective-permute-start | bytes 98312 | tf_op jit(solution)/shard_map/ppermute | solution.py:317
  34.5 20.8 %copy-start.5 = (bf16[256,256]{1,0:T(8,128)(2,1)S(1)}, bf16[256,256]{1,0:T(8,128)(2,1)}, u32[]{:S(2)}) copy-start(bf16[256,256]{1,0:T(8,128)(2,1)} %constant.18.clone.refs_4_) | copy-start | bytes 393220
  34.5 20.7 %copy-start.6 = (bf16[256,256]{1,0:T(8,128)(2,1)S(1)}, bf16[256,256]{1,0:T(8,128)(2,1)}, u32[]{:S(2)}) copy-start(bf16[256,256]{1,0:T(8,128)(2,1)} %constant.17.clone.refs_3_) | copy-start | bytes 393220
  34.6 20.7 %collective-permute-start.3 = (bf16[11,128,128]{2,1,0:T(8,128)(2,1)S(1)}, bf16[11,128,128]{2,1,0:T(8,128)(2,1)S(1)}, u32[]{:S(2)}, u32[]{:S(2)}) collective-permute-start(bf16[11,128,128]{2,1,0:T(8,128)(2,1)S(1)} %get-tuple-element.24.a_ref), channel_id=1, source_target_pairs={{0,16},{16,32},{32,48},{48,64},{64,80},{80,96},{96,112},{112,128},... | collective-permute-start | bytes 1081352 | tf_op jit(solution)/shard_map/ppermute | solution.py:340
  38.6 4.7 %collective-permute-start.4 = (bf16[1,128,128]{2,1,0:T(8,128)(2,1)S(1)}, bf16[1,128,128]{2,1,0:T(8,128)(2,1)S(1)}, u32[]{:S(2)}, u32[]{:S(2)}) collective-permute-start(bf16[1,128,128]{2,1,0:T(8,128)(2,1)S(1)} %get-tuple-element.27), channel_id=1, source_target_pairs={{1,0},{2,1},{3,2},{4,3},{5,4},{6,5},{7,6},{8,7},{9,8},{10,9},{11,1... | collective-permute-start | bytes 98312 | tf_op jit(solution)/shard_map/ppermute | solution.py:341
  43.3 16.1 %collective-permute-start.5 = (bf16[6,128,128]{2,1,0:T(8,128)(2,1)S(1)}, bf16[6,128,128]{2,1,0:T(8,128)(2,1)S(1)}, u32[]{:S(2)}, u32[]{:S(2)}) collective-permute-start(bf16[6,128,128]{2,1,0:T(8,128)(2,1)S(1)} %constant_dynamic-update-slice_fusion.b_ref), channel_id=1, source_target_pairs={{0,16},{16,32},{32,48},{48,64},{64,80},{80,96},{96,112},{112,128},... | collective-permute-start | bytes 589832 | tf_op jit(solution)/shard_map/ppermute | solution.py:343

commit v5 on v4

--- a/solution.py
+++ b/solution.py
@@ -72,14 +72,15 @@
     return jnp.concatenate([jnp.concatenate(high, 1), jnp.concatenate(low, 1)], 0)
 
 
-def prepare_kernel(image, last, head, sems):
-    rows = image.shape[1]
-    pairs = ((image.at[0, pl.ds(rows - EDGE, EDGE)], last), (image.at[0, pl.ds(0, EDGE)], head))
-    copies = [pltpu.make_async_copy(whence, where, sems.at[n]) for n, (whence, where) in enumerate(pairs)]
-    for copy in copies:
-        copy.start()
-    for copy in copies:
-        copy.wait()
+def prepare_kernel(image, inner, outer, sems):
+    last = image.shape[1] - EDGE
+    odd = lax.rem(lax.axis_index("tile"), 2)
+    to_inner = pltpu.make_async_copy(image.at[0, pl.ds(pl.multiple_of((1 - odd) * last, EDGE), EDGE)], inner, sems.at[0])
+    to_outer = pltpu.make_async_copy(image.at[0, pl.ds(pl.multiple_of(odd * last, EDGE), EDGE)], outer, sems.at[1])
+    to_inner.start()
+    to_outer.start()
+    to_inner.wait()
+    to_outer.wait()
 
 
 def lens_kernel(taps_ref, image_ref, weight_ref, blocks_ref, edge_ref):
@@ -101,35 +102,53 @@
 
 
 def pick_kernel(
-    taps_ref, src_ref, count_ref, low_ref, high_ref, edge_ref, weight_ref, blocks_ref, anchor_ref, out, first_ref, fixed_ref, out_sems
+    taps_ref, src_ref, count_ref, inner_ref, outer_ref, edge_ref, weight_ref, blocks_ref, anchor_ref, out, first_ref, zero_ref, fixed_ref, sems
 ):
     rows, cols = weight_ref.shape[1:]
     across = cols // B
     count = rows // B * across
-    for k in range(count):
-        fixed_ref[k] = blocks_ref[k]
-    fixed_ref[count] = jnp.zeros((B, B), BF16)
+    zero_ref[...] = jnp.zeros((B, B), BF16)
+    fixed_ref[count] = jnp.zeros((EDGE, B), BF16)
     first_ref[0] = anchor_ref[0]
+    inside = B - EDGE
+    sends, edges = [], []
+    for d in range(out.shape[0]):
+        for q in range(out.shape[1]):
+            live = q < count_ref[0, 0, d]
+            block = src_ref[0, 0, d, q]
+            upper = block < across
+            at = pl.multiple_of(jnp.where(upper, EDGE, 0), EDGE)
+            edges.append((d, q, jnp.where(live, block, count), pl.multiple_of(jnp.where(upper, 0, inside), EDGE)))
+            here = out.at[d, q, pl.ds(at, inside), :]
+            sends.append(pltpu.make_async_copy(blocks_ref.at[block, pl.ds(at, inside), :], here, sems.at[0, d, q]))
+
+            @pl.when(live)
+            def _(send=sends[-1]):
+                send.start()
+
+            @pl.when(jnp.logical_not(live))
+            def _(here=here, d=d, q=q):
+                pltpu.make_async_copy(zero_ref.at[pl.ds(0, inside), :], here, sems.at[0, d, q]).start()
+
     e = lax.broadcasted_iota(jnp.int32, (2 * EDGE, 2 * EDGE), 0)
     k = lax.broadcasted_iota(jnp.int32, (2 * EDGE, 2 * EDGE), 1)
     upper = (e < EDGE) & (k < EDGE)
     lower = (e >= EDGE) & (k >= EDGE)
     which = jnp.where(upper, k - (EDGE - 2) - e, k + (EDGE + 2) - e)
-    rim = jnp.concatenate([low_ref[...], high_ref[...]], 0)
+    odd = lax.rem(lax.axis_index("tile"), 2) == 1
+    inner, outer = inner_ref[...], outer_ref[...]
+    rim = jnp.concatenate([jnp.where(odd, inner, outer), jnp.where(odd, outer, inner)], 0)
     rims = jnp.concatenate([shifted(rim, b - 2) for b in range(5)], 0)
     both = dot(banded(taps_ref, which, upper | lower), rims)
     corrected = edge_ref[...] + (both[: 2 * EDGE] + both[2 * EDGE :])
     top = (corrected[:EDGE] * weight_ref[0, :EDGE].astype(F32)).astype(BF16)
     bottom = (corrected[EDGE:] * weight_ref[0, rows - EDGE :].astype(F32)).astype(BF16)
     for c in range(across):
-        fixed_ref[c, :EDGE] = top[:, c * B : c * B + B]
-        fixed_ref[count - across + c, B - EDGE :] = bottom[:, c * B : c * B + B]
-    sends = []
-    for d in range(out.shape[0]):
-        for q in range(out.shape[1]):
-            at = jnp.where(q < count_ref[0, 0, d], src_ref[0, 0, d, q], count)
-            sends.append(pltpu.make_async_copy(fixed_ref.at[at], out.at[d, q], out_sems.at[d, q]))
-            sends[-1].start()
+        fixed_ref[c] = top[:, c * B : c * B + B]
+        fixed_ref[count - across + c] = bottom[:, c * B : c * B + B]
+    for d, q, which, at in edges:
+        sends.append(pltpu.make_async_copy(fixed_ref.at[which], out.at[d, q, pl.ds(at, EDGE), :], sems.at[1, d, q]))
+        sends[-1].start()
     for send in sends:
         send.wait()
 
@@ -145,9 +164,7 @@
 
 
 def rest_kernel(a_ref, rest_ref, b_ref, first_ref):
-    count = rest_ref.shape[0]
-    b_ref[:count] = rest_ref[...].astype(BF16)
-    b_ref[count] = jnp.zeros((B, B), BF16)
+    b_ref[...] = rest_ref[...].astype(BF16)
     first_ref[0] = a_ref[0]
 
 
@@ -172,8 +189,8 @@
     spectra_out([a_ref[m] for m in range(EARLY)], *refs)
 
 
-def late_kernel(a_ref, b_ref, *refs):
-    spectra_out([a_ref[EARLY - 1]] + [b_ref[m] for m in range(b_ref.shape[0])], *refs)
+def late_kernel(a_ref, b_ref, rim_ref, *refs):
+    spectra_out([a_ref[EARLY - 1]] + [b_ref[m] for m in range(b_ref.shape[0])] + [rim_ref[0]], *refs)
 
 
 def correlate_chunk(cur_ref, blocks, tables, out, at, cross_ref, mag_ref, result_ref, sems):
@@ -238,13 +255,12 @@
     correlate_chunk(cur_ref, blocks, refs[:5], refs[5], 0, *refs[6:])
 
 
-def correlate_late(held, cur_ref, a_ref, b_ref, anchor_ref, border_ref, *refs):
+def correlate_late(held, cur_ref, a_ref, b_ref, rim_ref, anchor_ref, border_ref, *refs):
     del held
     is_first = lax.axis_index("sec") == 0
-    rest = b_ref.shape[0] - 1
     blocks = [jnp.where(is_first, anchor_ref[EARLY - 1], a_ref[EARLY - 1])]
-    blocks += [jnp.where(is_first, anchor_ref[EARLY + m], b_ref[m]) for m in range(rest)]
-    blocks += [jnp.where(is_first, border_ref[0], b_ref[rest])]
+    blocks += [jnp.where(is_first, anchor_ref[EARLY + m], b_ref[m]) for m in range(b_ref.shape[0])]
+    blocks += [jnp.where(is_first, border_ref[0], rim_ref[0])]
     correlate_chunk(cur_ref, blocks, refs[:5], refs[5], EARLY - 1, *refs[6:])
 
 
@@ -277,9 +293,8 @@
     count = anchor.shape[0]
     shape = jax.ShapeDtypeStruct
     whole = lambda *dims: pl.BlockSpec(dims, lambda i: (0,) * len(dims))
-    forth = [(i, i + 1) for i in range(strips - 1)]
     back = [(i + 1, i) for i in range(strips - 1)]
-    last, head = call(
+    inner, outer = call(
         prepare_kernel,
         (shape((EDGE, cols), BF16), shape((EDGE, cols), BF16)),
         [HBM],
@@ -290,8 +305,8 @@
         (image,),
         limit=PREPARE_VMEM_LIMIT,
     )
-    low = lax.ppermute(last, "tile", forth)
-    high = lax.ppermute(head, "tile", back)
+    inner = lax.ppermute(inner, "tile", [(t, t ^ 1) for t in range(strips)])
+    outer = lax.ppermute(outer, "tile", [(t, t + 2 * (t % 2) - 1) for t in range(1, strips - 1)])
     tile_blocks = rows // B * (cols // B)
     blocks, edge = call(
         lens_kernel,
@@ -308,10 +323,14 @@
         (shape((strips, slots, B, B), BF16), shape((1, B, B), BF16)),
         [SMEM] * 3 + [VMEM] * 6,
         (HBM, VMEM),
-        [pltpu.VMEM((tile_blocks + 1, B, B), BF16), pltpu.SemaphoreType.DMA((strips, slots))],
+        [
+            pltpu.VMEM((B, B), BF16),
+            pltpu.VMEM((tile_blocks + 1, EDGE, B), BF16),
+            pltpu.SemaphoreType.DMA((2, strips, slots)),
+        ],
         2**20,
         4 * 2 * rows * cols,
-        (lens_filter_taps, block_src, valid_count, low, high, edge, weight, blocks, anchor),
+        (lens_filter_taps, block_src, valid_count, inner, outer, edge, weight, blocks, anchor),
     )
     incoming = lax.all_to_all(outgoing, "tile", split_axis=0, concat_axis=0, tiled=True)
     border = lax.ppermute(anchor_first, "tile", back)
@@ -328,7 +347,7 @@
     )
     part_b, first = call(
         rest_kernel,
-        (shape((count - EARLY + 1, B, B), BF16), shape((1, B, B), BF16)),
+        (shape((count - EARLY, B, B), BF16), shape((1, B, B), BF16)),
         [VMEM] * 2,
         (VMEM, VMEM),
         [],
@@ -338,9 +357,10 @@
     )
     on = [(i, i + 1) for i in range(sections - 1)]
     prior_a = lax.ppermute(part_a, "sec", on)
+    prior_b = lax.ppermute(part_b, "sec", on)
     own_rim = lax.ppermute(first, "tile", back)
-    part_b = lax.dynamic_update_slice(part_b, own_rim, (count - EARLY, 0, 0))
-    prior_b = lax.ppermute(part_b, "sec", on)
+    across = [(s * strips + d + 1, (s + 1) * strips + d) for s in range(sections - 1) for d in range(strips - 1)]
+    prior_rim = lax.ppermute(first, ("sec", "tile"), across)
     right, left, middle, back_left, back_right = (jnp.asarray(t) for t in tables())
     early, late = EARLY - 1, count - EARLY + 1
     current = lambda kernel, pairs, *parts: call(
@@ -354,7 +374,7 @@
         (*parts, right, left, middle),
     )
     spectra_a = current(early_kernel, early, part_a)
-    spectra_b = current(late_kernel, late, part_a, part_b)
+    spectra_b = current(late_kernel, late, part_a, part_b, own_rim)
     result = shape((1, 2 * count, B, B), F32)
     scratch = lambda pairs: [
         pltpu.VMEM((pairs + 1, 2 * B, B), F32),
@@ -375,12 +395,12 @@
     return call(
         correlate_late,
         result,
-        [HBM] + [VMEM] * 10,
+        [HBM] + [VMEM] * 11,
         HBM,
         scratch(late),
         2**30,
         2**22,
-        (held, spectra_b, prior_a, prior_b, anchor, border, right, left, middle, back_left, back_right),
+        (held, spectra_b, prior_a, prior_b, prior_rim, anchor, border, right, left, middle, back_left, back_right),
         aliases={0: 0},
     )
 

time: 62.1 us -> 61.1 us (0.984)
  waiting for transfers between devices: 20.2 us -> 16.7 us
  starting transfers between devices: 28 us -> 30.3 us
    ppermute x2 -> x3, starting transfers between devices: 7.8 us -> 10.3 us  [the longest x1 5.08 us: body(): lax.ppermute(outer, 'tile', [(t, t + 2 * (t % 2) - 1) for t in range(1, s...]
    ppermute x1, waiting for transfers between devices: 1.58 us -> 0.01 us  [body(): own_rim = lax.ppermute(first, 'tile', back)]
    ppermute x1, waiting for transfers between devices: 6.49 us -> 5.42 us  [body(): prior_a = lax.ppermute(part_a, 'sec', on)]
    ppermute x1, waiting for transfers between devices: 1.46 us -> 0.62 us  [body(): prior_b = lax.ppermute(part_b, 'sec', on)]
  transfers between devices with their start and end apart: 7 -> 8, of which waited for: 5 -> 4; matrix products, arithmetic and copies ran while one was open for 0% -> 0% of each run, Pallas kernels for 11% -> 11%
where the time goes in v5:
time: 61.1 us; the launch traced here: 60.5 us
  starting transfers between devices  30.3 us (50%)
  waiting for transfers between devices  16.7 us (27%)
  Pallas kernels  12.9 us (21%)
    pallas_call x9, Pallas kernels, call(): pl.pallas_call(kernel, out_shape=out_shape, in_specs=in_specs, out_specs=...  12.9 us
    ppermute x1, waiting for transfers between devices, body(): border = lax.ppermute(anchor_first, 'tile', back)  8.11 us
    ppermute x1, waiting for transfers between devices, body(): prior_a = lax.ppermute(part_a, 'sec', on)  5.42 us
    ppermute x1, starting transfers between devices, body(): lax.ppermute(outer, 'tile', [(t, t + 2 * (t % 2) - 1) for t in range(1, s...  5.08 us
    all_to_all x1, starting transfers between devices, body(): lax.all_to_all(outgoing, 'tile', split_axis=0, concat_axis=0, tiled=True)  5.02 us
    ppermute x1, starting transfers between devices, body(): border = lax.ppermute(anchor_first, 'tile', back)  4.32 us
    ppermute x1, starting transfers between devices, body(): prior_a = lax.ppermute(part_a, 'sec', on)  3.96 us
    ppermute x1, starting transfers between devices, body(): prior_b = lax.ppermute(part_b, 'sec', on)  3.82 us
  transfers between devices with their start and end apart: 8, of which 4 were waited for; matrix products, arithmetic and copies ran while one was open for 0% of the time, Pallas kernels for 11%

profile of v5, /device:TPU:24, one launch (start us, length us, event | category | flops | bytes accessed | tf_op | source)
XLA Modules:
  0.0 60.5 jit_solution(1298507993402526892)
XLA Ops:
  0.0 0.0 copy-start.9
  0.0 0.0 copy-start.7
  0.0 0.0 copy-start.4
  0.0 0.9 %shard_map.118 = (bf16[16,1024]{1,0:T(8,128)(2,1)S(1)}, bf16[16,1024]{1,0:T(8,128)(2,1)S(1)}) custom-call(bf16[1,256,1024]{2,1,0:T(8,128)(2,1)} %image_ref.1), custom_call_target="tpu_custom_call" | custom-call | flops 8589934592 | bytes 131072 | tf_op jit(solution)/shard_map/pallas_call | solution.py:275
  0.9 1.9 %collective-permute-start = (bf16[16,1024]{1,0:T(8,128)(2,1)S(1)}, bf16[16,1024]{1,0:T(8,128)(2,1)S(1)}, u32[]{:S(2)}, u32[]{:S(2)}) collective-permute-start(bf16[16,1024]{1,0:T(8,128)(2,1)S(1)} %get-tuple-element.17), channel_id=1, source_target_pairs={{0,1},{1,0},{2,3},{3,2},{4,5},{5,4},{6,7},{7,6},{8,9},{9,8},{10,11... | collective-permute-start | bytes 98312 | tf_op jit(solution)/shard_map/ppermute | solution.py:308
  2.8 0.0 copy-start.10
  2.8 0.0 copy-start.1
  2.9 0.0 copy-start.8
  2.9 5.1 %collective-permute-start.1 = (bf16[16,1024]{1,0:T(8,128)(2,1)S(1)}, bf16[16,1024]{1,0:T(8,128)(2,1)S(1)}, u32[]{:S(2)}, u32[]{:S(2)}) collective-permute-start(bf16[16,1024]{1,0:T(8,128)(2,1)S(1)} %get-tuple-element.18), channel_id=1, source_target_pairs={{1,2},{2,1},{3,4},{4,3},{5,6},{6,5},{7,8},{8,7},{9,10},{10,9},{11,... | collective-permute-start | bytes 98312 | tf_op jit(solution)/shard_map/ppermute | solution.py:309
  8.0 0.0 copy-done.9
  8.0 0.0 copy-done.7
  8.0 0.0 copy-done.4
  8.0 2.2 %shard_map.119 = (bf16[16,128,128]{2,1,0:T(8,128)(2,1)S(1)}, f32[32,1024]{1,0:T(8,128)S(1)}) custom-call(f32[1,1,25]{2,1,0:T(1,128)S(1)} %copy-done.7, bf16[1,256,1024]{2,1,0:T(8,128)(2,1)S(1)} %copy-done.9, bf16[1,256,1024]{2,1,0:T(8,128)(2,1)S(1)} %copy-done.4), custom_call_target="tpu_custom_call" | custom-call | flops 1342177280 | bytes 1572864 | tf_op jit(solution)/shard_map/pallas_call | solution.py:275
  10.2 0.0 copy-done.10
  10.2 0.0 copy-start.11
  10.3 0.1 copy.14.src_ref
  10.3 0.0 collective-permute-done.inner_ref
  10.3 0.0 collective-permute-done.1.outer_ref
  10.3 0.0 copy-done.1
  10.4 0.0 copy-done.8
  10.4 2.4 %shard_map.120 = (bf16[16,2,128,128]{3,2,1,0:T(8,128)(2,1)}, bf16[1,128,128]{2,1,0:T(8,128)(2,1)S(1)}) custom-call(f32[1,1,25]{2,1,0:T(1,128)S(1)} %copy-done.7, s32[1,1,16,2]{3,2,1,0:T(8,128)S(1)} %copy.14.src_ref, s32[1,1,16]{2,1,0:T(1,128)S(1)} %copy-done.8, bf16[16,1024]{1,0:T(8,128)(2,1)S(1)} %collective-permute-done.inner_ref, ...), custom_call_target="tpu_custom_call" | custom-call | flops 1048576 | bytes 2097152 | tf_op jit(solution)/shard_map/pallas_call | solution.py:275
  12.7 0.0 copy-start
  12.7 0.0 copy-start.2
  12.7 0.0 copy-start.3
  12.8 5.0 %all-to-all-start = ((bf16[16,2,128,128]{3,2,1,0:T(8,128)(2,1)}), bf16[16,2,128,128]{3,2,1,0:T(8,128)(2,1)S(1)}, u32[]{:S(2)}, u32[]{:S(2)}) async-start(bf16[16,2,128,128]{3,2,1,0:T(8,128)(2,1)} %get-tuple-element.21), calls=%async_computation | async-start | bytes 2097152 | tf_op jit(solution)/shard_map/all_to_all | solution.py:335
  17.8 4.3 %collective-permute-start.2 = (bf16[1,128,128]{2,1,0:T(8,128)(2,1)S(1)}, bf16[1,128,128]{2,1,0:T(8,128)(2,1)S(1)}, u32[]{:S(2)}, u32[]{:S(2)}) collective-permute-start(bf16[1,128,128]{2,1,0:T(8,128)(2,1)S(1)} %get-tuple-element.22), channel_id=1, source_target_pairs={{1,0},{2,1},{3,2},{4,3},{5,4},{6,5},{7,6},{8,7},{9,8},{10,9},{11,1... | collective-permute-start | bytes 98312 | tf_op jit(solution)/shard_map/ppermute | solution.py:336
  22.1 0.0 copy-done.11
  22.1 0.1 copy.15.dst_ref
  22.2 8.1 %collective-permute-done.2.border_ref = bf16[1,128,128]{2,1,0:T(8,128)(2,1)S(1)} collective-permute-done((bf16[1,128,128]{2,1,0:T(8,128)(2,1)S(1)}, bf16[1,128,128]{2,1,0:T(8,128)(2,1)S(1)}, u32[]{:S(2)}, u32[]{:S(2)}) %collective-permute-start.2) | collective-permute-done | bytes 32800 | tf_op jit(solution)/shard_map/ppermute | solution.py:336
  30.3 2.6 %all-to-all-done.in_ref = bf16[16,2,128,128]{3,2,1,0:T(8,128)(2,1)S(1)} async-done(((bf16[16,2,128,128]{3,2,1,0:T(8,128)(2,1)}), bf16[16,2,128,128]{3,2,1,0:T(8,128)(2,1)S(1)}, u32[]{:S(2)}, u32[]{:S(2)}) %all-to-all-start) | async-done | bytes 1048608 | tf_op jit(solution)/shard_map/all_to_all | solution.py:335
  32.9 1.0 %shard_map.121 = (bf16[11,128,128]{2,1,0:T(8,128)(2,1)S(1)}, f32[5,128,128]{2,1,0:T(8,128)S(1)}) custom-call(s32[1,16,1,2]{3,2,1,0:T(1,128)S(1)} %copy.15.dst_ref, bf16[16,2,128,128]{3,2,1,0:T(8,128)(2,1)S(1)} %all-to-all-done.in_ref), custom_call_target="tpu_custom_call" | custom-call | flops 1048576 | bytes 2097152 | tf_op jit(solution)/shard_map/pallas_call | solution.py:275
  33.9 0.0 copy-start.5
  33.9 0.0 copy-start.6
  33.9 4.0 %collective-permute-start.3 = (bf16[11,128,128]{2,1,0:T(8,128)(2,1)S(1)}, bf16[11,128,128]{2,1,0:T(8,128)(2,1)S(1)}, u32[]{:S(2)}, u32[]{:S(2)}) collective-permute-start(bf16[11,128,128]{2,1,0:T(8,128)(2,1)S(1)} %get-tuple-element.24.a_ref), channel_id=1, source_target_pairs={{0,16},{16,32},{32,48},{48,64},{64,80},{80,96},{96,112},{112,128},... | collective-permute-start | bytes 1081352 | tf_op jit(solution)/shard_map/ppermute | solution.py:359
  37.9 3.8 %collective-permute-start.5 = (bf16[5,128,128]{2,1,0:T(8,128)(2,1)S(1)}, bf16[5,128,128]{2,1,0:T(8,128)(2,1)S(1)}, u32[]{:S(2)}, u32[]{:S(2)}) collective-permute-start(bf16[5,128,128]{2,1,0:T(8,128)(2,1)S(1)} %get-tuple-element.26.b_ref), channel_id=1, source_target_pairs={{0,16},{16,32},{32,48},{48,64},{64,80},{80,96},{96,112},{112,128},... | collective-permute-start | bytes 491528 | tf_op jit(solution)/shard_map/ppermute | solution.py:360
  41.8 2.8 %collective-permute-start.4 = (bf16[1,128,128]{2,1,0:T(8,128)(2,1)S(1)}, bf16[1,128,128]{2,1,0:T(8,128)(2,1)S(1)}, u32[]{:S(2)}, u32[]{:S(2)}) collective-permute-start(bf16[1,128,128]{2,1,0:T(8,128)(2,1)S(1)} %get-tuple-element.27), channel_id=1, source_target_pairs={{1,0},{2,1},{3,2},{4,3},{5,4},{6,5},{7,6},{8,7},{9,8},{10,9},{11,1... | collective-permute-start | bytes 98312 | tf_op jit(solution)/shard_map/ppermute | solution.py:361
  44.6 3.3 %collective-permute-start.6 = (bf16[1,128,128]{2,1,0:T(8,128)(2,1)S(1)}, bf16[1,128,128]{2,1,0:T(8,128)(2,1)S(1)}, u32[]{:S(2)}, u32[]{:S(2)}) collective-permute-start(bf16[1,128,128]{2,1,0:T(8,128)(2,1)S(1)} %get-tuple-element.27), channel_id=1, source_target_pairs={{1,16},{2,17},{3,18},{4,19},{5,20},{6,21},{7,22},{8,23},{9,24},{10... | collective-permute-start | bytes 98312 | tf_op jit(solution)/shard_map/ppermute | solution.py:363
  47.9 0.0 copy-done
  47.9 0.0 copy-done.2
  47.9 0.0 copy-done.3
  48.0 0.9 %shard_map.122.cur_ref = bf16[256,1408]{1,0:T(8,128)(2,1)S(1)} custom-call(bf16[11,128,128]{2,1,0:T(8,128)(2,1)S(1)} %get-tuple-element.24.a_ref, bf16[256,256]{1,0:T(8,128)(2,1)S(1)} %copy-done.3, bf16[256,256]{1,0:T(8,128)(2,1)S(1)} %copy-done.2, bf16[1408,128]{1,0:T(8,128)(2,1)S(1)} %copy-done), custom_call_target="tpu_custom_call" | custom-call | flops 1024 | bytes 1024 | tf_op jit(solution)/shard_map/pallas_call | solution.py:275
  48.9 0.0 collective-permute-done.4.rim_ref
  48.9 0.8 %shard_map.125.cur_ref = bf16[256,896]{1,0:T(8,128)(2,1)S(1)} custom-call(bf16[11,128,128]{2,1,0:T(8,128)(2,1)S(1)} %get-tuple-element.24.a_ref, bf16[5,128,128]{2,1,0:T(8,128)(2,1)S(1)} %get-tuple-element.26.b_ref, bf16[1,128,128]{2,1,0:T(8,128)(2,1)S(1)} %collective-permute-done.4.rim_ref, bf16[256,256]{1,0:T(8,128)(2,1)S(1)} %copy-done.3, ...), custom_call_target="tpu_custom_call" | custom-call | flops 1024 | bytes 1024 | tf_op jit(solution)/shard_map/pallas_call | solution.py:275
  49.7 5.4 %collective-permute-done.3.a_ref = bf16[11,128,128]{2,1,0:T(8,128)(2,1)S(1)} collective-permute-done((bf16[11,128,128]{2,1,0:T(8,128)(2,1)S(1)}, bf16[11,128,128]{2,1,0:T(8,128)(2,1)S(1)}, u32[]{:S(2)}, u32[]{:S(2)}) %collective-permute-start.3) | collective-permute-done | bytes 360480 | tf_op jit(solution)/shard_map/ppermute | solution.py:359
  55.1 0.0 copy-done.5
  55.1 0.0 copy-done.6
  55.1 2.6 %shard_map.123.held = f32[1,32,128,128]{3,2,1,0:T(8,128)} custom-call(bf16[256,1408]{1,0:T(8,128)(2,1)S(1)} %shard_map.122.cur_ref, bf16[11,128,128]{2,1,0:T(8,128)(2,1)S(1)} %collective-permute-done.3.a_ref, bf16[16,128,128]{2,1,0:T(8,128)(2,1)S(1)} %copy-done.1, bf16[256,256]{1,0:T(8,128)(2,1)S(1)} %copy-done.3, bf16[256,256]{1,0:T(8,128)(2,1)S(1)} %copy-done.2, ...), custom_call_target="tpu_custom_call" | custom-call | flops 1024 | bytes 1024 | tf_op jit(solution)/shard_map/pallas_call | solution.py:275
  57.7 0.0 collective-permute-done.6.rim_ref
  57.7 0.6 %collective-permute-done.5.b_ref = bf16[5,128,128]{2,1,0:T(8,128)(2,1)S(1)} collective-permute-done((bf16[5,128,128]{2,1,0:T(8,128)(2,1)S(1)}, bf16[5,128,128]{2,1,0:T(8,128)(2,1)S(1)}, u32[]{:S(2)}, u32[]{:S(2)}) %collective-permute-start.5) | collective-permute-done | bytes 163872 | tf_op jit(solution)/shard_map/ppermute | solution.py:360
  58.3 2.2 %shard_map.126 = f32[1,32,128,128]{3,2,1,0:T(8,128)} custom-call(f32[1,32,128,128]{3,2,1,0:T(8,128)} %shard_map.123.held, bf16[256,896]{1,0:T(8,128)(2,1)S(1)} %shard_map.125.cur_ref, bf16[11,128,128]{2,1,0:T(8,128)(2,1)S(1)} %collective-permute-done.3.a_ref, bf16[5,128,128]{2,1,0:T(8,128)(2,1)S(1)} %collective-permute-done.5.b_ref, ...), custom_call_target="tpu_custom_call", output_to_operand_aliasing={{}: (0, {})} | custom-call | flops 1073741824 | bytes 4194304 | tf_op jit(solution)/shard_map/pallas_call | solution.py:275
  (1 shorter events, 0.0 us)
Async XLA Ops:
  0.0 8.0 %copy-start.9 = (bf16[1,256,1024]{2,1,0:T(8,128)(2,1)S(1)}, bf16[1,256,1024]{2,1,0:T(8,128)(2,1)}, u32[]{:S(2)}) copy-start(bf16[1,256,1024]{2,1,0:T(8,128)(2,1)} %image_ref.1) | copy-start | bytes 1572868
  0.0 8.0 %copy-start.7 = (f32[1,1,25]{2,1,0:T(1,128)S(1)}, f32[1,1,25]{2,1,0:T(1,128)}, u32[]{:S(2)}) copy-start(f32[1,1,25]{2,1,0:T(1,128)} %taps_ref.3) | copy-start | bytes 304
  0.0 8.0 %copy-start.4 = (bf16[1,256,1024]{2,1,0:T(8,128)(2,1)S(1)}, bf16[1,256,1024]{2,1,0:T(8,128)(2,1)}, u32[]{:S(2)}) copy-start(bf16[1,256,1024]{2,1,0:T(8,128)(2,1)} %weight_ref.3) | copy-start | bytes 1572868
  0.9 9.4 %collective-permute-start = (bf16[16,1024]{1,0:T(8,128)(2,1)S(1)}, bf16[16,1024]{1,0:T(8,128)(2,1)S(1)}, u32[]{:S(2)}, u32[]{:S(2)}) collective-permute-start(bf16[16,1024]{1,0:T(8,128)(2,1)S(1)} %get-tuple-element.17), channel_id=1, source_target_pairs={{0,1},{1,0},{2,3},{3,2},{4,5},{5,4},{6,7},{7,6},{8,9},{9,8},{10,11... | collective-permute-start | bytes 98312 | tf_op jit(solution)/shard_map/ppermute | solution.py:308
  2.8 7.4 %copy-start.10 = (s32[1,1,16,2]{2,3,1,0:T(2,128)S(1)}, s32[1,1,16,2]{2,3,1,0:T(2,128)}, u32[]{:S(2)}) copy-start(s32[1,1,16,2]{2,3,1,0:T(2,128)} %param.15) | copy-start | bytes 388
  2.8 7.5 %copy-start.1 = (bf16[16,128,128]{2,1,0:T(8,128)(2,1)S(1)}, bf16[16,128,128]{2,1,0:T(8,128)(2,1)}, u32[]{:S(2)}) copy-start(bf16[16,128,128]{2,1,0:T(8,128)(2,1)} %anchor_ref.5) | copy-start | bytes 1572868
  2.9 7.5 %copy-start.8 = (s32[1,1,16]{2,1,0:T(1,128)S(1)}, s32[1,1,16]{2,1,0:T(1,128)}, u32[]{:S(2)}) copy-start(s32[1,1,16]{2,1,0:T(1,128)} %count_ref.1) | copy-start | bytes 196
  2.9 7.5 %collective-permute-start.1 = (bf16[16,1024]{1,0:T(8,128)(2,1)S(1)}, bf16[16,1024]{1,0:T(8,128)(2,1)S(1)}, u32[]{:S(2)}, u32[]{:S(2)}) collective-permute-start(bf16[16,1024]{1,0:T(8,128)(2,1)S(1)} %get-tuple-element.18), channel_id=1, source_target_pairs={{1,2},{2,1},{3,4},{4,3},{5,6},{6,5},{7,8},{8,7},{9,10},{10,9},{11,... | collective-permute-start | bytes 98312 | tf_op jit(solution)/shard_map/ppermute | solution.py:309
  10.2 11.9 %copy-start.11 = (s32[1,16,1,2]{1,3,2,0:T(2,128)S(1)}, s32[1,16,1,2]{1,3,2,0:T(2,128)}, u32[]{:S(2)}) copy-start(s32[1,16,1,2]{1,3,2,0:T(2,128)} %param.16) | copy-start | bytes 388
  12.7 35.2 %copy-start = (bf16[1408,128]{1,0:T(8,128)(2,1)S(1)}, bf16[1408,128]{1,0:T(8,128)(2,1)}, u32[]{:S(2)}) copy-start(bf16[1408,128]{1,0:T(8,128)(2,1)} %constant.12.clone.refs_2_) | copy-start | bytes 1081348
  12.7 35.2 %copy-start.2 = (bf16[256,256]{1,0:T(8,128)(2,1)S(1)}, bf16[256,256]{1,0:T(8,128)(2,1)}, u32[]{:S(2)}) copy-start(bf16[256,256]{1,0:T(8,128)(2,1)} %constant.11.clone.refs_1_) | copy-start | bytes 393220
  12.7 35.2 %copy-start.3 = (bf16[256,256]{1,0:T(8,128)(2,1)S(1)}, bf16[256,256]{1,0:T(8,128)(2,1)}, u32[]{:S(2)}) copy-start(bf16[256,256]{1,0:T(8,128)(2,1)} %constant.10.clone.refs_0_) | copy-start | bytes 393220
  12.8 20.1 %all-to-all-start = ((bf16[16,2,128,128]{3,2,1,0:T(8,128)(2,1)}), bf16[16,2,128,128]{3,2,1,0:T(8,128)(2,1)S(1)}, u32[]{:S(2)}, u32[]{:S(2)}) async-start(bf16[16,2,128,128]{3,2,1,0:T(8,128)(2,1)} %get-tuple-element.21), calls=%async_computation | async-start | bytes 2097152 | tf_op jit(solution)/shard_map/all_to_all | solution.py:335
  17.8 12.5 %collective-permute-start.2 = (bf16[1,128,128]{2,1,0:T(8,128)(2,1)S(1)}, bf16[1,128,128]{2,1,0:T(8,128)(2,1)S(1)}, u32[]{:S(2)}, u32[]{:S(2)}) collective-permute-start(bf16[1,128,128]{2,1,0:T(8,128)(2,1)S(1)} %get-tuple-element.22), channel_id=1, source_target_pairs={{1,0},{2,1},{3,2},{4,3},{5,4},{6,5},{7,6},{8,7},{9,8},{10,9},{11,1... | collective-permute-start | bytes 98312 | tf_op jit(solution)/shard_map/ppermute | solution.py:336
  33.9 21.2 %copy-start.5 = (bf16[256,256]{1,0:T(8,128)(2,1)S(1)}, bf16[256,256]{1,0:T(8,128)(2,1)}, u32[]{:S(2)}) copy-start(bf16[256,256]{1,0:T(8,128)(2,1)} %constant.14.clone.refs_4_) | copy-start | bytes 393220
  33.9 21.2 %copy-start.6 = (bf16[256,256]{1,0:T(8,128)(2,1)S(1)}, bf16[256,256]{1,0:T(8,128)(2,1)}, u32[]{:S(2)}) copy-start(bf16[256,256]{1,0:T(8,128)(2,1)} %constant.13.clone.refs_3_) | copy-start | bytes 393220
  33.9 21.2 %collective-permute-start.3 = (bf16[11,128,128]{2,1,0:T(8,128)(2,1)S(1)}, bf16[11,128,128]{2,1,0:T(8,128)(2,1)S(1)}, u32[]{:S(2)}, u32[]{:S(2)}) collective-permute-start(bf16[11,128,128]{2,1,0:T(8,128)(2,1)S(1)} %get-tuple-element.24.a_ref), channel_id=1, source_target_pairs={{0,16},{16,32},{32,48},{48,64},{64,80},{80,96},{96,112},{112,128},... | collective-permute-start | bytes 1081352 | tf_op jit(solution)/shard_map/ppermute | solution.py:359
  37.9 20.4 %collective-permute-start.5 = (bf16[5,128,128]{2,1,0:T(8,128)(2,1)S(1)}, bf16[5,128,128]{2,1,0:T(8,128)(2,1)S(1)}, u32[]{:S(2)}, u32[]{:S(2)}) collective-permute-start(bf16[5,128,128]{2,1,0:T(8,128)(2,1)S(1)} %get-tuple-element.26.b_ref), channel_id=1, source_target_pairs={{0,16},{16,32},{32,48},{48,64},{64,80},{80,96},{96,112},{112,128},... | collective-permute-start | bytes 491528 | tf_op jit(solution)/shard_map/ppermute | solution.py:360
  41.8 7.1 %collective-permute-start.4 = (bf16[1,128,128]{2,1,0:T(8,128)(2,1)S(1)}, bf16[1,128,128]{2,1,0:T(8,128)(2,1)S(1)}, u32[]{:S(2)}, u32[]{:S(2)}) collective-permute-start(bf16[1,128,128]{2,1,0:T(8,128)(2,1)S(1)} %get-tuple-element.27), channel_id=1, source_target_pairs={{1,0},{2,1},{3,2},{4,3},{5,4},{6,5},{7,6},{8,7},{9,8},{10,9},{11,1... | collective-permute-start | bytes 98312 | tf_op jit(solution)/shard_map/ppermute | solution.py:361
  44.6 13.1 %collective-permute-start.6 = (bf16[1,128,128]{2,1,0:T(8,128)(2,1)S(1)}, bf16[1,128,128]{2,1,0:T(8,128)(2,1)S(1)}, u32[]{:S(2)}, u32[]{:S(2)}) collective-permute-start(bf16[1,128,128]{2,1,0:T(8,128)(2,1)S(1)} %get-tuple-element.27), channel_id=1, source_target_pairs={{1,16},{2,17},{3,18},{4,19},{5,20},{6,21},{7,22},{8,23},{9,24},{10... | collective-permute-start | bytes 98312 | tf_op jit(solution)/shard_map/ppermute | solution.py:363

commit v6 on v5

--- a/solution.py
+++ b/solution.py
@@ -76,23 +76,47 @@
     last = image.shape[1] - EDGE
     odd = lax.rem(lax.axis_index("tile"), 2)
     to_inner = pltpu.make_async_copy(image.at[0, pl.ds(pl.multiple_of((1 - odd) * last, EDGE), EDGE)], inner, sems.at[0])
-    to_outer = pltpu.make_async_copy(image.at[0, pl.ds(pl.multiple_of(odd * last, EDGE), EDGE)], outer, sems.at[1])
+    wide = outer.shape[0]
+    last = image.shape[1] - wide
+    to_outer = pltpu.make_async_copy(image.at[0, pl.ds(pl.multiple_of(odd * last, EDGE), wide)], outer, sems.at[1])
     to_inner.start()
     to_outer.start()
     to_inner.wait()
     to_outer.wait()
 
 
-def lens_kernel(taps_ref, image_ref, weight_ref, blocks_ref, edge_ref):
+def edge_bands(taps_ref):
+    e = lax.broadcasted_iota(jnp.int32, (2 * EDGE, 2 * EDGE), 0)
+    k = lax.broadcasted_iota(jnp.int32, (2 * EDGE, 2 * EDGE), 1)
+    upper = (e < EDGE) & (k < EDGE)
+    lower = (e >= EDGE) & (k >= EDGE)
+    return banded(taps_ref, jnp.where(upper, k - (EDGE - 2) - e, k + (EDGE + 2) - e), upper | lower)
+
+
+def lens_kernel(taps_ref, image_ref, weight_ref, blocks_ref, edge_ref, bands_ref):
     x = image_ref[0]
     rows, cols = x.shape
     across = cols // B
-    i = lax.broadcasted_iota(jnp.int32, (rows, rows), 0)
-    j = lax.broadcasted_iota(jnp.int32, (rows, rows), 1)
+    i = lax.broadcasted_iota(jnp.int32, (B, B), 0)
+    j = lax.broadcasted_iota(jnp.int32, (B, B), 1)
     bands = banded(taps_ref, j - i + 2, None)
-    stack = jnp.concatenate([shifted(x, b - 2) for b in range(5)], 0)
+    columns = [shifted(x, b - 2) for b in range(5)]
+    stack = jnp.concatenate([jnp.concatenate([c[:B] for c in columns], 0), jnp.concatenate([c[B:] for c in columns], 0)], 1)
     both = dot(bands, stack)
-    corrected = both[:rows] + both[rows:]
+    main = both[:B] + both[B:]
+    edges = edge_bands(taps_ref)
+    bands_ref[...] = edges
+    both = dot(edges, jnp.concatenate([c[B - EDGE : B + EDGE] for c in columns], 0))
+    middle = both[: 2 * EDGE] + both[2 * EDGE :]
+    corrected = jnp.concatenate(
+        [
+            main[: B - EDGE, :cols],
+            main[B - EDGE :, :cols] + middle[EDGE:],
+            main[:EDGE, cols:] + middle[:EDGE],
+            main[EDGE:, cols:],
+        ],
+        0,
+    )
     edge_ref[:EDGE] = corrected[:EDGE]
     edge_ref[EDGE:] = corrected[rows - EDGE :]
     weighted = (corrected * weight_ref[0].astype(F32)).astype(BF16)
@@ -102,55 +126,33 @@
 
 
 def pick_kernel(
-    taps_ref, src_ref, count_ref, inner_ref, outer_ref, edge_ref, weight_ref, blocks_ref, anchor_ref, out, first_ref, zero_ref, fixed_ref, sems
+    bands_ref, src_ref, count_ref, inner_ref, outer_ref, edge_ref, weight_ref, blocks_ref, dst_ref, out, dst_out, fixed_ref
 ):
+    dst_out[...] = dst_ref[...]
     rows, cols = weight_ref.shape[1:]
     across = cols // B
     count = rows // B * across
-    zero_ref[...] = jnp.zeros((B, B), BF16)
-    fixed_ref[count] = jnp.zeros((EDGE, B), BF16)
-    first_ref[0] = anchor_ref[0]
-    inside = B - EDGE
-    sends, edges = [], []
+    places = []
     for d in range(out.shape[0]):
         for q in range(out.shape[1]):
             live = q < count_ref[0, 0, d]
             block = src_ref[0, 0, d, q]
-            upper = block < across
-            at = pl.multiple_of(jnp.where(upper, EDGE, 0), EDGE)
-            edges.append((d, q, jnp.where(live, block, count), pl.multiple_of(jnp.where(upper, 0, inside), EDGE)))
-            here = out.at[d, q, pl.ds(at, inside), :]
-            sends.append(pltpu.make_async_copy(blocks_ref.at[block, pl.ds(at, inside), :], here, sems.at[0, d, q]))
-
-            @pl.when(live)
-            def _(send=sends[-1]):
-                send.start()
-
-            @pl.when(jnp.logical_not(live))
-            def _(here=here, d=d, q=q):
-                pltpu.make_async_copy(zero_ref.at[pl.ds(0, inside), :], here, sems.at[0, d, q]).start()
-
-    e = lax.broadcasted_iota(jnp.int32, (2 * EDGE, 2 * EDGE), 0)
-    k = lax.broadcasted_iota(jnp.int32, (2 * EDGE, 2 * EDGE), 1)
-    upper = (e < EDGE) & (k < EDGE)
-    lower = (e >= EDGE) & (k >= EDGE)
-    which = jnp.where(upper, k - (EDGE - 2) - e, k + (EDGE + 2) - e)
+            out[d, q] = jnp.where(live, blocks_ref[block], jnp.zeros((), BF16))
+            places.append((d, q, live, block))
     odd = lax.rem(lax.axis_index("tile"), 2) == 1
     inner, outer = inner_ref[...], outer_ref[...]
-    rim = jnp.concatenate([jnp.where(odd, inner, outer), jnp.where(odd, outer, inner)], 0)
+    rim = jnp.concatenate([jnp.where(odd, inner, outer[EDGE:]), jnp.where(odd, outer[:EDGE], inner)], 0)
     rims = jnp.concatenate([shifted(rim, b - 2) for b in range(5)], 0)
-    both = dot(banded(taps_ref, which, upper | lower), rims)
+    both = dot(bands_ref[...], rims)
     corrected = edge_ref[...] + (both[: 2 * EDGE] + both[2 * EDGE :])
     top = (corrected[:EDGE] * weight_ref[0, :EDGE].astype(F32)).astype(BF16)
     bottom = (corrected[EDGE:] * weight_ref[0, rows - EDGE :].astype(F32)).astype(BF16)
     for c in range(across):
         fixed_ref[c] = top[:, c * B : c * B + B]
         fixed_ref[count - across + c] = bottom[:, c * B : c * B + B]
-    for d, q, which, at in edges:
-        sends.append(pltpu.make_async_copy(fixed_ref.at[which], out.at[d, q, pl.ds(at, EDGE), :], sems.at[1, d, q]))
-        sends[-1].start()
-    for send in sends:
-        send.wait()
+    for d, q, live, block in places:
+        at = pl.multiple_of(jnp.where(block < across, 0, B - EDGE), EDGE)
+        out[d, q, pl.ds(at, EDGE), :] = jnp.where(live, fixed_ref[block], jnp.zeros((), BF16))
 
 
 def strip_kernel(dst_ref, in_ref, a_ref, rest_ref, acc_ref):
@@ -163,9 +165,10 @@
     rest_ref[...] = acc_ref[EARLY:]
 
 
-def rest_kernel(a_ref, rest_ref, b_ref, first_ref):
+def rest_kernel(a_ref, rest_ref, anchor_ref, b_ref, first_ref, anchor_first_ref):
     b_ref[...] = rest_ref[...].astype(BF16)
     first_ref[0] = a_ref[0]
+    anchor_first_ref[0] = anchor_ref[0]
 
 
 def forward(blocks, right, left, middle):
@@ -296,7 +299,7 @@
     back = [(i + 1, i) for i in range(strips - 1)]
     inner, outer = call(
         prepare_kernel,
-        (shape((EDGE, cols), BF16), shape((EDGE, cols), BF16)),
+        (shape((EDGE, cols), BF16), shape((2 * EDGE, cols), BF16)),
         [HBM],
         (VMEM,) * 2,
         [pltpu.SemaphoreType.DMA((2,))],
@@ -305,36 +308,30 @@
         (image,),
         limit=PREPARE_VMEM_LIMIT,
     )
+    outer = lax.ppermute(outer, "tile", [(t, t + 2 * (t % 2) - 1) for t in range(1, strips - 1)])
     inner = lax.ppermute(inner, "tile", [(t, t ^ 1) for t in range(strips)])
-    outer = lax.ppermute(outer, "tile", [(t, t + 2 * (t % 2) - 1) for t in range(1, strips - 1)])
     tile_blocks = rows // B * (cols // B)
-    blocks, edge = call(
+    blocks, edge, bands = call(
         lens_kernel,
-        (shape((tile_blocks, B, B), BF16), shape((2 * EDGE, cols), F32)),
+        (shape((tile_blocks, B, B), BF16), shape((2 * EDGE, cols), F32), shape((4 * EDGE, 10 * EDGE), BF16)),
         [SMEM, VMEM, VMEM],
+        (VMEM, VMEM, VMEM),
+        [],
+        2**10,
+        2**10,
+        (lens_filter_taps, image, weight),
+    )
+    outgoing, places = call(
+        pick_kernel,
+        (shape((strips, slots, B, B), BF16), shape((1, strips, 1, slots), jnp.int32)),
+        [VMEM, SMEM, SMEM] + [VMEM] * 6,
         (VMEM, VMEM),
-        [],
-        2 * 10 * rows * rows * cols,
-        3 * 2 * rows * cols,
-        (lens_filter_taps, image, weight),
-    )
-    outgoing, anchor_first = call(
-        pick_kernel,
-        (shape((strips, slots, B, B), BF16), shape((1, B, B), BF16)),
-        [SMEM] * 3 + [VMEM] * 6,
-        (HBM, VMEM),
-        [
-            pltpu.VMEM((B, B), BF16),
-            pltpu.VMEM((tile_blocks + 1, EDGE, B), BF16),
-            pltpu.SemaphoreType.DMA((2, strips, slots)),
-        ],
+        [pltpu.VMEM((tile_blocks, EDGE, B), BF16)],
         2**20,
         4 * 2 * rows * cols,
-        (lens_filter_taps, block_src, valid_count, inner, outer, edge, weight, blocks, anchor),
+        (bands, block_src, valid_count, inner, outer, edge, weight, blocks, block_dst),
     )
     incoming = lax.all_to_all(outgoing, "tile", split_axis=0, concat_axis=0, tiled=True)
-    border = lax.ppermute(anchor_first, "tile", back)
-    incoming, border = lax.optimization_barrier((incoming, border))
     part_a, rest = call(
         strip_kernel,
         (shape((EARLY, B, B), BF16), shape((count - EARLY, B, B), F32)),
@@ -343,17 +340,17 @@
         [pltpu.VMEM((count, B, B), F32)],
         2**20,
         4 * 2 * rows * cols,
-        (block_dst, incoming),
-    )
-    part_b, first = call(
+        (places, incoming),
+    )
+    part_b, first, anchor_first = call(
         rest_kernel,
-        (shape((count - EARLY, B, B), BF16), shape((1, B, B), BF16)),
-        [VMEM] * 2,
-        (VMEM, VMEM),
+        (shape((count - EARLY, B, B), BF16), shape((1, B, B), BF16), shape((1, B, B), BF16)),
+        [VMEM] * 3,
+        (VMEM, VMEM, VMEM),
         [],
         2**18,
         6 * EARLY * B * B,
-        (part_a, rest),
+        (part_a, rest, anchor),
     )
     on = [(i, i + 1) for i in range(sections - 1)]
     prior_a = lax.ppermute(part_a, "sec", on)
@@ -361,6 +358,7 @@
     own_rim = lax.ppermute(first, "tile", back)
     across = [(s * strips + d + 1, (s + 1) * strips + d) for s in range(sections - 1) for d in range(strips - 1)]
     prior_rim = lax.ppermute(first, ("sec", "tile"), across)
+    border = lax.ppermute(anchor_first, "tile", back)
     right, left, middle, back_left, back_right = (jnp.asarray(t) for t in tables())
     early, late = EARLY - 1, count - EARLY + 1
     current = lambda kernel, pairs, *parts: call(

time: 61.1 us -> 58.6 us (0.959)
  blocking collectives: 0 us -> 19.7 us
  waiting for transfers between devices: 16.7 us -> 4.26 us
  starting transfers between devices: 30.3 us -> 22.4 us
  Pallas kernels: 12.9 us -> 11.3 us
    all_to_all x0 -> x1, blocking collectives: none -> 19.7 us  [body(): lax.all_to_all(outgoing, 'tile', split_axis=0, concat_axis=0, tiled=True)]
    ppermute x1, waiting for transfers between devices: 8.11 us -> 0.01 us  [body(): border = lax.ppermute(anchor_first, 'tile', back)]
    all_to_all x1 -> x0, starting transfers between devices: 5.02 us -> none  [body(): lax.all_to_all(outgoing, 'tile', split_axis=0, concat_axis=0, tiled=True)]
    all_to_all x1 -> x0, waiting for transfers between devices: 2.57 us -> none  [body(): lax.all_to_all(outgoing, 'tile', split_axis=0, concat_axis=0, tiled=True)]
    ppermute x1, waiting for transfers between devices: 5.42 us -> 3.25 us  [body(): prior_a = lax.ppermute(part_a, 'sec', on)]
    ppermute x1, starting transfers between devices: 4.32 us -> 2.35 us  [body(): border = lax.ppermute(anchor_first, 'tile', back)]
    pallas_call x9, Pallas kernels: 12.9 us -> 11.3 us  [call(): pl.pallas_call(kernel, out_shape=out_shape, in_specs=in_specs, out_specs=...]
    ppermute x1, starting transfers between devices: 5.08 us -> 4.29 us  [body(): lax.ppermute(outer, 'tile', [(t, t + 2 * (t % 2) - 1) for t in range(1, s...]
  transfers between devices with their start and end apart: 8 -> 7, of which waited for: 4 -> 3; matrix products, arithmetic and copies ran while one was open for 0% -> 0% of each run, Pallas kernels for 11% -> 10%
where the time goes in v6:
time: 58.6 us; the launch traced here: 58.2 us
  starting transfers between devices  22.4 us (38%)
  blocking collectives  19.7 us (34%)
  Pallas kernels  11.3 us (19%)
  waiting for transfers between devices  4.26 us (7%)
    all_to_all x1, blocking collectives, body(): lax.all_to_all(outgoing, 'tile', split_axis=0, concat_axis=0, tiled=True)  19.7 us
    pallas_call x9, Pallas kernels, call(): pl.pallas_call(kernel, out_shape=out_shape, in_specs=in_specs, out_specs=...  11.3 us
    ppermute x1, starting transfers between devices, body(): lax.ppermute(outer, 'tile', [(t, t + 2 * (t % 2) - 1) for t in range(1, s...  4.29 us
    ppermute x1, starting transfers between devices, body(): prior_b = lax.ppermute(part_b, 'sec', on)  3.96 us
    ppermute x1, starting transfers between devices, body(): prior_a = lax.ppermute(part_a, 'sec', on)  3.83 us
    ppermute x1, starting transfers between devices, body(): prior_rim = lax.ppermute(first, ('sec', 'tile'), across)  3.27 us
    ppermute x1, waiting for transfers between devices, body(): prior_a = lax.ppermute(part_a, 'sec', on)  3.25 us
    ppermute x1, starting transfers between devices, body(): own_rim = lax.ppermute(first, 'tile', back)  2.78 us
  transfers between devices with their start and end apart: 7, of which 3 were waited for; matrix products, arithmetic and copies ran while one was open for 0% of the time, Pallas kernels for 10%

profile of v6, /device:TPU:24, one launch (start us, length us, event | category | flops | bytes accessed | tf_op | source)
XLA Modules:
  0.0 58.2 jit_solution(9238971190899112806)
XLA Ops:
  0.0 0.0 copy-start.7
  0.0 0.0 copy-start.2
  0.0 0.0 copy-start.9
  0.0 0.0 copy-start.10
  0.0 0.0 copy-start.11
  0.0 0.0 copy-start.8
  0.0 1.0 %shard_map.119 = (bf16[16,1024]{1,0:T(8,128)(2,1)S(1)}, bf16[32,1024]{1,0:T(8,128)(2,1)S(1)}) custom-call(bf16[1,256,1024]{2,1,0:T(8,128)(2,1)} %image.1), custom_call_target="tpu_custom_call" | custom-call | flops 8589934592 | bytes 131072 | tf_op jit(solution)/shard_map/pallas_call | solution.py:278
  1.0 4.3 %collective-permute-start.1 = (bf16[32,1024]{1,0:T(8,128)(2,1)S(1)}, bf16[32,1024]{1,0:T(8,128)(2,1)S(1)}, u32[]{:S(2)}, u32[]{:S(2)}) collective-permute-start(bf16[32,1024]{1,0:T(8,128)(2,1)S(1)} %get-tuple-element.19), channel_id=1, source_target_pairs={{1,2},{2,1},{3,4},{4,3},{5,6},{6,5},{7,8},{8,7},{9,10},{10,9},{11,... | collective-permute-start | bytes 196616 | tf_op jit(solution)/shard_map/ppermute | solution.py:311
  5.3 1.9 %collective-permute-start = (bf16[16,1024]{1,0:T(8,128)(2,1)S(1)}, bf16[16,1024]{1,0:T(8,128)(2,1)S(1)}, u32[]{:S(2)}, u32[]{:S(2)}) collective-permute-start(bf16[16,1024]{1,0:T(8,128)(2,1)S(1)} %get-tuple-element.18), channel_id=1, source_target_pairs={{0,1},{1,0},{2,3},{3,2},{4,5},{5,4},{6,7},{7,6},{8,9},{9,8},{10,11... | collective-permute-start | bytes 98312 | tf_op jit(solution)/shard_map/ppermute | solution.py:312
  7.2 0.0 copy-done.7
  7.2 0.0 copy-done.2
  7.3 0.0 copy-done.9
  7.3 1.7 %shard_map.118 = (bf16[16,128,128]{2,1,0:T(8,128)(2,1)S(1)}, f32[32,1024]{1,0:T(8,128)S(1)}, bf16[64,160]{1,0:T(8,128)(2,1)S(1)}) custom-call(f32[1,1,25]{2,1,0:T(1,128)S(1)} %copy-done.9, bf16[1,256,1024]{2,1,0:T(8,128)(2,1)S(1)} %copy-done.7, bf16[1,256,1024]{2,1,0:T(8,128)(2,1)S(1)} %copy-done.2), custom_call_target="tpu_custom_call" | custom-call | flops 1024 | bytes 1024 | tf_op jit(solution)/shard_map/pallas_call | solution.py:278
  9.0 0.0 copy-done.10
  9.0 0.1 copy.14.src_ref
  9.1 0.0 copy-done.11
  9.1 0.1 copy.15.dst_ref
  9.2 0.0 collective-permute-done.inner_ref
  9.2 0.0 collective-permute-done.1.outer_ref
  9.2 0.0 copy-done.8
  9.2 0.0 copy-start.1
  9.2 1.2 %shard_map.120 = (bf16[16,2,128,128]{3,2,1,0:T(8,128)(2,1)S(1)}, s32[1,16,1,2]{3,2,1,0:T(1,128)S(1)}) custom-call(bf16[64,160]{1,0:T(8,128)(2,1)S(1)} %get-tuple-element.17.bands_ref, s32[1,1,16,2]{3,2,1,0:T(8,128)S(1)} %copy.14.src_ref, s32[1,1,16]{2,1,0:T(1,128)S(1)} %copy-done.8, bf16[16,1024]{1,0:T(8,128)(2,1)S(1)} %collective-permute-done.inner_ref, ...), custom_call_target="tpu_custom_call" | custom-call | flops 1048576 | bytes 2097152 | tf_op jit(solution)/shard_map/pallas_call | solution.py:278
  10.4 0.0 copy-start
  10.4 0.0 copy-start.3
  10.4 0.0 copy-start.4
  10.4 19.7 %all_to_all.5.in_ref = bf16[16,2,128,128]{3,2,1,0:T(8,128)(2,1)S(1)} all-to-all(bf16[16,2,128,128]{3,2,1,0:T(8,128)(2,1)S(1)} %get-tuple-element.23), channel_id=1, replica_groups=mesh['sec'=32,'tile'=16] {'tile'}, dimensions={0} | all-to-all | bytes 2097152 | tf_op jit(solution)/shard_map/all_to_all | solution.py:334
  30.2 1.0 %shard_map.121 = (bf16[11,128,128]{2,1,0:T(8,128)(2,1)S(1)}, f32[5,128,128]{2,1,0:T(8,128)S(1)}) custom-call(s32[1,16,1,2]{3,2,1,0:T(1,128)S(1)} %get-tuple-element.22.dst_ref, bf16[16,2,128,128]{3,2,1,0:T(8,128)(2,1)S(1)} %all_to_all.5.in_ref), custom_call_target="tpu_custom_call" | custom-call | flops 1048576 | bytes 2097152 | tf_op jit(solution)/shard_map/pallas_call | solution.py:278
  31.2 3.8 %collective-permute-start.2 = (bf16[11,128,128]{2,1,0:T(8,128)(2,1)S(1)}, bf16[11,128,128]{2,1,0:T(8,128)(2,1)S(1)}, u32[]{:S(2)}, u32[]{:S(2)}) collective-permute-start(bf16[11,128,128]{2,1,0:T(8,128)(2,1)S(1)} %get-tuple-element.24.a_ref), channel_id=1, source_target_pairs={{0,16},{16,32},{32,48},{48,64},{64,80},{80,96},{96,112},{112,128},... | collective-permute-start | bytes 1081352 | tf_op jit(solution)/shard_map/ppermute | solution.py:356
  35.0 0.0 copy-done.1
  35.0 0.0 copy-start.5
  35.0 0.0 copy-start.6
  35.1 4.0 %collective-permute-start.4 = (bf16[5,128,128]{2,1,0:T(8,128)(2,1)S(1)}, bf16[5,128,128]{2,1,0:T(8,128)(2,1)S(1)}, u32[]{:S(2)}, u32[]{:S(2)}) collective-permute-start(bf16[5,128,128]{2,1,0:T(8,128)(2,1)S(1)} %get-tuple-element.26.b_ref), channel_id=1, source_target_pairs={{0,16},{16,32},{32,48},{48,64},{64,80},{80,96},{96,112},{112,128},... | collective-permute-start | bytes 491528 | tf_op jit(solution)/shard_map/ppermute | solution.py:357
  39.0 2.8 %collective-permute-start.3 = (bf16[1,128,128]{2,1,0:T(8,128)(2,1)S(1)}, bf16[1,128,128]{2,1,0:T(8,128)(2,1)S(1)}, u32[]{:S(2)}, u32[]{:S(2)}) collective-permute-start(bf16[1,128,128]{2,1,0:T(8,128)(2,1)S(1)} %get-tuple-element.27), channel_id=1, source_target_pairs={{1,0},{2,1},{3,2},{4,3},{5,4},{6,5},{7,6},{8,7},{9,8},{10,9},{11,1... | collective-permute-start | bytes 98312 | tf_op jit(solution)/shard_map/ppermute | solution.py:358
  41.8 2.3 %collective-permute-start.6 = (bf16[1,128,128]{2,1,0:T(8,128)(2,1)S(1)}, bf16[1,128,128]{2,1,0:T(8,128)(2,1)S(1)}, u32[]{:S(2)}, u32[]{:S(2)}) collective-permute-start(bf16[1,128,128]{2,1,0:T(8,128)(2,1)S(1)} %get-tuple-element.28), channel_id=1, source_target_pairs={{1,0},{2,1},{3,2},{4,3},{5,4},{6,5},{7,6},{8,7},{9,8},{10,9},{11,1... | collective-permute-start | bytes 98312 | tf_op jit(solution)/shard_map/ppermute | solution.py:361
  44.2 3.3 %collective-permute-start.5 = (bf16[1,128,128]{2,1,0:T(8,128)(2,1)S(1)}, bf16[1,128,128]{2,1,0:T(8,128)(2,1)S(1)}, u32[]{:S(2)}, u32[]{:S(2)}) collective-permute-start(bf16[1,128,128]{2,1,0:T(8,128)(2,1)S(1)} %get-tuple-element.27), channel_id=1, source_target_pairs={{1,16},{2,17},{3,18},{4,19},{5,20},{6,21},{7,22},{8,23},{9,24},{10... | collective-permute-start | bytes 98312 | tf_op jit(solution)/shard_map/ppermute | solution.py:360
  47.5 0.0 copy-done
  47.5 0.0 copy-done.3
  47.5 0.0 copy-done.4
  47.5 0.9 %shard_map.122.cur_ref = bf16[256,1408]{1,0:T(8,128)(2,1)S(1)} custom-call(bf16[11,128,128]{2,1,0:T(8,128)(2,1)S(1)} %get-tuple-element.24.a_ref, bf16[256,256]{1,0:T(8,128)(2,1)S(1)} %copy-done.4, bf16[256,256]{1,0:T(8,128)(2,1)S(1)} %copy-done.3, bf16[1408,128]{1,0:T(8,128)(2,1)S(1)} %copy-done), custom_call_target="tpu_custom_call" | custom-call | flops 1024 | bytes 1024 | tf_op jit(solution)/shard_map/pallas_call | solution.py:278
  48.4 0.0 collective-permute-done.3.rim_ref
  48.4 0.8 %shard_map.125.cur_ref = bf16[256,896]{1,0:T(8,128)(2,1)S(1)} custom-call(bf16[11,128,128]{2,1,0:T(8,128)(2,1)S(1)} %get-tuple-element.24.a_ref, bf16[5,128,128]{2,1,0:T(8,128)(2,1)S(1)} %get-tuple-element.26.b_ref, bf16[1,128,128]{2,1,0:T(8,128)(2,1)S(1)} %collective-permute-done.3.rim_ref, bf16[256,256]{1,0:T(8,128)(2,1)S(1)} %copy-done.4, ...), custom_call_target="tpu_custom_call" | custom-call | flops 1024 | bytes 1024 | tf_op jit(solution)/shard_map/pallas_call | solution.py:278
  49.2 3.3 %collective-permute-done.2.a_ref = bf16[11,128,128]{2,1,0:T(8,128)(2,1)S(1)} collective-permute-done((bf16[11,128,128]{2,1,0:T(8,128)(2,1)S(1)}, bf16[11,128,128]{2,1,0:T(8,128)(2,1)S(1)}, u32[]{:S(2)}, u32[]{:S(2)}) %collective-permute-start.2) | collective-permute-done | bytes 360480 | tf_op jit(solution)/shard_map/ppermute | solution.py:356
  52.5 0.0 copy-done.5
  52.5 0.0 copy-done.6
  52.5 2.6 %shard_map.123.held = f32[1,32,128,128]{3,2,1,0:T(8,128)} custom-call(bf16[256,1408]{1,0:T(8,128)(2,1)S(1)} %shard_map.122.cur_ref, bf16[11,128,128]{2,1,0:T(8,128)(2,1)S(1)} %collective-permute-done.2.a_ref, bf16[16,128,128]{2,1,0:T(8,128)(2,1)S(1)} %copy-done.1, bf16[256,256]{1,0:T(8,128)(2,1)S(1)} %copy-done.4, bf16[256,256]{1,0:T(8,128)(2,1)S(1)} %copy-done.3, ...), custom_call_target="tpu_custom_call" | custom-call | flops 1024 | bytes 1024 | tf_op jit(solution)/shard_map/pallas_call | solution.py:278
  55.0 0.0 collective-permute-done.6.border_ref
  55.0 0.7 %collective-permute-done.5.rim_ref = bf16[1,128,128]{2,1,0:T(8,128)(2,1)S(1)} collective-permute-done((bf16[1,128,128]{2,1,0:T(8,128)(2,1)S(1)}, bf16[1,128,128]{2,1,0:T(8,128)(2,1)S(1)}, u32[]{:S(2)}, u32[]{:S(2)}) %collective-permute-start.5) | collective-permute-done | bytes 32800 | tf_op jit(solution)/shard_map/ppermute | solution.py:360
  55.7 0.3 collective-permute-done.4.b_ref
  56.0 2.2 %shard_map.126 = f32[1,32,128,128]{3,2,1,0:T(8,128)} custom-call(f32[1,32,128,128]{3,2,1,0:T(8,128)} %shard_map.123.held, bf16[256,896]{1,0:T(8,128)(2,1)S(1)} %shard_map.125.cur_ref, bf16[11,128,128]{2,1,0:T(8,128)(2,1)S(1)} %collective-permute-done.2.a_ref, bf16[5,128,128]{2,1,0:T(8,128)(2,1)S(1)} %collective-permute-done.4.b_ref, ...), custom_call_target="tpu_custom_call", output_to_operand_aliasing={{}: (0, {})} | custom-call | flops 1073741824 | bytes 4194304 | tf_op jit(solution)/shard_map/pallas_call | solution.py:278
  (1 shorter events, 0.0 us)
Async XLA Ops:
  0.0 7.2 %copy-start.7 = (bf16[1,256,1024]{2,1,0:T(8,128)(2,1)S(1)}, bf16[1,256,1024]{2,1,0:T(8,128)(2,1)}, u32[]{:S(2)}) copy-start(bf16[1,256,1024]{2,1,0:T(8,128)(2,1)} %image.1) | copy-start | bytes 1572868
  0.0 7.2 %copy-start.2 = (bf16[1,256,1024]{2,1,0:T(8,128)(2,1)S(1)}, bf16[1,256,1024]{2,1,0:T(8,128)(2,1)}, u32[]{:S(2)}) copy-start(bf16[1,256,1024]{2,1,0:T(8,128)(2,1)} %weight_ref.3) | copy-start | bytes 1572868
  0.0 7.3 %copy-start.9 = (f32[1,1,25]{2,1,0:T(1,128)S(1)}, f32[1,1,25]{2,1,0:T(1,128)}, u32[]{:S(2)}) copy-start(f32[1,1,25]{2,1,0:T(1,128)} %taps_ref.1) | copy-start | bytes 304
  0.0 9.0 %copy-start.10 = (s32[1,1,16,2]{2,3,1,0:T(2,128)S(1)}, s32[1,1,16,2]{2,3,1,0:T(2,128)}, u32[]{:S(2)}) copy-start(s32[1,1,16,2]{2,3,1,0:T(2,128)} %param.15) | copy-start | bytes 388
  0.0 9.1 %copy-start.11 = (s32[1,16,1,2]{1,3,2,0:T(2,128)S(1)}, s32[1,16,1,2]{1,3,2,0:T(2,128)}, u32[]{:S(2)}) copy-start(s32[1,16,1,2]{1,3,2,0:T(2,128)} %param.16) | copy-start | bytes 388
  0.0 9.1 %copy-start.8 = (s32[1,1,16]{2,1,0:T(1,128)S(1)}, s32[1,1,16]{2,1,0:T(1,128)}, u32[]{:S(2)}) copy-start(s32[1,1,16]{2,1,0:T(1,128)} %count_ref.1) | copy-start | bytes 196
  1.0 8.2 %collective-permute-start.1 = (bf16[32,1024]{1,0:T(8,128)(2,1)S(1)}, bf16[32,1024]{1,0:T(8,128)(2,1)S(1)}, u32[]{:S(2)}, u32[]{:S(2)}) collective-permute-start(bf16[32,1024]{1,0:T(8,128)(2,1)S(1)} %get-tuple-element.19), channel_id=1, source_target_pairs={{1,2},{2,1},{3,4},{4,3},{5,6},{6,5},{7,8},{8,7},{9,10},{10,9},{11,... | collective-permute-start | bytes 196616 | tf_op jit(solution)/shard_map/ppermute | solution.py:311
  5.3 3.9 %collective-permute-start = (bf16[16,1024]{1,0:T(8,128)(2,1)S(1)}, bf16[16,1024]{1,0:T(8,128)(2,1)S(1)}, u32[]{:S(2)}, u32[]{:S(2)}) collective-permute-start(bf16[16,1024]{1,0:T(8,128)(2,1)S(1)} %get-tuple-element.18), channel_id=1, source_target_pairs={{0,1},{1,0},{2,3},{3,2},{4,5},{5,4},{6,7},{7,6},{8,9},{9,8},{10,11... | collective-permute-start | bytes 98312 | tf_op jit(solution)/shard_map/ppermute | solution.py:312
  9.2 25.8 %copy-start.1 = (bf16[16,128,128]{2,1,0:T(8,128)(2,1)S(1)}, bf16[16,128,128]{2,1,0:T(8,128)(2,1)}, u32[]{:S(2)}) copy-start(bf16[16,128,128]{2,1,0:T(8,128)(2,1)} %anchor_ref.5) | copy-start | bytes 1572868
  10.4 37.1 %copy-start = (bf16[1408,128]{1,0:T(8,128)(2,1)S(1)}, bf16[1408,128]{1,0:T(8,128)(2,1)}, u32[]{:S(2)}) copy-start(bf16[1408,128]{1,0:T(8,128)(2,1)} %constant.12.clone.refs_2_) | copy-start | bytes 1081348
  10.4 37.1 %copy-start.3 = (bf16[256,256]{1,0:T(8,128)(2,1)S(1)}, bf16[256,256]{1,0:T(8,128)(2,1)}, u32[]{:S(2)}) copy-start(bf16[256,256]{1,0:T(8,128)(2,1)} %constant.11.clone.refs_1_) | copy-start | bytes 393220
  10.4 37.1 %copy-start.4 = (bf16[256,256]{1,0:T(8,128)(2,1)S(1)}, bf16[256,256]{1,0:T(8,128)(2,1)}, u32[]{:S(2)}) copy-start(bf16[256,256]{1,0:T(8,128)(2,1)} %constant.10.clone.refs_0_) | copy-start | bytes 393220
  31.2 21.3 %collective-permute-start.2 = (bf16[11,128,128]{2,1,0:T(8,128)(2,1)S(1)}, bf16[11,128,128]{2,1,0:T(8,128)(2,1)S(1)}, u32[]{:S(2)}, u32[]{:S(2)}) collective-permute-start(bf16[11,128,128]{2,1,0:T(8,128)(2,1)S(1)} %get-tuple-element.24.a_ref), channel_id=1, source_target_pairs={{0,16},{16,32},{32,48},{48,64},{64,80},{80,96},{96,112},{112,128},... | collective-permute-start | bytes 1081352 | tf_op jit(solution)/shard_map/ppermute | solution.py:356
  35.0 17.4 %copy-start.5 = (bf16[256,256]{1,0:T(8,128)(2,1)S(1)}, bf16[256,256]{1,0:T(8,128)(2,1)}, u32[]{:S(2)}) copy-start(bf16[256,256]{1,0:T(8,128)(2,1)} %constant.14.clone.refs_4_) | copy-start | bytes 393220
  35.0 17.4 %copy-start.6 = (bf16[256,256]{1,0:T(8,128)(2,1)S(1)}, bf16[256,256]{1,0:T(8,128)(2,1)}, u32[]{:S(2)}) copy-start(bf16[256,256]{1,0:T(8,128)(2,1)} %constant.13.clone.refs_3_) | copy-start | bytes 393220
  35.1 21.0 %collective-permute-start.4 = (bf16[5,128,128]{2,1,0:T(8,128)(2,1)S(1)}, bf16[5,128,128]{2,1,0:T(8,128)(2,1)S(1)}, u32[]{:S(2)}, u32[]{:S(2)}) collective-permute-start(bf16[5,128,128]{2,1,0:T(8,128)(2,1)S(1)} %get-tuple-element.26.b_ref), channel_id=1, source_target_pairs={{0,16},{16,32},{32,48},{48,64},{64,80},{80,96},{96,112},{112,128},... | collective-permute-start | bytes 491528 | tf_op jit(solution)/shard_map/ppermute | solution.py:357
  39.0 9.4 %collective-permute-start.3 = (bf16[1,128,128]{2,1,0:T(8,128)(2,1)S(1)}, bf16[1,128,128]{2,1,0:T(8,128)(2,1)S(1)}, u32[]{:S(2)}, u32[]{:S(2)}) collective-permute-start(bf16[1,128,128]{2,1,0:T(8,128)(2,1)S(1)} %get-tuple-element.27), channel_id=1, source_target_pairs={{1,0},{2,1},{3,2},{4,3},{5,4},{6,5},{7,6},{8,7},{9,8},{10,9},{11,1... | collective-permute-start | bytes 98312 | tf_op jit(solution)/shard_map/ppermute | solution.py:358
  41.8 13.2 %collective-permute-start.6 = (bf16[1,128,128]{2,1,0:T(8,128)(2,1)S(1)}, bf16[1,128,128]{2,1,0:T(8,128)(2,1)S(1)}, u32[]{:S(2)}, u32[]{:S(2)}) collective-permute-start(bf16[1,128,128]{2,1,0:T(8,128)(2,1)S(1)} %get-tuple-element.28), channel_id=1, source_target_pairs={{1,0},{2,1},{3,2},{4,3},{5,4},{6,5},{7,6},{8,7},{9,8},{10,9},{11,1... | collective-permute-start | bytes 98312 | tf_op jit(solution)/shard_map/ppermute | solution.py:361
  44.2 11.5 %collective-permute-start.5 = (bf16[1,128,128]{2,1,0:T(8,128)(2,1)S(1)}, bf16[1,128,128]{2,1,0:T(8,128)(2,1)S(1)}, u32[]{:S(2)}, u32[]{:S(2)}) collective-permute-start(bf16[1,128,128]{2,1,0:T(8,128)(2,1)S(1)} %get-tuple-element.27), channel_id=1, source_target_pairs={{1,16},{2,17},{3,18},{4,19},{5,20},{6,21},{7,22},{8,23},{9,24},{10... | collective-permute-start | bytes 98312 | tf_op jit(solution)/shard_map/ppermute | solution.py:360

commit v7 on v6

--- a/solution.py
+++ b/solution.py
@@ -165,10 +165,19 @@
     rest_ref[...] = acc_ref[EARLY:]
 
 
+def packed_rim(block):
+    return jnp.concatenate([block[:H, :H], block[H:, :H]], 1)
+
+
+def unpacked_rim(rim):
+    gap = jnp.zeros((H, H), rim.dtype)
+    return jnp.concatenate([jnp.concatenate([rim[:, :H], gap], 1), jnp.concatenate([rim[:, H:], gap], 1)], 0)
+
+
 def rest_kernel(a_ref, rest_ref, anchor_ref, b_ref, first_ref, anchor_first_ref):
     b_ref[...] = rest_ref[...].astype(BF16)
-    first_ref[0] = a_ref[0]
-    anchor_first_ref[0] = anchor_ref[0]
+    first_ref[...] = packed_rim(a_ref[0])
+    anchor_first_ref[...] = packed_rim(anchor_ref[0])
 
 
 def forward(blocks, right, left, middle):
@@ -193,7 +202,7 @@
 
 
 def late_kernel(a_ref, b_ref, rim_ref, *refs):
-    spectra_out([a_ref[EARLY - 1]] + [b_ref[m] for m in range(b_ref.shape[0])] + [rim_ref[0]], *refs)
+    spectra_out([a_ref[EARLY - 1]] + [b_ref[m] for m in range(b_ref.shape[0])] + [unpacked_rim(rim_ref[...])], *refs)
 
 
 def correlate_chunk(cur_ref, blocks, tables, out, at, cross_ref, mag_ref, result_ref, sems):
@@ -263,7 +272,7 @@
     is_first = lax.axis_index("sec") == 0
     blocks = [jnp.where(is_first, anchor_ref[EARLY - 1], a_ref[EARLY - 1])]
     blocks += [jnp.where(is_first, anchor_ref[EARLY + m], b_ref[m]) for m in range(b_ref.shape[0])]
-    blocks += [jnp.where(is_first, border_ref[0], rim_ref[0])]
+    blocks += [unpacked_rim(jnp.where(is_first, border_ref[...], rim_ref[...]))]
     correlate_chunk(cur_ref, blocks, refs[:5], refs[5], EARLY - 1, *refs[6:])
 
 
@@ -344,7 +353,7 @@
     )
     part_b, first, anchor_first = call(
         rest_kernel,
-        (shape((count - EARLY, B, B), BF16), shape((1, B, B), BF16), shape((1, B, B), BF16)),
+        (shape((count - EARLY, B, B), BF16), shape((H, B), BF16), shape((H, B), BF16)),
         [VMEM] * 3,
         (VMEM, VMEM, VMEM),
         [],

time: 58.6 us -> 58.2 us (level)
  no operation moved by 1% of the time
where the time goes in v7:
time: 58.2 us; the launch traced here: 57.9 us
  starting transfers between devices  22.4 us (38%)
  blocking collectives  19.7 us (34%)
  Pallas kernels  11.4 us (20%)
  waiting for transfers between devices  3.92 us (7%)
    all_to_all x1, blocking collectives, body(): lax.all_to_all(outgoing, 'tile', split_axis=0, concat_axis=0, tiled=True)  19.7 us
    pallas_call x9, Pallas kernels, call(): pl.pallas_call(kernel, out_shape=out_shape, in_specs=in_specs, out_specs=...  11.4 us
    ppermute x1, starting transfers between devices, body(): lax.ppermute(outer, 'tile', [(t, t + 2 * (t % 2) - 1) for t in range(1, s...  4.29 us
    ppermute x1, starting transfers between devices, body(): prior_b = lax.ppermute(part_b, 'sec', on)  3.95 us
    ppermute x1, starting transfers between devices, body(): prior_a = lax.ppermute(part_a, 'sec', on)  3.82 us
    ppermute x1, starting transfers between devices, body(): prior_rim = lax.ppermute(first, ('sec', 'tile'), across)  3.27 us
    ppermute x1, waiting for transfers between devices, body(): prior_a = lax.ppermute(part_a, 'sec', on)  3.23 us
    ppermute x1, starting transfers between devices, body(): own_rim = lax.ppermute(first, 'tile', back)  2.78 us
  transfers between devices with their start and end apart: 7, of which 3 were waited for; matrix products, arithmetic and copies ran while one was open for 0% of the time, Pallas kernels for 10%

profile of v7, /device:TPU:24, one launch (start us, length us, event | category | flops | bytes accessed | tf_op | source)
XLA Modules:
  0.0 57.9 jit_solution(1121570818485271812)
XLA Ops:
  0.0 0.0 copy-start.7
  0.0 0.0 copy-start.2
  0.0 0.0 copy-start.9
  0.0 0.0 copy-start.10
  0.0 0.0 copy-start.11
  0.0 0.0 copy-start.8
  0.0 1.0 %shard_map.119 = (bf16[16,1024]{1,0:T(8,128)(2,1)S(1)}, bf16[32,1024]{1,0:T(8,128)(2,1)S(1)}) custom-call(bf16[1,256,1024]{2,1,0:T(8,128)(2,1)} %image.1), custom_call_target="tpu_custom_call" | custom-call | flops 8589934592 | bytes 131072 | tf_op jit(solution)/shard_map/pallas_call | solution.py:287
  1.0 4.3 %collective-permute-start.1 = (bf16[32,1024]{1,0:T(8,128)(2,1)S(1)}, bf16[32,1024]{1,0:T(8,128)(2,1)S(1)}, u32[]{:S(2)}, u32[]{:S(2)}) collective-permute-start(bf16[32,1024]{1,0:T(8,128)(2,1)S(1)} %get-tuple-element.19), channel_id=1, source_target_pairs={{1,2},{2,1},{3,4},{4,3},{5,6},{6,5},{7,8},{8,7},{9,10},{10,9},{11,... | collective-permute-start | bytes 196616 | tf_op jit(solution)/shard_map/ppermute | solution.py:320
  5.3 1.9 %collective-permute-start = (bf16[16,1024]{1,0:T(8,128)(2,1)S(1)}, bf16[16,1024]{1,0:T(8,128)(2,1)S(1)}, u32[]{:S(2)}, u32[]{:S(2)}) collective-permute-start(bf16[16,1024]{1,0:T(8,128)(2,1)S(1)} %get-tuple-element.18), channel_id=1, source_target_pairs={{0,1},{1,0},{2,3},{3,2},{4,5},{5,4},{6,7},{7,6},{8,9},{9,8},{10,11... | collective-permute-start | bytes 98312 | tf_op jit(solution)/shard_map/ppermute | solution.py:321
  7.2 0.0 copy-done.7
  7.2 0.0 copy-done.2
  7.3 0.0 copy-done.9
  7.3 1.7 %shard_map.118 = (bf16[16,128,128]{2,1,0:T(8,128)(2,1)S(1)}, f32[32,1024]{1,0:T(8,128)S(1)}, bf16[64,160]{1,0:T(8,128)(2,1)S(1)}) custom-call(f32[1,1,25]{2,1,0:T(1,128)S(1)} %copy-done.9, bf16[1,256,1024]{2,1,0:T(8,128)(2,1)S(1)} %copy-done.7, bf16[1,256,1024]{2,1,0:T(8,128)(2,1)S(1)} %copy-done.2), custom_call_target="tpu_custom_call" | custom-call | flops 1024 | bytes 1024 | tf_op jit(solution)/shard_map/pallas_call | solution.py:287
  9.0 0.0 copy-done.10
  9.0 0.1 copy.14.src_ref
  9.1 0.0 copy-done.11
  9.1 0.1 copy.15.dst_ref
  9.2 0.0 collective-permute-done.inner_ref
  9.2 0.0 collective-permute-done.1.outer_ref
  9.2 0.0 copy-done.8
  9.2 0.0 copy-start.1
  9.2 1.2 %shard_map.120 = (bf16[16,2,128,128]{3,2,1,0:T(8,128)(2,1)S(1)}, s32[1,16,1,2]{3,2,1,0:T(1,128)S(1)}) custom-call(bf16[64,160]{1,0:T(8,128)(2,1)S(1)} %get-tuple-element.17.bands_ref, s32[1,1,16,2]{3,2,1,0:T(8,128)S(1)} %copy.14.src_ref, s32[1,1,16]{2,1,0:T(1,128)S(1)} %copy-done.8, bf16[16,1024]{1,0:T(8,128)(2,1)S(1)} %collective-permute-done.inner_ref, ...), custom_call_target="tpu_custom_call" | custom-call | flops 1048576 | bytes 2097152 | tf_op jit(solution)/shard_map/pallas_call | solution.py:287
  10.4 0.0 copy-start
  10.4 0.0 copy-start.3
  10.4 0.0 copy-start.4
  10.4 19.7 %all_to_all.5.in_ref = bf16[16,2,128,128]{3,2,1,0:T(8,128)(2,1)S(1)} all-to-all(bf16[16,2,128,128]{3,2,1,0:T(8,128)(2,1)S(1)} %get-tuple-element.23), channel_id=1, replica_groups=mesh['sec'=32,'tile'=16] {'tile'}, dimensions={0} | all-to-all | bytes 2097152 | tf_op jit(solution)/shard_map/all_to_all | solution.py:343
  30.2 1.0 %shard_map.121 = (bf16[11,128,128]{2,1,0:T(8,128)(2,1)S(1)}, f32[5,128,128]{2,1,0:T(8,128)S(1)}) custom-call(s32[1,16,1,2]{3,2,1,0:T(1,128)S(1)} %get-tuple-element.22.dst_ref, bf16[16,2,128,128]{3,2,1,0:T(8,128)(2,1)S(1)} %all_to_all.5.in_ref), custom_call_target="tpu_custom_call" | custom-call | flops 1048576 | bytes 2097152 | tf_op jit(solution)/shard_map/pallas_call | solution.py:287
  31.2 3.8 %collective-permute-start.2 = (bf16[11,128,128]{2,1,0:T(8,128)(2,1)S(1)}, bf16[11,128,128]{2,1,0:T(8,128)(2,1)S(1)}, u32[]{:S(2)}, u32[]{:S(2)}) collective-permute-start(bf16[11,128,128]{2,1,0:T(8,128)(2,1)S(1)} %get-tuple-element.24.a_ref), channel_id=1, source_target_pairs={{0,16},{16,32},{32,48},{48,64},{64,80},{80,96},{96,112},{112,128},... | collective-permute-start | bytes 1081352 | tf_op jit(solution)/shard_map/ppermute | solution.py:365
  35.0 0.0 copy-done.1
  35.0 0.0 copy-start.5
  35.0 0.0 copy-start.6
  35.0 0.1 shard_map.124
  35.1 3.9 %collective-permute-start.4 = (bf16[5,128,128]{2,1,0:T(8,128)(2,1)S(1)}, bf16[5,128,128]{2,1,0:T(8,128)(2,1)S(1)}, u32[]{:S(2)}, u32[]{:S(2)}) collective-permute-start(bf16[5,128,128]{2,1,0:T(8,128)(2,1)S(1)} %get-tuple-element.26.b_ref), channel_id=1, source_target_pairs={{0,16},{16,32},{32,48},{48,64},{64,80},{80,96},{96,112},{112,128},... | collective-permute-start | bytes 491528 | tf_op jit(solution)/shard_map/ppermute | solution.py:366
  39.1 2.8 %collective-permute-start.3 = (bf16[64,128]{1,0:T(8,128)(2,1)S(1)}, bf16[64,128]{1,0:T(8,128)(2,1)S(1)}, u32[]{:S(2)}, u32[]{:S(2)}) collective-permute-start(bf16[64,128]{1,0:T(8,128)(2,1)S(1)} %get-tuple-element.27), channel_id=1, source_target_pairs={{1,0},{2,1},{3,2},{4,3},{5,4},{6,5},{7,6},{8,7},{9,8},{10,9},{11,1... | collective-permute-start | bytes 49160 | tf_op jit(solution)/shard_map/ppermute | solution.py:367
  41.9 2.3 %collective-permute-start.6 = (bf16[64,128]{1,0:T(8,128)(2,1)S(1)}, bf16[64,128]{1,0:T(8,128)(2,1)S(1)}, u32[]{:S(2)}, u32[]{:S(2)}) collective-permute-start(bf16[64,128]{1,0:T(8,128)(2,1)S(1)} %get-tuple-element.28), channel_id=1, source_target_pairs={{1,0},{2,1},{3,2},{4,3},{5,4},{6,5},{7,6},{8,7},{9,8},{10,9},{11,1... | collective-permute-start | bytes 49160 | tf_op jit(solution)/shard_map/ppermute | solution.py:370
  44.2 3.3 %collective-permute-start.5 = (bf16[64,128]{1,0:T(8,128)(2,1)S(1)}, bf16[64,128]{1,0:T(8,128)(2,1)S(1)}, u32[]{:S(2)}, u32[]{:S(2)}) collective-permute-start(bf16[64,128]{1,0:T(8,128)(2,1)S(1)} %get-tuple-element.27), channel_id=1, source_target_pairs={{1,16},{2,17},{3,18},{4,19},{5,20},{6,21},{7,22},{8,23},{9,24},{10... | collective-permute-start | bytes 49160 | tf_op jit(solution)/shard_map/ppermute | solution.py:369
  47.5 0.0 copy-done
  47.5 0.0 copy-done.3
  47.5 0.0 copy-done.4
  47.5 0.9 %shard_map.122.cur_ref = bf16[256,1408]{1,0:T(8,128)(2,1)S(1)} custom-call(bf16[11,128,128]{2,1,0:T(8,128)(2,1)S(1)} %get-tuple-element.24.a_ref, bf16[256,256]{1,0:T(8,128)(2,1)S(1)} %copy-done.4, bf16[256,256]{1,0:T(8,128)(2,1)S(1)} %copy-done.3, bf16[1408,128]{1,0:T(8,128)(2,1)S(1)} %copy-done), custom_call_target="tpu_custom_call" | custom-call | flops 1024 | bytes 1024 | tf_op jit(solution)/shard_map/pallas_call | solution.py:287
  48.5 0.0 collective-permute-done.3.rim_ref
  48.5 0.8 %shard_map.125.cur_ref = bf16[256,896]{1,0:T(8,128)(2,1)S(1)} custom-call(bf16[11,128,128]{2,1,0:T(8,128)(2,1)S(1)} %get-tuple-element.24.a_ref, bf16[5,128,128]{2,1,0:T(8,128)(2,1)S(1)} %get-tuple-element.26.b_ref, bf16[64,128]{1,0:T(8,128)(2,1)S(1)} %collective-permute-done.3.rim_ref, bf16[256,256]{1,0:T(8,128)(2,1)S(1)} %copy-done.4, ...), custom_call_target="tpu_custom_call" | custom-call | flops 1024 | bytes 1024 | tf_op jit(solution)/shard_map/pallas_call | solution.py:287
  49.2 3.2 %collective-permute-done.2.a_ref = bf16[11,128,128]{2,1,0:T(8,128)(2,1)S(1)} collective-permute-done((bf16[11,128,128]{2,1,0:T(8,128)(2,1)S(1)}, bf16[11,128,128]{2,1,0:T(8,128)(2,1)S(1)}, u32[]{:S(2)}, u32[]{:S(2)}) %collective-permute-start.2) | collective-permute-done | bytes 360480 | tf_op jit(solution)/shard_map/ppermute | solution.py:365
  52.5 0.0 copy-done.5
  52.5 0.0 copy-done.6
  52.5 2.6 %shard_map.123.held = f32[1,32,128,128]{3,2,1,0:T(8,128)} custom-call(bf16[256,1408]{1,0:T(8,128)(2,1)S(1)} %shard_map.122.cur_ref, bf16[11,128,128]{2,1,0:T(8,128)(2,1)S(1)} %collective-permute-done.2.a_ref, bf16[16,128,128]{2,1,0:T(8,128)(2,1)S(1)} %copy-done.1, bf16[256,256]{1,0:T(8,128)(2,1)S(1)} %copy-done.4, bf16[256,256]{1,0:T(8,128)(2,1)S(1)} %copy-done.3, ...), custom_call_target="tpu_custom_call" | custom-call | flops 1024 | bytes 1024 | tf_op jit(solution)/shard_map/pallas_call | solution.py:287
  55.0 0.0 collective-permute-done.6.border_ref
  55.1 0.1 collective-permute-done.5.rim_ref
  55.2 0.6 %collective-permute-done.4.b_ref = bf16[5,128,128]{2,1,0:T(8,128)(2,1)S(1)} collective-permute-done((bf16[5,128,128]{2,1,0:T(8,128)(2,1)S(1)}, bf16[5,128,128]{2,1,0:T(8,128)(2,1)S(1)}, u32[]{:S(2)}, u32[]{:S(2)}) %collective-permute-start.4) | collective-permute-done | bytes 163872 | tf_op jit(solution)/shard_map/ppermute | solution.py:366
  55.7 2.2 %shard_map.126 = f32[1,32,128,128]{3,2,1,0:T(8,128)} custom-call(f32[1,32,128,128]{3,2,1,0:T(8,128)} %shard_map.123.held, bf16[256,896]{1,0:T(8,128)(2,1)S(1)} %shard_map.125.cur_ref, bf16[11,128,128]{2,1,0:T(8,128)(2,1)S(1)} %collective-permute-done.2.a_ref, bf16[5,128,128]{2,1,0:T(8,128)(2,1)S(1)} %collective-permute-done.4.b_ref, ...), custom_call_target="tpu_custom_call", output_to_operand_aliasing={{}: (0, {})} | custom-call | flops 1073741824 | bytes 4194304 | tf_op jit(solution)/shard_map/pallas_call | solution.py:287
Async XLA Ops:
  0.0 7.2 %copy-start.7 = (bf16[1,256,1024]{2,1,0:T(8,128)(2,1)S(1)}, bf16[1,256,1024]{2,1,0:T(8,128)(2,1)}, u32[]{:S(2)}) copy-start(bf16[1,256,1024]{2,1,0:T(8,128)(2,1)} %image.1) | copy-start | bytes 1572868
  0.0 7.2 %copy-start.2 = (bf16[1,256,1024]{2,1,0:T(8,128)(2,1)S(1)}, bf16[1,256,1024]{2,1,0:T(8,128)(2,1)}, u32[]{:S(2)}) copy-start(bf16[1,256,1024]{2,1,0:T(8,128)(2,1)} %weight_ref.3) | copy-start | bytes 1572868
  0.0 7.3 %copy-start.9 = (f32[1,1,25]{2,1,0:T(1,128)S(1)}, f32[1,1,25]{2,1,0:T(1,128)}, u32[]{:S(2)}) copy-start(f32[1,1,25]{2,1,0:T(1,128)} %taps_ref.1) | copy-start | bytes 304
  0.0 9.0 %copy-start.10 = (s32[1,1,16,2]{2,3,1,0:T(2,128)S(1)}, s32[1,1,16,2]{2,3,1,0:T(2,128)}, u32[]{:S(2)}) copy-start(s32[1,1,16,2]{2,3,1,0:T(2,128)} %param.15) | copy-start | bytes 388
  0.0 9.1 %copy-start.11 = (s32[1,16,1,2]{1,3,2,0:T(2,128)S(1)}, s32[1,16,1,2]{1,3,2,0:T(2,128)}, u32[]{:S(2)}) copy-start(s32[1,16,1,2]{1,3,2,0:T(2,128)} %param.16) | copy-start | bytes 388
  0.0 9.1 %copy-start.8 = (s32[1,1,16]{2,1,0:T(1,128)S(1)}, s32[1,1,16]{2,1,0:T(1,128)}, u32[]{:S(2)}) copy-start(s32[1,1,16]{2,1,0:T(1,128)} %count_ref.1) | copy-start | bytes 196
  1.0 8.2 %collective-permute-start.1 = (bf16[32,1024]{1,0:T(8,128)(2,1)S(1)}, bf16[32,1024]{1,0:T(8,128)(2,1)S(1)}, u32[]{:S(2)}, u32[]{:S(2)}) collective-permute-start(bf16[32,1024]{1,0:T(8,128)(2,1)S(1)} %get-tuple-element.19), channel_id=1, source_target_pairs={{1,2},{2,1},{3,4},{4,3},{5,6},{6,5},{7,8},{8,7},{9,10},{10,9},{11,... | collective-permute-start | bytes 196616 | tf_op jit(solution)/shard_map/ppermute | solution.py:320
  5.3 3.9 %collective-permute-start = (bf16[16,1024]{1,0:T(8,128)(2,1)S(1)}, bf16[16,1024]{1,0:T(8,128)(2,1)S(1)}, u32[]{:S(2)}, u32[]{:S(2)}) collective-permute-start(bf16[16,1024]{1,0:T(8,128)(2,1)S(1)} %get-tuple-element.18), channel_id=1, source_target_pairs={{0,1},{1,0},{2,3},{3,2},{4,5},{5,4},{6,7},{7,6},{8,9},{9,8},{10,11... | collective-permute-start | bytes 98312 | tf_op jit(solution)/shard_map/ppermute | solution.py:321
  9.2 25.8 %copy-start.1 = (bf16[16,128,128]{2,1,0:T(8,128)(2,1)S(1)}, bf16[16,128,128]{2,1,0:T(8,128)(2,1)}, u32[]{:S(2)}) copy-start(bf16[16,128,128]{2,1,0:T(8,128)(2,1)} %anchor_ref.5) | copy-start | bytes 1572868
  10.4 37.1 %copy-start = (bf16[1408,128]{1,0:T(8,128)(2,1)S(1)}, bf16[1408,128]{1,0:T(8,128)(2,1)}, u32[]{:S(2)}) copy-start(bf16[1408,128]{1,0:T(8,128)(2,1)} %constant.12.clone.refs_2_) | copy-start | bytes 1081348
  10.4 37.1 %copy-start.3 = (bf16[256,256]{1,0:T(8,128)(2,1)S(1)}, bf16[256,256]{1,0:T(8,128)(2,1)}, u32[]{:S(2)}) copy-start(bf16[256,256]{1,0:T(8,128)(2,1)} %constant.11.clone.refs_1_) | copy-start | bytes 393220
  10.4 37.1 %copy-start.4 = (bf16[256,256]{1,0:T(8,128)(2,1)S(1)}, bf16[256,256]{1,0:T(8,128)(2,1)}, u32[]{:S(2)}) copy-start(bf16[256,256]{1,0:T(8,128)(2,1)} %constant.10.clone.refs_0_) | copy-start | bytes 393220
  31.2 21.3 %collective-permute-start.2 = (bf16[11,128,128]{2,1,0:T(8,128)(2,1)S(1)}, bf16[11,128,128]{2,1,0:T(8,128)(2,1)S(1)}, u32[]{:S(2)}, u32[]{:S(2)}) collective-permute-start(bf16[11,128,128]{2,1,0:T(8,128)(2,1)S(1)} %get-tuple-element.24.a_ref), channel_id=1, source_target_pairs={{0,16},{16,32},{32,48},{48,64},{64,80},{80,96},{96,112},{112,128},... | collective-permute-start | bytes 1081352 | tf_op jit(solution)/shard_map/ppermute | solution.py:365
  35.0 17.4 %copy-start.5 = (bf16[256,256]{1,0:T(8,128)(2,1)S(1)}, bf16[256,256]{1,0:T(8,128)(2,1)}, u32[]{:S(2)}) copy-start(bf16[256,256]{1,0:T(8,128)(2,1)} %constant.14.clone.refs_4_) | copy-start | bytes 393220
  35.0 17.4 %copy-start.6 = (bf16[256,256]{1,0:T(8,128)(2,1)S(1)}, bf16[256,256]{1,0:T(8,128)(2,1)}, u32[]{:S(2)}) copy-start(bf16[256,256]{1,0:T(8,128)(2,1)} %constant.13.clone.refs_3_) | copy-start | bytes 393220
  35.1 20.6 %collective-permute-start.4 = (bf16[5,128,128]{2,1,0:T(8,128)(2,1)S(1)}, bf16[5,128,128]{2,1,0:T(8,128)(2,1)S(1)}, u32[]{:S(2)}, u32[]{:S(2)}) collective-permute-start(bf16[5,128,128]{2,1,0:T(8,128)(2,1)S(1)} %get-tuple-element.26.b_ref), channel_id=1, source_target_pairs={{0,16},{16,32},{32,48},{48,64},{64,80},{80,96},{96,112},{112,128},... | collective-permute-start | bytes 491528 | tf_op jit(solution)/shard_map/ppermute | solution.py:366
  39.1 9.4 %collective-permute-start.3 = (bf16[64,128]{1,0:T(8,128)(2,1)S(1)}, bf16[64,128]{1,0:T(8,128)(2,1)S(1)}, u32[]{:S(2)}, u32[]{:S(2)}) collective-permute-start(bf16[64,128]{1,0:T(8,128)(2,1)S(1)} %get-tuple-element.27), channel_id=1, source_target_pairs={{1,0},{2,1},{3,2},{4,3},{5,4},{6,5},{7,6},{8,7},{9,8},{10,9},{11,1... | collective-permute-start | bytes 49160 | tf_op jit(solution)/shard_map/ppermute | solution.py:367
  41.9 13.2 %collective-permute-start.6 = (bf16[64,128]{1,0:T(8,128)(2,1)S(1)}, bf16[64,128]{1,0:T(8,128)(2,1)S(1)}, u32[]{:S(2)}, u32[]{:S(2)}) collective-permute-start(bf16[64,128]{1,0:T(8,128)(2,1)S(1)} %get-tuple-element.28), channel_id=1, source_target_pairs={{1,0},{2,1},{3,2},{4,3},{5,4},{6,5},{7,6},{8,7},{9,8},{10,9},{11,1... | collective-permute-start | bytes 49160 | tf_op jit(solution)/shard_map/ppermute | solution.py:370
  44.2 10.9 %collective-permute-start.5 = (bf16[64,128]{1,0:T(8,128)(2,1)S(1)}, bf16[64,128]{1,0:T(8,128)(2,1)S(1)}, u32[]{:S(2)}, u32[]{:S(2)}) collective-permute-start(bf16[64,128]{1,0:T(8,128)(2,1)S(1)} %get-tuple-element.27), channel_id=1, source_target_pairs={{1,16},{2,17},{3,18},{4,19},{5,20},{6,21},{7,22},{8,23},{9,24},{10... | collective-permute-start | bytes 49160 | tf_op jit(solution)/shard_map/ppermute | solution.py:369

commit v8 on v7

--- a/solution.py
+++ b/solution.py
@@ -63,7 +63,8 @@
     for b in range(5):
         band = jnp.zeros(which.shape, F32)
         for a in range(5):
-            band = jnp.where(which == a, taps_ref[0, 0, 5 * a + b], band)
+            tap = taps_ref[0, :, 5 * a + b : 5 * a + b + 1]
+            band = jnp.where(which == a, tap, band)
         if valid is not None:
             band = jnp.where(valid, band, 0.0)
         top = band.astype(BF16)
@@ -126,19 +127,15 @@
 
 
 def pick_kernel(
-    bands_ref, src_ref, count_ref, inner_ref, outer_ref, edge_ref, weight_ref, blocks_ref, dst_ref, out, dst_out, fixed_ref
+    bands_ref, src, counts, inner_ref, outer_ref, edge_ref, weight_ref, blocks_ref, dst_ref, out, dst_out, fixed_ref, src_ref, count_ref, sems
 ):
+    loads = [pltpu.make_async_copy(src, src_ref, sems.at[0]), pltpu.make_async_copy(counts, count_ref, sems.at[1])]
+    for load in loads:
+        load.start()
     dst_out[...] = dst_ref[...]
     rows, cols = weight_ref.shape[1:]
     across = cols // B
     count = rows // B * across
-    places = []
-    for d in range(out.shape[0]):
-        for q in range(out.shape[1]):
-            live = q < count_ref[0, 0, d]
-            block = src_ref[0, 0, d, q]
-            out[d, q] = jnp.where(live, blocks_ref[block], jnp.zeros((), BF16))
-            places.append((d, q, live, block))
     odd = lax.rem(lax.axis_index("tile"), 2) == 1
     inner, outer = inner_ref[...], outer_ref[...]
     rim = jnp.concatenate([jnp.where(odd, inner, outer[EDGE:]), jnp.where(odd, outer[:EDGE], inner)], 0)
@@ -150,13 +147,25 @@
     for c in range(across):
         fixed_ref[c] = top[:, c * B : c * B + B]
         fixed_ref[count - across + c] = bottom[:, c * B : c * B + B]
+    for load in loads:
+        load.wait()
+    places = []
+    for d in range(out.shape[0]):
+        for q in range(out.shape[1]):
+            live = q < count_ref[0, 0, d]
+            block = src_ref[0, 0, d, q]
+            out[d, q] = jnp.where(live, blocks_ref[block], jnp.zeros((), BF16))
+            places.append((d, q, live, block))
     for d, q, live, block in places:
         at = pl.multiple_of(jnp.where(block < across, 0, B - EDGE), EDGE)
         out[d, q, pl.ds(at, EDGE), :] = jnp.where(live, fixed_ref[block], jnp.zeros((), BF16))
 
 
-def strip_kernel(dst_ref, in_ref, a_ref, rest_ref, acc_ref):
+def strip_kernel(dst, in_ref, a_ref, rest_ref, acc_ref, dst_ref, sem):
+    load = pltpu.make_async_copy(dst, dst_ref, sem)
+    load.start()
     acc_ref[...] = jnp.zeros_like(acc_ref)
+    load.wait()
     for d in range(in_ref.shape[0]):
         for q in range(in_ref.shape[1]):
             j = dst_ref[0, d, 0, q]
@@ -323,7 +332,7 @@
     blocks, edge, bands = call(
         lens_kernel,
         (shape((tile_blocks, B, B), BF16), shape((2 * EDGE, cols), F32), shape((4 * EDGE, 10 * EDGE), BF16)),
-        [SMEM, VMEM, VMEM],
+        [VMEM, VMEM, VMEM],
         (VMEM, VMEM, VMEM),
         [],
         2**10,
@@ -333,9 +342,14 @@
     outgoing, places = call(
         pick_kernel,
         (shape((strips, slots, B, B), BF16), shape((1, strips, 1, slots), jnp.int32)),
-        [VMEM, SMEM, SMEM] + [VMEM] * 6,
+        [VMEM] * 9,
         (VMEM, VMEM),
-        [pltpu.VMEM((tile_blocks, EDGE, B), BF16)],
+        [
+            pltpu.VMEM((tile_blocks, EDGE, B), BF16),
+            pltpu.SMEM(block_src.shape, jnp.int32),
+            pltpu.SMEM(valid_count.shape, jnp.int32),
+            pltpu.SemaphoreType.DMA((2,)),
+        ],
         2**20,
         4 * 2 * rows * cols,
         (bands, block_src, valid_count, inner, outer, edge, weight, blocks, block_dst),
@@ -344,9 +358,9 @@
     part_a, rest = call(
         strip_kernel,
         (shape((EARLY, B, B), BF16), shape((count - EARLY, B, B), F32)),
-        [SMEM, VMEM],
+        [VMEM, VMEM],
         (VMEM, VMEM),
-        [pltpu.VMEM((count, B, B), F32)],
+        [pltpu.VMEM((count, B, B), F32), pltpu.SMEM(block_dst.shape, jnp.int32), pltpu.SemaphoreType.DMA],
         2**20,
         4 * 2 * rows * cols,
         (places, incoming),

time: 58.2 us -> 57.5 us (0.988)
  Pallas kernels: 11.4 us -> 10.7 us
    pallas_call x9, Pallas kernels: 11.4 us -> 10.7 us  [call(): pl.pallas_call(kernel, out_shape=out_shape, in_specs=in_specs, out_specs=...]
  transfers between devices with their start and end apart: 7 -> 7, of which waited for: 3 -> 4; matrix products, arithmetic and copies ran while one was open for 0% -> 0% of each run, Pallas kernels for 10% -> 10%
where the time goes in v8:
time: 57.5 us; the launch traced here: 57.2 us
  starting transfers between devices  22.4 us (39%)
  blocking collectives  19.7 us (34%)
  Pallas kernels  10.7 us (19%)
  waiting for transfers between devices  3.98 us (7%)
    all_to_all x1, blocking collectives, body(): lax.all_to_all(outgoing, 'tile', split_axis=0, concat_axis=0, tiled=True)  19.7 us
    pallas_call x9, Pallas kernels, call(): pl.pallas_call(kernel, out_shape=out_shape, in_specs=in_specs, out_specs=...  10.7 us
    ppermute x1, starting transfers between devices, body(): lax.ppermute(outer, 'tile', [(t, t + 2 * (t % 2) - 1) for t in range(1, s...  4.29 us
    ppermute x1, starting transfers between devices, body(): prior_b = lax.ppermute(part_b, 'sec', on)  3.95 us
    ppermute x1, starting transfers between devices, body(): prior_a = lax.ppermute(part_a, 'sec', on)  3.83 us
    ppermute x1, starting transfers between devices, body(): prior_rim = lax.ppermute(first, ('sec', 'tile'), across)  3.27 us
    ppermute x1, waiting for transfers between devices, body(): prior_a = lax.ppermute(part_a, 'sec', on)  3.22 us
    ppermute x1, starting transfers between devices, body(): own_rim = lax.ppermute(first, 'tile', back)  2.78 us
  transfers between devices with their start and end apart: 7, of which 4 were waited for; matrix products, arithmetic and copies ran while one was open for 0% of the time, Pallas kernels for 10%

profile of v8, /device:TPU:24, one launch (start us, length us, event | category | flops | bytes accessed | tf_op | source)
XLA Modules:
  0.0 57.2 jit_solution(1824221110010551585)
XLA Ops:
  0.0 0.0 copy-start.7
  0.0 0.0 copy-start.2
  0.0 0.0 copy-start.9
  0.0 0.0 copy-start.10
  0.0 0.0 copy-start.11
  0.0 0.0 copy-start.8
  0.0 1.0 %shard_map.119 = (bf16[16,1024]{1,0:T(8,128)(2,1)S(1)}, bf16[32,1024]{1,0:T(8,128)(2,1)S(1)}) custom-call(bf16[1,256,1024]{2,1,0:T(8,128)(2,1)} %image.1), custom_call_target="tpu_custom_call" | custom-call | flops 8589934592 | bytes 131072 | tf_op jit(solution)/shard_map/pallas_call | solution.py:296
  1.0 4.3 %collective-permute-start.1 = (bf16[32,1024]{1,0:T(8,128)(2,1)S(1)}, bf16[32,1024]{1,0:T(8,128)(2,1)S(1)}, u32[]{:S(2)}, u32[]{:S(2)}) collective-permute-start(bf16[32,1024]{1,0:T(8,128)(2,1)S(1)} %get-tuple-element.19), channel_id=1, source_target_pairs={{1,2},{2,1},{3,4},{4,3},{5,6},{6,5},{7,8},{8,7},{9,10},{10,9},{11,... | collective-permute-start | bytes 196616 | tf_op jit(solution)/shard_map/ppermute | solution.py:329
  5.3 1.9 %collective-permute-start = (bf16[16,1024]{1,0:T(8,128)(2,1)S(1)}, bf16[16,1024]{1,0:T(8,128)(2,1)S(1)}, u32[]{:S(2)}, u32[]{:S(2)}) collective-permute-start(bf16[16,1024]{1,0:T(8,128)(2,1)S(1)} %get-tuple-element.18), channel_id=1, source_target_pairs={{0,1},{1,0},{2,3},{3,2},{4,5},{5,4},{6,7},{7,6},{8,9},{9,8},{10,11... | collective-permute-start | bytes 98312 | tf_op jit(solution)/shard_map/ppermute | solution.py:330
  7.2 0.0 copy-done.7
  7.2 0.0 copy-done.2
  7.3 0.0 copy-done.9
  7.3 1.2 %shard_map.118 = (bf16[16,128,128]{2,1,0:T(8,128)(2,1)S(1)}, f32[32,1024]{1,0:T(8,128)S(1)}, bf16[64,160]{1,0:T(8,128)(2,1)S(1)}) custom-call(f32[1,1,25]{2,1,0:T(1,128)S(1)} %copy-done.9, bf16[1,256,1024]{2,1,0:T(8,128)(2,1)S(1)} %copy-done.7, bf16[1,256,1024]{2,1,0:T(8,128)(2,1)S(1)} %copy-done.2), custom_call_target="tpu_custom_call" | custom-call | flops 1024 | bytes 1024 | tf_op jit(solution)/shard_map/pallas_call | solution.py:296
  8.5 0.0 copy-done.10
  8.5 0.1 copy.14.src
  8.5 0.0 copy-done.11
  8.6 0.1 copy.15.dst_ref
  8.6 0.0 collective-permute-done.inner_ref
  8.6 0.1 collective-permute-done.1.outer_ref
  8.7 0.0 copy-done.8
  8.7 0.0 copy-start.1
  8.7 1.0 %shard_map.120 = (bf16[16,2,128,128]{3,2,1,0:T(8,128)(2,1)S(1)}, s32[1,16,1,2]{3,2,1,0:T(1,128)S(1)}) custom-call(bf16[64,160]{1,0:T(8,128)(2,1)S(1)} %get-tuple-element.17.bands_ref, s32[1,1,16,2]{3,2,1,0:T(8,128)S(1)} %copy.14.src, s32[1,1,16]{2,1,0:T(1,128)S(1)} %copy-done.8, bf16[16,1024]{1,0:T(8,128)(2,1)S(1)} %collective-permute-done.inner_ref, ...), custom_call_target="tpu_custom_call" | custom-call | flops 1048576 | bytes 2097152 | tf_op jit(solution)/shard_map/pallas_call | solution.py:296
  9.8 0.0 copy-start
  9.8 0.0 copy-start.3
  9.8 0.0 copy-start.4
  9.8 19.7 %all_to_all.5.in_ref = bf16[16,2,128,128]{3,2,1,0:T(8,128)(2,1)S(1)} all-to-all(bf16[16,2,128,128]{3,2,1,0:T(8,128)(2,1)S(1)} %get-tuple-element.23), channel_id=1, replica_groups=mesh['sec'=32,'tile'=16] {'tile'}, dimensions={0} | all-to-all | bytes 2097152 | tf_op jit(solution)/shard_map/all_to_all | solution.py:357
  29.5 1.0 %shard_map.121 = (bf16[11,128,128]{2,1,0:T(8,128)(2,1)S(1)}, f32[5,128,128]{2,1,0:T(8,128)S(1)}) custom-call(s32[1,16,1,2]{3,2,1,0:T(1,128)S(1)} %get-tuple-element.22.dst, bf16[16,2,128,128]{3,2,1,0:T(8,128)(2,1)S(1)} %all_to_all.5.in_ref), custom_call_target="tpu_custom_call" | custom-call | flops 1048576 | bytes 2097152 | tf_op jit(solution)/shard_map/pallas_call | solution.py:296
  30.4 3.8 %collective-permute-start.2 = (bf16[11,128,128]{2,1,0:T(8,128)(2,1)S(1)}, bf16[11,128,128]{2,1,0:T(8,128)(2,1)S(1)}, u32[]{:S(2)}, u32[]{:S(2)}) collective-permute-start(bf16[11,128,128]{2,1,0:T(8,128)(2,1)S(1)} %get-tuple-element.24.a_ref), channel_id=1, source_target_pairs={{0,16},{16,32},{32,48},{48,64},{64,80},{80,96},{96,112},{112,128},... | collective-permute-start | bytes 1081352 | tf_op jit(solution)/shard_map/ppermute | solution.py:379
  34.3 0.0 copy-done.1
  34.3 0.0 copy-start.5
  34.3 0.0 copy-start.6
  34.3 0.1 shard_map.124
  34.4 4.0 %collective-permute-start.4 = (bf16[5,128,128]{2,1,0:T(8,128)(2,1)S(1)}, bf16[5,128,128]{2,1,0:T(8,128)(2,1)S(1)}, u32[]{:S(2)}, u32[]{:S(2)}) collective-permute-start(bf16[5,128,128]{2,1,0:T(8,128)(2,1)S(1)} %get-tuple-element.26.b_ref), channel_id=1, source_target_pairs={{0,16},{16,32},{32,48},{48,64},{64,80},{80,96},{96,112},{112,128},... | collective-permute-start | bytes 491528 | tf_op jit(solution)/shard_map/ppermute | solution.py:380
  38.4 2.8 %collective-permute-start.3 = (bf16[64,128]{1,0:T(8,128)(2,1)S(1)}, bf16[64,128]{1,0:T(8,128)(2,1)S(1)}, u32[]{:S(2)}, u32[]{:S(2)}) collective-permute-start(bf16[64,128]{1,0:T(8,128)(2,1)S(1)} %get-tuple-element.27), channel_id=1, source_target_pairs={{1,0},{2,1},{3,2},{4,3},{5,4},{6,5},{7,6},{8,7},{9,8},{10,9},{11,1... | collective-permute-start | bytes 49160 | tf_op jit(solution)/shard_map/ppermute | solution.py:381
  41.1 2.3 %collective-permute-start.6 = (bf16[64,128]{1,0:T(8,128)(2,1)S(1)}, bf16[64,128]{1,0:T(8,128)(2,1)S(1)}, u32[]{:S(2)}, u32[]{:S(2)}) collective-permute-start(bf16[64,128]{1,0:T(8,128)(2,1)S(1)} %get-tuple-element.28), channel_id=1, source_target_pairs={{1,0},{2,1},{3,2},{4,3},{5,4},{6,5},{7,6},{8,7},{9,8},{10,9},{11,1... | collective-permute-start | bytes 49160 | tf_op jit(solution)/shard_map/ppermute | solution.py:384
  43.5 3.3 %collective-permute-start.5 = (bf16[64,128]{1,0:T(8,128)(2,1)S(1)}, bf16[64,128]{1,0:T(8,128)(2,1)S(1)}, u32[]{:S(2)}, u32[]{:S(2)}) collective-permute-start(bf16[64,128]{1,0:T(8,128)(2,1)S(1)} %get-tuple-element.27), channel_id=1, source_target_pairs={{1,16},{2,17},{3,18},{4,19},{5,20},{6,21},{7,22},{8,23},{9,24},{10... | collective-permute-start | bytes 49160 | tf_op jit(solution)/shard_map/ppermute | solution.py:383
  46.8 0.0 copy-done
  46.8 0.0 copy-done.3
  46.8 0.0 copy-done.4
  46.8 0.9 %shard_map.122.cur_ref = bf16[256,1408]{1,0:T(8,128)(2,1)S(1)} custom-call(bf16[11,128,128]{2,1,0:T(8,128)(2,1)S(1)} %get-tuple-element.24.a_ref, bf16[256,256]{1,0:T(8,128)(2,1)S(1)} %copy-done.4, bf16[256,256]{1,0:T(8,128)(2,1)S(1)} %copy-done.3, bf16[1408,128]{1,0:T(8,128)(2,1)S(1)} %copy-done), custom_call_target="tpu_custom_call" | custom-call | flops 1024 | bytes 1024 | tf_op jit(solution)/shard_map/pallas_call | solution.py:296
  47.7 0.0 collective-permute-done.3.rim_ref
  47.7 0.8 %shard_map.125.cur_ref = bf16[256,896]{1,0:T(8,128)(2,1)S(1)} custom-call(bf16[11,128,128]{2,1,0:T(8,128)(2,1)S(1)} %get-tuple-element.24.a_ref, bf16[5,128,128]{2,1,0:T(8,128)(2,1)S(1)} %get-tuple-element.26.b_ref, bf16[64,128]{1,0:T(8,128)(2,1)S(1)} %collective-permute-done.3.rim_ref, bf16[256,256]{1,0:T(8,128)(2,1)S(1)} %copy-done.4, ...), custom_call_target="tpu_custom_call" | custom-call | flops 1024 | bytes 1024 | tf_op jit(solution)/shard_map/pallas_call | solution.py:296
  48.5 3.2 %collective-permute-done.2.a_ref = bf16[11,128,128]{2,1,0:T(8,128)(2,1)S(1)} collective-permute-done((bf16[11,128,128]{2,1,0:T(8,128)(2,1)S(1)}, bf16[11,128,128]{2,1,0:T(8,128)(2,1)S(1)}, u32[]{:S(2)}, u32[]{:S(2)}) %collective-permute-start.2) | collective-permute-done | bytes 360480 | tf_op jit(solution)/shard_map/ppermute | solution.py:379
  51.7 0.0 copy-done.5
  51.7 0.0 copy-done.6
  51.7 2.6 %shard_map.123.held = f32[1,32,128,128]{3,2,1,0:T(8,128)} custom-call(bf16[256,1408]{1,0:T(8,128)(2,1)S(1)} %shard_map.122.cur_ref, bf16[11,128,128]{2,1,0:T(8,128)(2,1)S(1)} %collective-permute-done.2.a_ref, bf16[16,128,128]{2,1,0:T(8,128)(2,1)S(1)} %copy-done.1, bf16[256,256]{1,0:T(8,128)(2,1)S(1)} %copy-done.4, bf16[256,256]{1,0:T(8,128)(2,1)S(1)} %copy-done.3, ...), custom_call_target="tpu_custom_call" | custom-call | flops 1024 | bytes 1024 | tf_op jit(solution)/shard_map/pallas_call | solution.py:296
  54.3 0.0 collective-permute-done.6.border_ref
  54.3 0.1 collective-permute-done.5.rim_ref
  54.4 0.6 collective-permute-done.4.b_ref
  55.0 2.2 %shard_map.126 = f32[1,32,128,128]{3,2,1,0:T(8,128)} custom-call(f32[1,32,128,128]{3,2,1,0:T(8,128)} %shard_map.123.held, bf16[256,896]{1,0:T(8,128)(2,1)S(1)} %shard_map.125.cur_ref, bf16[11,128,128]{2,1,0:T(8,128)(2,1)S(1)} %collective-permute-done.2.a_ref, bf16[5,128,128]{2,1,0:T(8,128)(2,1)S(1)} %collective-permute-done.4.b_ref, ...), custom_call_target="tpu_custom_call", output_to_operand_aliasing={{}: (0, {})} | custom-call | flops 1073741824 | bytes 4194304 | tf_op jit(solution)/shard_map/pallas_call | solution.py:296
Async XLA Ops:
  0.0 7.2 %copy-start.7 = (bf16[1,256,1024]{2,1,0:T(8,128)(2,1)S(1)}, bf16[1,256,1024]{2,1,0:T(8,128)(2,1)}, u32[]{:S(2)}) copy-start(bf16[1,256,1024]{2,1,0:T(8,128)(2,1)} %image.1) | copy-start | bytes 1572868
  0.0 7.2 %copy-start.2 = (bf16[1,256,1024]{2,1,0:T(8,128)(2,1)S(1)}, bf16[1,256,1024]{2,1,0:T(8,128)(2,1)}, u32[]{:S(2)}) copy-start(bf16[1,256,1024]{2,1,0:T(8,128)(2,1)} %weight_ref.3) | copy-start | bytes 1572868
  0.0 7.3 %copy-start.9 = (f32[1,1,25]{2,1,0:T(1,128)S(1)}, f32[1,1,25]{2,1,0:T(1,128)}, u32[]{:S(2)}) copy-start(f32[1,1,25]{2,1,0:T(1,128)} %taps_ref.1) | copy-start | bytes 304
  0.0 8.4 %copy-start.10 = (s32[1,1,16,2]{2,3,1,0:T(2,128)S(1)}, s32[1,1,16,2]{2,3,1,0:T(2,128)}, u32[]{:S(2)}) copy-start(s32[1,1,16,2]{2,3,1,0:T(2,128)} %param.15) | copy-start | bytes 388
  0.0 8.5 %copy-start.11 = (s32[1,16,1,2]{1,3,2,0:T(2,128)S(1)}, s32[1,16,1,2]{1,3,2,0:T(2,128)}, u32[]{:S(2)}) copy-start(s32[1,16,1,2]{1,3,2,0:T(2,128)} %param.16) | copy-start | bytes 388
  0.0 8.7 %copy-start.8 = (s32[1,1,16]{2,1,0:T(1,128)S(1)}, s32[1,1,16]{2,1,0:T(1,128)}, u32[]{:S(2)}) copy-start(s32[1,1,16]{2,1,0:T(1,128)} %counts.1) | copy-start | bytes 196
  1.0 7.7 %collective-permute-start.1 = (bf16[32,1024]{1,0:T(8,128)(2,1)S(1)}, bf16[32,1024]{1,0:T(8,128)(2,1)S(1)}, u32[]{:S(2)}, u32[]{:S(2)}) collective-permute-start(bf16[32,1024]{1,0:T(8,128)(2,1)S(1)} %get-tuple-element.19), channel_id=1, source_target_pairs={{1,2},{2,1},{3,4},{4,3},{5,6},{6,5},{7,8},{8,7},{9,10},{10,9},{11,... | collective-permute-start | bytes 196616 | tf_op jit(solution)/shard_map/ppermute | solution.py:329
  5.3 3.3 %collective-permute-start = (bf16[16,1024]{1,0:T(8,128)(2,1)S(1)}, bf16[16,1024]{1,0:T(8,128)(2,1)S(1)}, u32[]{:S(2)}, u32[]{:S(2)}) collective-permute-start(bf16[16,1024]{1,0:T(8,128)(2,1)S(1)} %get-tuple-element.18), channel_id=1, source_target_pairs={{0,1},{1,0},{2,3},{3,2},{4,5},{5,4},{6,7},{7,6},{8,9},{9,8},{10,11... | collective-permute-start | bytes 98312 | tf_op jit(solution)/shard_map/ppermute | solution.py:330
  8.7 25.6 %copy-start.1 = (bf16[16,128,128]{2,1,0:T(8,128)(2,1)S(1)}, bf16[16,128,128]{2,1,0:T(8,128)(2,1)}, u32[]{:S(2)}) copy-start(bf16[16,128,128]{2,1,0:T(8,128)(2,1)} %anchor_ref.5) | copy-start | bytes 1572868
  9.8 37.0 %copy-start = (bf16[1408,128]{1,0:T(8,128)(2,1)S(1)}, bf16[1408,128]{1,0:T(8,128)(2,1)}, u32[]{:S(2)}) copy-start(bf16[1408,128]{1,0:T(8,128)(2,1)} %constant.12.clone.refs_2_) | copy-start | bytes 1081348
  9.8 37.0 %copy-start.3 = (bf16[256,256]{1,0:T(8,128)(2,1)S(1)}, bf16[256,256]{1,0:T(8,128)(2,1)}, u32[]{:S(2)}) copy-start(bf16[256,256]{1,0:T(8,128)(2,1)} %constant.11.clone.refs_1_) | copy-start | bytes 393220
  9.8 37.0 %copy-start.4 = (bf16[256,256]{1,0:T(8,128)(2,1)S(1)}, bf16[256,256]{1,0:T(8,128)(2,1)}, u32[]{:S(2)}) copy-start(bf16[256,256]{1,0:T(8,128)(2,1)} %constant.10.clone.refs_0_) | copy-start | bytes 393220
  30.4 21.3 %collective-permute-start.2 = (bf16[11,128,128]{2,1,0:T(8,128)(2,1)S(1)}, bf16[11,128,128]{2,1,0:T(8,128)(2,1)S(1)}, u32[]{:S(2)}, u32[]{:S(2)}) collective-permute-start(bf16[11,128,128]{2,1,0:T(8,128)(2,1)S(1)} %get-tuple-element.24.a_ref), channel_id=1, source_target_pairs={{0,16},{16,32},{32,48},{48,64},{64,80},{80,96},{96,112},{112,128},... | collective-permute-start | bytes 1081352 | tf_op jit(solution)/shard_map/ppermute | solution.py:379
  34.3 17.4 %copy-start.5 = (bf16[256,256]{1,0:T(8,128)(2,1)S(1)}, bf16[256,256]{1,0:T(8,128)(2,1)}, u32[]{:S(2)}) copy-start(bf16[256,256]{1,0:T(8,128)(2,1)} %constant.14.clone.refs_4_) | copy-start | bytes 393220
  34.3 17.4 %copy-start.6 = (bf16[256,256]{1,0:T(8,128)(2,1)S(1)}, bf16[256,256]{1,0:T(8,128)(2,1)}, u32[]{:S(2)}) copy-start(bf16[256,256]{1,0:T(8,128)(2,1)} %constant.13.clone.refs_3_) | copy-start | bytes 393220
  34.4 20.6 %collective-permute-start.4 = (bf16[5,128,128]{2,1,0:T(8,128)(2,1)S(1)}, bf16[5,128,128]{2,1,0:T(8,128)(2,1)S(1)}, u32[]{:S(2)}, u32[]{:S(2)}) collective-permute-start(bf16[5,128,128]{2,1,0:T(8,128)(2,1)S(1)} %get-tuple-element.26.b_ref), channel_id=1, source_target_pairs={{0,16},{16,32},{32,48},{48,64},{64,80},{80,96},{96,112},{112,128},... | collective-permute-start | bytes 491528 | tf_op jit(solution)/shard_map/ppermute | solution.py:380
  38.4 9.4 %collective-permute-start.3 = (bf16[64,128]{1,0:T(8,128)(2,1)S(1)}, bf16[64,128]{1,0:T(8,128)(2,1)S(1)}, u32[]{:S(2)}, u32[]{:S(2)}) collective-permute-start(bf16[64,128]{1,0:T(8,128)(2,1)S(1)} %get-tuple-element.27), channel_id=1, source_target_pairs={{1,0},{2,1},{3,2},{4,3},{5,4},{6,5},{7,6},{8,7},{9,8},{10,9},{11,1... | collective-permute-start | bytes 49160 | tf_op jit(solution)/shard_map/ppermute | solution.py:381
  41.1 13.2 %collective-permute-start.6 = (bf16[64,128]{1,0:T(8,128)(2,1)S(1)}, bf16[64,128]{1,0:T(8,128)(2,1)S(1)}, u32[]{:S(2)}, u32[]{:S(2)}) collective-permute-start(bf16[64,128]{1,0:T(8,128)(2,1)S(1)} %get-tuple-element.28), channel_id=1, source_target_pairs={{1,0},{2,1},{3,2},{4,3},{5,4},{6,5},{7,6},{8,7},{9,8},{10,9},{11,1... | collective-permute-start | bytes 49160 | tf_op jit(solution)/shard_map/ppermute | solution.py:384
  43.5 10.9 %collective-permute-start.5 = (bf16[64,128]{1,0:T(8,128)(2,1)S(1)}, bf16[64,128]{1,0:T(8,128)(2,1)S(1)}, u32[]{:S(2)}, u32[]{:S(2)}) collective-permute-start(bf16[64,128]{1,0:T(8,128)(2,1)S(1)} %get-tuple-element.27), channel_id=1, source_target_pairs={{1,16},{2,17},{3,18},{4,19},{5,20},{6,21},{7,22},{8,23},{9,24},{10... | collective-permute-start | bytes 49160 | tf_op jit(solution)/shard_map/ppermute | solution.py:383

commit v9 on v8

--- a/solution.py
+++ b/solution.py
@@ -141,21 +141,21 @@
     rim = jnp.concatenate([jnp.where(odd, inner, outer[EDGE:]), jnp.where(odd, outer[:EDGE], inner)], 0)
     rims = jnp.concatenate([shifted(rim, b - 2) for b in range(5)], 0)
     both = dot(bands_ref[...], rims)
+    for load in loads:
+        load.wait()
+    places = []
+    for d in range(out.shape[0]):
+        for q in range(out.shape[1]):
+            live = q < count_ref[0, 0, d]
+            block = src_ref[0, 0, q, d]
+            out[d, q] = jnp.where(live, blocks_ref[block], jnp.zeros((), BF16))
+            places.append((d, q, live, block))
     corrected = edge_ref[...] + (both[: 2 * EDGE] + both[2 * EDGE :])
     top = (corrected[:EDGE] * weight_ref[0, :EDGE].astype(F32)).astype(BF16)
     bottom = (corrected[EDGE:] * weight_ref[0, rows - EDGE :].astype(F32)).astype(BF16)
     for c in range(across):
         fixed_ref[c] = top[:, c * B : c * B + B]
         fixed_ref[count - across + c] = bottom[:, c * B : c * B + B]
-    for load in loads:
-        load.wait()
-    places = []
-    for d in range(out.shape[0]):
-        for q in range(out.shape[1]):
-            live = q < count_ref[0, 0, d]
-            block = src_ref[0, 0, d, q]
-            out[d, q] = jnp.where(live, blocks_ref[block], jnp.zeros((), BF16))
-            places.append((d, q, live, block))
     for d, q, live, block in places:
         at = pl.multiple_of(jnp.where(block < across, 0, B - EDGE), EDGE)
         out[d, q, pl.ds(at, EDGE), :] = jnp.where(live, fixed_ref[block], jnp.zeros((), BF16))
@@ -168,7 +168,7 @@
     load.wait()
     for d in range(in_ref.shape[0]):
         for q in range(in_ref.shape[1]):
-            j = dst_ref[0, d, 0, q]
+            j = dst_ref[0, 0, q, d]
             acc_ref[j] = acc_ref[j] + in_ref[d, q].astype(F32)
     a_ref[...] = acc_ref[:EARLY].astype(BF16)
     rest_ref[...] = acc_ref[EARLY:]
@@ -313,6 +313,8 @@
     slots = block_src.shape[-1]
     count = anchor.shape[0]
     shape = jax.ShapeDtypeStruct
+    block_src = block_src.transpose(0, 1, 3, 2)
+    block_dst = block_dst.transpose(0, 2, 3, 1)
     whole = lambda *dims: pl.BlockSpec(dims, lambda i: (0,) * len(dims))
     back = [(i + 1, i) for i in range(strips - 1)]
     inner, outer = call(
@@ -341,7 +343,7 @@
     )
     outgoing, places = call(
         pick_kernel,
-        (shape((strips, slots, B, B), BF16), shape((1, strips, 1, slots), jnp.int32)),
+        (shape((strips, slots, B, B), BF16), shape(block_dst.shape, jnp.int32)),
         [VMEM] * 9,
         (VMEM, VMEM),
         [

time: 57.5 us -> 57.1 us (level)
  no operation moved by 1% of the time
where the time goes in v9:
time: 57.1 us; the launch traced here: 56.8 us
  starting transfers between devices  22.4 us (39%)
  blocking collectives  19.5 us (34%)
  Pallas kernels  10.4 us (18%)
  waiting for transfers between devices  4.15 us (7%)
    all_to_all x1, blocking collectives, body(): lax.all_to_all(outgoing, 'tile', split_axis=0, concat_axis=0, tiled=True)  19.5 us
    pallas_call x9, Pallas kernels, call(): pl.pallas_call(kernel, out_shape=out_shape, in_specs=in_specs, out_specs=...  10.4 us
    ppermute x1, starting transfers between devices, body(): lax.ppermute(outer, 'tile', [(t, t + 2 * (t % 2) - 1) for t in range(1, s...  4.29 us
    ppermute x1, starting transfers between devices, body(): prior_b = lax.ppermute(part_b, 'sec', on)  3.95 us
    ppermute x1, starting transfers between devices, body(): prior_a = lax.ppermute(part_a, 'sec', on)  3.82 us
    ppermute x1, starting transfers between devices, body(): prior_rim = lax.ppermute(first, ('sec', 'tile'), across)  3.28 us
    ppermute x1, waiting for transfers between devices, body(): prior_a = lax.ppermute(part_a, 'sec', on)  3.21 us
    ppermute x1, starting transfers between devices, body(): own_rim = lax.ppermute(first, 'tile', back)  2.78 us
  transfers between devices with their start and end apart: 7, of which 4 were waited for; matrix products, arithmetic and copies ran while one was open for 0% of the time, Pallas kernels for 10%

profile of v9, /device:TPU:24, one launch (start us, length us, event | category | flops | bytes accessed | tf_op | source)
XLA Modules:
  0.0 56.8 jit_solution(2296784780953677997)
XLA Ops:
  0.0 0.0 copy-start.7
  0.0 0.0 copy-start.2
  0.0 0.0 copy-start.10
  0.0 0.0 copy-start.11
  0.0 0.0 copy-start.9
  0.0 0.0 copy-start.8
  0.0 1.0 %shard_map.119 = (bf16[16,1024]{1,0:T(8,128)(2,1)S(1)}, bf16[32,1024]{1,0:T(8,128)(2,1)S(1)}) custom-call(bf16[1,256,1024]{2,1,0:T(8,128)(2,1)} %image.1), custom_call_target="tpu_custom_call" | custom-call | flops 8589934592 | bytes 131072 | tf_op jit(solution)/shard_map/pallas_call | solution.py:296
  1.0 4.3 %collective-permute-start.1 = (bf16[32,1024]{1,0:T(8,128)(2,1)S(1)}, bf16[32,1024]{1,0:T(8,128)(2,1)S(1)}, u32[]{:S(2)}, u32[]{:S(2)}) collective-permute-start(bf16[32,1024]{1,0:T(8,128)(2,1)S(1)} %get-tuple-element.19), channel_id=1, source_target_pairs={{1,2},{2,1},{3,4},{4,3},{5,6},{6,5},{7,8},{8,7},{9,10},{10,9},{11,... | collective-permute-start | bytes 196616 | tf_op jit(solution)/shard_map/ppermute | solution.py:331
  5.3 1.9 %collective-permute-start = (bf16[16,1024]{1,0:T(8,128)(2,1)S(1)}, bf16[16,1024]{1,0:T(8,128)(2,1)S(1)}, u32[]{:S(2)}, u32[]{:S(2)}) collective-permute-start(bf16[16,1024]{1,0:T(8,128)(2,1)S(1)} %get-tuple-element.18), channel_id=1, source_target_pairs={{0,1},{1,0},{2,3},{3,2},{4,5},{5,4},{6,7},{7,6},{8,9},{9,8},{10,11... | collective-permute-start | bytes 98312 | tf_op jit(solution)/shard_map/ppermute | solution.py:332
  7.2 0.0 copy-done.7
  7.2 0.0 copy-done.2
  7.3 0.0 copy-done.10
  7.3 1.2 %shard_map.118 = (bf16[16,128,128]{2,1,0:T(8,128)(2,1)S(1)}, f32[32,1024]{1,0:T(8,128)S(1)}, bf16[64,160]{1,0:T(8,128)(2,1)S(1)}) custom-call(f32[1,1,25]{2,1,0:T(1,128)S(1)} %copy-done.10, bf16[1,256,1024]{2,1,0:T(8,128)(2,1)S(1)} %copy-done.7, bf16[1,256,1024]{2,1,0:T(8,128)(2,1)S(1)} %copy-done.2), custom_call_target="tpu_custom_call" | custom-call | flops 1024 | bytes 1024 | tf_op jit(solution)/shard_map/pallas_call | solution.py:296
  8.5 0.0 collective-permute-done.inner_ref
  8.5 0.2 collective-permute-done.1.outer_ref
  8.7 0.0 copy-done.11
  8.7 0.0 copy-done.9
  8.7 0.0 copy-done.8
  8.7 0.0 copy-start.1
  8.7 0.9 %shard_map.120 = (bf16[16,2,128,128]{3,2,1,0:T(8,128)(2,1)S(1)}, s32[1,1,2,16]{3,2,1,0:T(2,128)S(1)}) custom-call(bf16[64,160]{1,0:T(8,128)(2,1)S(1)} %get-tuple-element.17.bands_ref, s32[1,1,2,16]{3,2,1,0:T(2,128)S(1)} %bitcast.2, s32[1,1,16]{2,1,0:T(1,128)S(1)} %copy-done.11, bf16[16,1024]{1,0:T(8,128)(2,1)S(1)} %collective-permute-done.inner_ref, ...), custom_call_target="tpu_custom_call" | custom-call | flops 1048576 | bytes 2097152 | tf_op jit(solution)/shard_map/pallas_call | solution.py:296
  9.7 0.0 copy-start
  9.7 0.0 copy-start.3
  9.7 0.0 copy-start.4
  9.7 19.5 %all_to_all.5.in_ref = bf16[16,2,128,128]{3,2,1,0:T(8,128)(2,1)S(1)} all-to-all(bf16[16,2,128,128]{3,2,1,0:T(8,128)(2,1)S(1)} %get-tuple-element.23), channel_id=1, replica_groups=mesh['sec'=32,'tile'=16] {'tile'}, dimensions={0} | all-to-all | bytes 2097152 | tf_op jit(solution)/shard_map/all_to_all | solution.py:359
  29.2 0.8 %shard_map.121 = (bf16[11,128,128]{2,1,0:T(8,128)(2,1)S(1)}, f32[5,128,128]{2,1,0:T(8,128)S(1)}) custom-call(s32[1,1,2,16]{3,2,1,0:T(2,128)S(1)} %get-tuple-element.22.dst, bf16[16,2,128,128]{3,2,1,0:T(8,128)(2,1)S(1)} %all_to_all.5.in_ref), custom_call_target="tpu_custom_call" | custom-call | flops 1048576 | bytes 2097152 | tf_op jit(solution)/shard_map/pallas_call | solution.py:296
  30.1 3.8 %collective-permute-start.2 = (bf16[11,128,128]{2,1,0:T(8,128)(2,1)S(1)}, bf16[11,128,128]{2,1,0:T(8,128)(2,1)S(1)}, u32[]{:S(2)}, u32[]{:S(2)}) collective-permute-start(bf16[11,128,128]{2,1,0:T(8,128)(2,1)S(1)} %get-tuple-element.24.a_ref), channel_id=1, source_target_pairs={{0,16},{16,32},{32,48},{48,64},{64,80},{80,96},{96,112},{112,128},... | collective-permute-start | bytes 1081352 | tf_op jit(solution)/shard_map/ppermute | solution.py:381
  33.9 0.0 copy-done.1
  33.9 0.0 copy-start.5
  33.9 0.0 copy-start.6
  33.9 0.1 shard_map.124
  34.0 3.9 %collective-permute-start.4 = (bf16[5,128,128]{2,1,0:T(8,128)(2,1)S(1)}, bf16[5,128,128]{2,1,0:T(8,128)(2,1)S(1)}, u32[]{:S(2)}, u32[]{:S(2)}) collective-permute-start(bf16[5,128,128]{2,1,0:T(8,128)(2,1)S(1)} %get-tuple-element.26.b_ref), channel_id=1, source_target_pairs={{0,16},{16,32},{32,48},{48,64},{64,80},{80,96},{96,112},{112,128},... | collective-permute-start | bytes 491528 | tf_op jit(solution)/shard_map/ppermute | solution.py:382
  38.0 2.8 %collective-permute-start.3 = (bf16[64,128]{1,0:T(8,128)(2,1)S(1)}, bf16[64,128]{1,0:T(8,128)(2,1)S(1)}, u32[]{:S(2)}, u32[]{:S(2)}) collective-permute-start(bf16[64,128]{1,0:T(8,128)(2,1)S(1)} %get-tuple-element.27), channel_id=1, source_target_pairs={{1,0},{2,1},{3,2},{4,3},{5,4},{6,5},{7,6},{8,7},{9,8},{10,9},{11,1... | collective-permute-start | bytes 49160 | tf_op jit(solution)/shard_map/ppermute | solution.py:383
  40.8 2.3 %collective-permute-start.6 = (bf16[64,128]{1,0:T(8,128)(2,1)S(1)}, bf16[64,128]{1,0:T(8,128)(2,1)S(1)}, u32[]{:S(2)}, u32[]{:S(2)}) collective-permute-start(bf16[64,128]{1,0:T(8,128)(2,1)S(1)} %get-tuple-element.28), channel_id=1, source_target_pairs={{1,0},{2,1},{3,2},{4,3},{5,4},{6,5},{7,6},{8,7},{9,8},{10,9},{11,1... | collective-permute-start | bytes 49160 | tf_op jit(solution)/shard_map/ppermute | solution.py:386
  43.1 3.3 %collective-permute-start.5 = (bf16[64,128]{1,0:T(8,128)(2,1)S(1)}, bf16[64,128]{1,0:T(8,128)(2,1)S(1)}, u32[]{:S(2)}, u32[]{:S(2)}) collective-permute-start(bf16[64,128]{1,0:T(8,128)(2,1)S(1)} %get-tuple-element.27), channel_id=1, source_target_pairs={{1,16},{2,17},{3,18},{4,19},{5,20},{6,21},{7,22},{8,23},{9,24},{10... | collective-permute-start | bytes 49160 | tf_op jit(solution)/shard_map/ppermute | solution.py:385
  46.4 0.0 copy-done
  46.4 0.0 copy-done.3
  46.4 0.0 copy-done.4
  46.4 0.9 %shard_map.122.cur_ref = bf16[256,1408]{1,0:T(8,128)(2,1)S(1)} custom-call(bf16[11,128,128]{2,1,0:T(8,128)(2,1)S(1)} %get-tuple-element.24.a_ref, bf16[256,256]{1,0:T(8,128)(2,1)S(1)} %copy-done.4, bf16[256,256]{1,0:T(8,128)(2,1)S(1)} %copy-done.3, bf16[1408,128]{1,0:T(8,128)(2,1)S(1)} %copy-done), custom_call_target="tpu_custom_call" | custom-call | flops 1024 | bytes 1024 | tf_op jit(solution)/shard_map/pallas_call | solution.py:296
  47.4 0.0 collective-permute-done.3.rim_ref
  47.4 0.8 %shard_map.125.cur_ref = bf16[256,896]{1,0:T(8,128)(2,1)S(1)} custom-call(bf16[11,128,128]{2,1,0:T(8,128)(2,1)S(1)} %get-tuple-element.24.a_ref, bf16[5,128,128]{2,1,0:T(8,128)(2,1)S(1)} %get-tuple-element.26.b_ref, bf16[64,128]{1,0:T(8,128)(2,1)S(1)} %collective-permute-done.3.rim_ref, bf16[256,256]{1,0:T(8,128)(2,1)S(1)} %copy-done.4, ...), custom_call_target="tpu_custom_call" | custom-call | flops 1024 | bytes 1024 | tf_op jit(solution)/shard_map/pallas_call | solution.py:296
  48.1 3.2 %collective-permute-done.2.a_ref = bf16[11,128,128]{2,1,0:T(8,128)(2,1)S(1)} collective-permute-done((bf16[11,128,128]{2,1,0:T(8,128)(2,1)S(1)}, bf16[11,128,128]{2,1,0:T(8,128)(2,1)S(1)}, u32[]{:S(2)}, u32[]{:S(2)}) %collective-permute-start.2) | collective-permute-done | bytes 360480 | tf_op jit(solution)/shard_map/ppermute | solution.py:381
  51.3 0.0 copy-done.5
  51.3 0.0 copy-done.6
  51.4 2.6 %shard_map.123.held = f32[1,32,128,128]{3,2,1,0:T(8,128)} custom-call(bf16[256,1408]{1,0:T(8,128)(2,1)S(1)} %shard_map.122.cur_ref, bf16[11,128,128]{2,1,0:T(8,128)(2,1)S(1)} %collective-permute-done.2.a_ref, bf16[16,128,128]{2,1,0:T(8,128)(2,1)S(1)} %copy-done.1, bf16[256,256]{1,0:T(8,128)(2,1)S(1)} %copy-done.4, bf16[256,256]{1,0:T(8,128)(2,1)S(1)} %copy-done.3, ...), custom_call_target="tpu_custom_call" | custom-call | flops 1024 | bytes 1024 | tf_op jit(solution)/shard_map/pallas_call | solution.py:296
  53.9 0.0 collective-permute-done.6.border_ref
  54.0 0.1 collective-permute-done.5.rim_ref
  54.1 0.6 collective-permute-done.4.b_ref
  54.6 2.2 %shard_map.126 = f32[1,32,128,128]{3,2,1,0:T(8,128)} custom-call(f32[1,32,128,128]{3,2,1,0:T(8,128)} %shard_map.123.held, bf16[256,896]{1,0:T(8,128)(2,1)S(1)} %shard_map.125.cur_ref, bf16[11,128,128]{2,1,0:T(8,128)(2,1)S(1)} %collective-permute-done.2.a_ref, bf16[5,128,128]{2,1,0:T(8,128)(2,1)S(1)} %collective-permute-done.4.b_ref, ...), custom_call_target="tpu_custom_call", output_to_operand_aliasing={{}: (0, {})} | custom-call | flops 1073741824 | bytes 4194304 | tf_op jit(solution)/shard_map/pallas_call | solution.py:296
Async XLA Ops:
  0.0 7.2 %copy-start.7 = (bf16[1,256,1024]{2,1,0:T(8,128)(2,1)S(1)}, bf16[1,256,1024]{2,1,0:T(8,128)(2,1)}, u32[]{:S(2)}) copy-start(bf16[1,256,1024]{2,1,0:T(8,128)(2,1)} %image.1) | copy-start | bytes 1572868
  0.0 7.2 %copy-start.2 = (bf16[1,256,1024]{2,1,0:T(8,128)(2,1)S(1)}, bf16[1,256,1024]{2,1,0:T(8,128)(2,1)}, u32[]{:S(2)}) copy-start(bf16[1,256,1024]{2,1,0:T(8,128)(2,1)} %weight_ref.3) | copy-start | bytes 1572868
  0.0 7.3 %copy-start.10 = (f32[1,1,25]{2,1,0:T(1,128)S(1)}, f32[1,1,25]{2,1,0:T(1,128)}, u32[]{:S(2)}) copy-start(f32[1,1,25]{2,1,0:T(1,128)} %taps_ref.1) | copy-start | bytes 304
  0.0 8.7 %copy-start.11 = (s32[1,1,16]{2,1,0:T(1,128)S(1)}, s32[1,1,16]{2,1,0:T(1,128)}, u32[]{:S(2)}) copy-start(s32[1,1,16]{2,1,0:T(1,128)} %counts.1) | copy-start | bytes 196
  0.0 8.7 %copy-start.9 = (s32[1,16,1,2]{1,3,2,0:T(2,128)S(1)}, s32[1,16,1,2]{1,3,2,0:T(2,128)}, u32[]{:S(2)}) copy-start(s32[1,16,1,2]{1,3,2,0:T(2,128)} %param.16) | copy-start | bytes 388
  0.0 8.7 %copy-start.8 = (s32[1,1,16,2]{2,3,1,0:T(2,128)S(1)}, s32[1,1,16,2]{2,3,1,0:T(2,128)}, u32[]{:S(2)}) copy-start(s32[1,1,16,2]{2,3,1,0:T(2,128)} %param.15) | copy-start | bytes 388
  1.0 7.7 %collective-permute-start.1 = (bf16[32,1024]{1,0:T(8,128)(2,1)S(1)}, bf16[32,1024]{1,0:T(8,128)(2,1)S(1)}, u32[]{:S(2)}, u32[]{:S(2)}) collective-permute-start(bf16[32,1024]{1,0:T(8,128)(2,1)S(1)} %get-tuple-element.19), channel_id=1, source_target_pairs={{1,2},{2,1},{3,4},{4,3},{5,6},{6,5},{7,8},{8,7},{9,10},{10,9},{11,... | collective-permute-start | bytes 196616 | tf_op jit(solution)/shard_map/ppermute | solution.py:331
  5.3 3.2 %collective-permute-start = (bf16[16,1024]{1,0:T(8,128)(2,1)S(1)}, bf16[16,1024]{1,0:T(8,128)(2,1)S(1)}, u32[]{:S(2)}, u32[]{:S(2)}) collective-permute-start(bf16[16,1024]{1,0:T(8,128)(2,1)S(1)} %get-tuple-element.18), channel_id=1, source_target_pairs={{0,1},{1,0},{2,3},{3,2},{4,5},{5,4},{6,7},{7,6},{8,9},{9,8},{10,11... | collective-permute-start | bytes 98312 | tf_op jit(solution)/shard_map/ppermute | solution.py:332
  8.7 25.2 %copy-start.1 = (bf16[16,128,128]{2,1,0:T(8,128)(2,1)S(1)}, bf16[16,128,128]{2,1,0:T(8,128)(2,1)}, u32[]{:S(2)}) copy-start(bf16[16,128,128]{2,1,0:T(8,128)(2,1)} %anchor_ref.5) | copy-start | bytes 1572868
  9.7 36.7 %copy-start = (bf16[1408,128]{1,0:T(8,128)(2,1)S(1)}, bf16[1408,128]{1,0:T(8,128)(2,1)}, u32[]{:S(2)}) copy-start(bf16[1408,128]{1,0:T(8,128)(2,1)} %constant.12.clone.refs_2_) | copy-start | bytes 1081348
  9.7 36.7 %copy-start.3 = (bf16[256,256]{1,0:T(8,128)(2,1)S(1)}, bf16[256,256]{1,0:T(8,128)(2,1)}, u32[]{:S(2)}) copy-start(bf16[256,256]{1,0:T(8,128)(2,1)} %constant.11.clone.refs_1_) | copy-start | bytes 393220
  9.7 36.7 %copy-start.4 = (bf16[256,256]{1,0:T(8,128)(2,1)S(1)}, bf16[256,256]{1,0:T(8,128)(2,1)}, u32[]{:S(2)}) copy-start(bf16[256,256]{1,0:T(8,128)(2,1)} %constant.10.clone.refs_0_) | copy-start | bytes 393220
  30.1 21.3 %collective-permute-start.2 = (bf16[11,128,128]{2,1,0:T(8,128)(2,1)S(1)}, bf16[11,128,128]{2,1,0:T(8,128)(2,1)S(1)}, u32[]{:S(2)}, u32[]{:S(2)}) collective-permute-start(bf16[11,128,128]{2,1,0:T(8,128)(2,1)S(1)} %get-tuple-element.24.a_ref), channel_id=1, source_target_pairs={{0,16},{16,32},{32,48},{48,64},{64,80},{80,96},{96,112},{112,128},... | collective-permute-start | bytes 1081352 | tf_op jit(solution)/shard_map/ppermute | solution.py:381
  33.9 17.4 %copy-start.5 = (bf16[256,256]{1,0:T(8,128)(2,1)S(1)}, bf16[256,256]{1,0:T(8,128)(2,1)}, u32[]{:S(2)}) copy-start(bf16[256,256]{1,0:T(8,128)(2,1)} %constant.14.clone.refs_4_) | copy-start | bytes 393220
  33.9 17.4 %copy-start.6 = (bf16[256,256]{1,0:T(8,128)(2,1)S(1)}, bf16[256,256]{1,0:T(8,128)(2,1)}, u32[]{:S(2)}) copy-start(bf16[256,256]{1,0:T(8,128)(2,1)} %constant.13.clone.refs_3_) | copy-start | bytes 393220
  34.0 20.6 %collective-permute-start.4 = (bf16[5,128,128]{2,1,0:T(8,128)(2,1)S(1)}, bf16[5,128,128]{2,1,0:T(8,128)(2,1)S(1)}, u32[]{:S(2)}, u32[]{:S(2)}) collective-permute-start(bf16[5,128,128]{2,1,0:T(8,128)(2,1)S(1)} %get-tuple-element.26.b_ref), channel_id=1, source_target_pairs={{0,16},{16,32},{32,48},{48,64},{64,80},{80,96},{96,112},{112,128},... | collective-permute-start | bytes 491528 | tf_op jit(solution)/shard_map/ppermute | solution.py:382
  38.0 9.4 %collective-permute-start.3 = (bf16[64,128]{1,0:T(8,128)(2,1)S(1)}, bf16[64,128]{1,0:T(8,128)(2,1)S(1)}, u32[]{:S(2)}, u32[]{:S(2)}) collective-permute-start(bf16[64,128]{1,0:T(8,128)(2,1)S(1)} %get-tuple-element.27), channel_id=1, source_target_pairs={{1,0},{2,1},{3,2},{4,3},{5,4},{6,5},{7,6},{8,7},{9,8},{10,9},{11,1... | collective-permute-start | bytes 49160 | tf_op jit(solution)/shard_map/ppermute | solution.py:383
  40.8 13.2 %collective-permute-start.6 = (bf16[64,128]{1,0:T(8,128)(2,1)S(1)}, bf16[64,128]{1,0:T(8,128)(2,1)S(1)}, u32[]{:S(2)}, u32[]{:S(2)}) collective-permute-start(bf16[64,128]{1,0:T(8,128)(2,1)S(1)} %get-tuple-element.28), channel_id=1, source_target_pairs={{1,0},{2,1},{3,2},{4,3},{5,4},{6,5},{7,6},{8,7},{9,8},{10,9},{11,1... | collective-permute-start | bytes 49160 | tf_op jit(solution)/shard_map/ppermute | solution.py:386
  43.1 11.0 %collective-permute-start.5 = (bf16[64,128]{1,0:T(8,128)(2,1)S(1)}, bf16[64,128]{1,0:T(8,128)(2,1)S(1)}, u32[]{:S(2)}, u32[]{:S(2)}) collective-permute-start(bf16[64,128]{1,0:T(8,128)(2,1)S(1)} %get-tuple-element.27), channel_id=1, source_target_pairs={{1,16},{2,17},{3,18},{4,19},{5,20},{6,21},{7,22},{8,23},{9,24},{10... | collective-permute-start | bytes 49160 | tf_op jit(solution)/shard_map/ppermute | solution.py:385

commit v10 on v9

--- a/solution.py
+++ b/solution.py
@@ -80,8 +80,8 @@
     wide = outer.shape[0]
     last = image.shape[1] - wide
     to_outer = pltpu.make_async_copy(image.at[0, pl.ds(pl.multiple_of(odd * last, EDGE), wide)], outer, sems.at[1])
-    to_inner.start()
-    to_outer.start()
+    to_outer.start(priority=1)
+    to_inner.start(priority=1)
     to_inner.wait()
     to_outer.wait()
 
@@ -127,12 +127,11 @@
 
 
 def pick_kernel(
-    bands_ref, src, counts, inner_ref, outer_ref, edge_ref, weight_ref, blocks_ref, dst_ref, out, dst_out, fixed_ref, src_ref, count_ref, sems
+    bands_ref, src, counts, inner_ref, outer_ref, edge_ref, weight_ref, blocks_ref, out, fixed_ref, src_ref, count_ref, sems
 ):
     loads = [pltpu.make_async_copy(src, src_ref, sems.at[0]), pltpu.make_async_copy(counts, count_ref, sems.at[1])]
     for load in loads:
         load.start()
-    dst_out[...] = dst_ref[...]
     rows, cols = weight_ref.shape[1:]
     across = cols // B
     count = rows // B * across
@@ -341,11 +340,11 @@
         2**10,
         (lens_filter_taps, image, weight),
     )
-    outgoing, places = call(
+    outgoing = call(
         pick_kernel,
-        (shape((strips, slots, B, B), BF16), shape(block_dst.shape, jnp.int32)),
-        [VMEM] * 9,
-        (VMEM, VMEM),
+        shape((strips, slots, B, B), BF16),
+        [VMEM] * 8,
+        VMEM,
         [
             pltpu.VMEM((tile_blocks, EDGE, B), BF16),
             pltpu.SMEM(block_src.shape, jnp.int32),
@@ -354,7 +353,7 @@
         ],
         2**20,
         4 * 2 * rows * cols,
-        (bands, block_src, valid_count, inner, outer, edge, weight, blocks, block_dst),
+        (bands, block_src, valid_count, inner, outer, edge, weight, blocks),
     )
     incoming = lax.all_to_all(outgoing, "tile", split_axis=0, concat_axis=0, tiled=True)
     part_a, rest = call(
@@ -365,7 +364,7 @@
         [pltpu.VMEM((count, B, B), F32), pltpu.SMEM(block_dst.shape, jnp.int32), pltpu.SemaphoreType.DMA],
         2**20,
         4 * 2 * rows * cols,
-        (places, incoming),
+        (block_dst, incoming),
     )
     part_b, first, anchor_first = call(
         rest_kernel,

time: 57.1 us -> 57.2 us (level)
  no operation moved by 1% of the time
where the time goes in v10:
time: 57.2 us; the launch traced here: 56.8 us
  starting transfers between devices  22.4 us (39%)
  blocking collectives  19.5 us (34%)
  Pallas kernels  10.5 us (18%)
  waiting for transfers between devices  4.15 us (7%)
    all_to_all x1, blocking collectives, body(): lax.all_to_all(outgoing, 'tile', split_axis=0, concat_axis=0, tiled=True)  19.5 us
    pallas_call x9, Pallas kernels, call(): pl.pallas_call(kernel, out_shape=out_shape, in_specs=in_specs, out_specs=...  10.5 us
    ppermute x1, starting transfers between devices, body(): lax.ppermute(outer, 'tile', [(t, t + 2 * (t % 2) - 1) for t in range(1, s...  4.29 us
    ppermute x1, starting transfers between devices, body(): prior_b = lax.ppermute(part_b, 'sec', on)  3.94 us
    ppermute x1, starting transfers between devices, body(): prior_a = lax.ppermute(part_a, 'sec', on)  3.83 us
    ppermute x1, starting transfers between devices, body(): prior_rim = lax.ppermute(first, ('sec', 'tile'), across)  3.28 us
    ppermute x1, waiting for transfers between devices, body(): prior_a = lax.ppermute(part_a, 'sec', on)  3.21 us
    ppermute x1, starting transfers between devices, body(): own_rim = lax.ppermute(first, 'tile', back)  2.78 us
  transfers between devices with their start and end apart: 7, of which 4 were waited for; matrix products, arithmetic and copies ran while one was open for 0% of the time, Pallas kernels for 10%

profile of v10, /device:TPU:24, one launch (start us, length us, event | category | flops | bytes accessed | tf_op | source)
XLA Modules:
  0.0 56.8 jit_solution(100043217004674690)
XLA Ops:
  0.0 0.0 copy-start.7
  0.0 0.0 copy-start.2
  0.0 0.0 copy-start.10
  0.0 0.0 copy-start.11
  0.0 0.0 copy-start.8
  0.0 1.0 %shard_map.119 = (bf16[16,1024]{1,0:T(8,128)(2,1)S(1)}, bf16[32,1024]{1,0:T(8,128)(2,1)S(1)}) custom-call(bf16[1,256,1024]{2,1,0:T(8,128)(2,1)} %image.1), custom_call_target="tpu_custom_call" | custom-call | flops 8589934592 | bytes 131072 | tf_op jit(solution)/shard_map/pallas_call | solution.py:295
  1.0 4.3 %collective-permute-start.1 = (bf16[32,1024]{1,0:T(8,128)(2,1)S(1)}, bf16[32,1024]{1,0:T(8,128)(2,1)S(1)}, u32[]{:S(2)}, u32[]{:S(2)}) collective-permute-start(bf16[32,1024]{1,0:T(8,128)(2,1)S(1)} %get-tuple-element.17), channel_id=1, source_target_pairs={{1,2},{2,1},{3,4},{4,3},{5,6},{6,5},{7,8},{8,7},{9,10},{10,9},{11,... | collective-permute-start | bytes 196616 | tf_op jit(solution)/shard_map/ppermute | solution.py:330
  5.3 1.9 %collective-permute-start = (bf16[16,1024]{1,0:T(8,128)(2,1)S(1)}, bf16[16,1024]{1,0:T(8,128)(2,1)S(1)}, u32[]{:S(2)}, u32[]{:S(2)}) collective-permute-start(bf16[16,1024]{1,0:T(8,128)(2,1)S(1)} %get-tuple-element.16), channel_id=1, source_target_pairs={{0,1},{1,0},{2,3},{3,2},{4,5},{5,4},{6,7},{7,6},{8,9},{9,8},{10,11... | collective-permute-start | bytes 98312 | tf_op jit(solution)/shard_map/ppermute | solution.py:331
  7.2 0.0 copy-done.7
  7.2 0.0 copy-done.2
  7.2 0.0 copy-done.10
  7.2 1.2 %shard_map.118 = (bf16[16,128,128]{2,1,0:T(8,128)(2,1)S(1)}, f32[32,1024]{1,0:T(8,128)S(1)}, bf16[64,160]{1,0:T(8,128)(2,1)S(1)}) custom-call(f32[1,1,25]{2,1,0:T(1,128)S(1)} %copy-done.10, bf16[1,256,1024]{2,1,0:T(8,128)(2,1)S(1)} %copy-done.7, bf16[1,256,1024]{2,1,0:T(8,128)(2,1)S(1)} %copy-done.2), custom_call_target="tpu_custom_call" | custom-call | flops 1024 | bytes 1024 | tf_op jit(solution)/shard_map/pallas_call | solution.py:295
  8.4 0.0 collective-permute-done.inner_ref
  8.4 0.2 collective-permute-done.1.outer_ref
  8.7 0.0 copy-done.11
  8.7 0.0 copy-done.8
  8.7 0.0 copy-start.9
  8.7 1.0 %shard_map.120 = bf16[16,2,128,128]{3,2,1,0:T(8,128)(2,1)S(1)} custom-call(bf16[64,160]{1,0:T(8,128)(2,1)S(1)} %get-tuple-element.15.bands_ref, s32[1,1,2,16]{3,2,1,0:T(2,128)S(1)} %bitcast.2, s32[1,1,16]{2,1,0:T(1,128)S(1)} %copy-done.11, bf16[16,1024]{1,0:T(8,128)(2,1)S(1)} %collective-permute-done.inner_ref, ...), custom_call_target="tpu_custom_call" | custom-call | flops 1048576 | bytes 2097152 | tf_op jit(solution)/shard_map/pallas_call | solution.py:295
  9.7 0.0 copy-start.1
  9.7 0.0 copy-start
  9.7 0.0 copy-start.3
  9.7 0.0 copy-start.4
  9.7 19.5 %all_to_all.5.in_ref = bf16[16,2,128,128]{3,2,1,0:T(8,128)(2,1)S(1)} all-to-all(bf16[16,2,128,128]{3,2,1,0:T(8,128)(2,1)S(1)} %shard_map.120), channel_id=1, replica_groups=mesh['sec'=32,'tile'=16] {'tile'}, dimensions={0} | all-to-all | bytes 2097152 | tf_op jit(solution)/shard_map/all_to_all | solution.py:358
  29.3 0.0 copy-done.9
  29.3 0.8 %shard_map.121 = (bf16[11,128,128]{2,1,0:T(8,128)(2,1)S(1)}, f32[5,128,128]{2,1,0:T(8,128)S(1)}) custom-call(s32[1,1,2,16]{3,2,1,0:T(2,128)S(1)} %bitcast.3, bf16[16,2,128,128]{3,2,1,0:T(8,128)(2,1)S(1)} %all_to_all.5.in_ref), custom_call_target="tpu_custom_call" | custom-call | flops 1048576 | bytes 2097152 | tf_op jit(solution)/shard_map/pallas_call | solution.py:295
  30.1 3.8 %collective-permute-start.2 = (bf16[11,128,128]{2,1,0:T(8,128)(2,1)S(1)}, bf16[11,128,128]{2,1,0:T(8,128)(2,1)S(1)}, u32[]{:S(2)}, u32[]{:S(2)}) collective-permute-start(bf16[11,128,128]{2,1,0:T(8,128)(2,1)S(1)} %get-tuple-element.20.a_ref), channel_id=1, source_target_pairs={{0,16},{16,32},{32,48},{48,64},{64,80},{80,96},{96,112},{112,128},... | collective-permute-start | bytes 1081352 | tf_op jit(solution)/shard_map/ppermute | solution.py:380
  34.0 0.0 copy-done.1
  34.0 0.0 copy-start.5
  34.0 0.0 copy-start.6
  34.0 0.1 shard_map.124
  34.1 3.9 %collective-permute-start.4 = (bf16[5,128,128]{2,1,0:T(8,128)(2,1)S(1)}, bf16[5,128,128]{2,1,0:T(8,128)(2,1)S(1)}, u32[]{:S(2)}, u32[]{:S(2)}) collective-permute-start(bf16[5,128,128]{2,1,0:T(8,128)(2,1)S(1)} %get-tuple-element.22.b_ref), channel_id=1, source_target_pairs={{0,16},{16,32},{32,48},{48,64},{64,80},{80,96},{96,112},{112,128},... | collective-permute-start | bytes 491528 | tf_op jit(solution)/shard_map/ppermute | solution.py:381
  38.0 2.8 %collective-permute-start.3 = (bf16[64,128]{1,0:T(8,128)(2,1)S(1)}, bf16[64,128]{1,0:T(8,128)(2,1)S(1)}, u32[]{:S(2)}, u32[]{:S(2)}) collective-permute-start(bf16[64,128]{1,0:T(8,128)(2,1)S(1)} %get-tuple-element.23), channel_id=1, source_target_pairs={{1,0},{2,1},{3,2},{4,3},{5,4},{6,5},{7,6},{8,7},{9,8},{10,9},{11,1... | collective-permute-start | bytes 49160 | tf_op jit(solution)/shard_map/ppermute | solution.py:382
  40.8 2.3 %collective-permute-start.6 = (bf16[64,128]{1,0:T(8,128)(2,1)S(1)}, bf16[64,128]{1,0:T(8,128)(2,1)S(1)}, u32[]{:S(2)}, u32[]{:S(2)}) collective-permute-start(bf16[64,128]{1,0:T(8,128)(2,1)S(1)} %get-tuple-element.24), channel_id=1, source_target_pairs={{1,0},{2,1},{3,2},{4,3},{5,4},{6,5},{7,6},{8,7},{9,8},{10,9},{11,1... | collective-permute-start | bytes 49160 | tf_op jit(solution)/shard_map/ppermute | solution.py:385
  43.2 3.3 %collective-permute-start.5 = (bf16[64,128]{1,0:T(8,128)(2,1)S(1)}, bf16[64,128]{1,0:T(8,128)(2,1)S(1)}, u32[]{:S(2)}, u32[]{:S(2)}) collective-permute-start(bf16[64,128]{1,0:T(8,128)(2,1)S(1)} %get-tuple-element.23), channel_id=1, source_target_pairs={{1,16},{2,17},{3,18},{4,19},{5,20},{6,21},{7,22},{8,23},{9,24},{10... | collective-permute-start | bytes 49160 | tf_op jit(solution)/shard_map/ppermute | solution.py:384
  46.4 0.0 copy-done
  46.5 0.0 copy-done.3
  46.5 0.0 copy-done.4
  46.5 0.9 %shard_map.122.cur_ref = bf16[256,1408]{1,0:T(8,128)(2,1)S(1)} custom-call(bf16[11,128,128]{2,1,0:T(8,128)(2,1)S(1)} %get-tuple-element.20.a_ref, bf16[256,256]{1,0:T(8,128)(2,1)S(1)} %copy-done.4, bf16[256,256]{1,0:T(8,128)(2,1)S(1)} %copy-done.3, bf16[1408,128]{1,0:T(8,128)(2,1)S(1)} %copy-done), custom_call_target="tpu_custom_call" | custom-call | flops 1024 | bytes 1024 | tf_op jit(solution)/shard_map/pallas_call | solution.py:295
  47.4 0.0 collective-permute-done.3.rim_ref
  47.4 0.8 %shard_map.125.cur_ref = bf16[256,896]{1,0:T(8,128)(2,1)S(1)} custom-call(bf16[11,128,128]{2,1,0:T(8,128)(2,1)S(1)} %get-tuple-element.20.a_ref, bf16[5,128,128]{2,1,0:T(8,128)(2,1)S(1)} %get-tuple-element.22.b_ref, bf16[64,128]{1,0:T(8,128)(2,1)S(1)} %collective-permute-done.3.rim_ref, bf16[256,256]{1,0:T(8,128)(2,1)S(1)} %copy-done.4, ...), custom_call_target="tpu_custom_call" | custom-call | flops 1024 | bytes 1024 | tf_op jit(solution)/shard_map/pallas_call | solution.py:295
  48.2 3.2 %collective-permute-done.2.a_ref = bf16[11,128,128]{2,1,0:T(8,128)(2,1)S(1)} collective-permute-done((bf16[11,128,128]{2,1,0:T(8,128)(2,1)S(1)}, bf16[11,128,128]{2,1,0:T(8,128)(2,1)S(1)}, u32[]{:S(2)}, u32[]{:S(2)}) %collective-permute-start.2) | collective-permute-done | bytes 360480 | tf_op jit(solution)/shard_map/ppermute | solution.py:380
  51.4 0.0 copy-done.5
  51.4 0.0 copy-done.6
  51.4 2.6 %shard_map.123.held = f32[1,32,128,128]{3,2,1,0:T(8,128)} custom-call(bf16[256,1408]{1,0:T(8,128)(2,1)S(1)} %shard_map.122.cur_ref, bf16[11,128,128]{2,1,0:T(8,128)(2,1)S(1)} %collective-permute-done.2.a_ref, bf16[16,128,128]{2,1,0:T(8,128)(2,1)S(1)} %copy-done.1, bf16[256,256]{1,0:T(8,128)(2,1)S(1)} %copy-done.4, bf16[256,256]{1,0:T(8,128)(2,1)S(1)} %copy-done.3, ...), custom_call_target="tpu_custom_call" | custom-call | flops 1024 | bytes 1024 | tf_op jit(solution)/shard_map/pallas_call | solution.py:295
  54.0 0.0 collective-permute-done.6.border_ref
  54.0 0.1 collective-permute-done.5.rim_ref
  54.1 0.6 collective-permute-done.4.b_ref
  54.7 2.2 %shard_map.126 = f32[1,32,128,128]{3,2,1,0:T(8,128)} custom-call(f32[1,32,128,128]{3,2,1,0:T(8,128)} %shard_map.123.held, bf16[256,896]{1,0:T(8,128)(2,1)S(1)} %shard_map.125.cur_ref, bf16[11,128,128]{2,1,0:T(8,128)(2,1)S(1)} %collective-permute-done.2.a_ref, bf16[5,128,128]{2,1,0:T(8,128)(2,1)S(1)} %collective-permute-done.4.b_ref, ...), custom_call_target="tpu_custom_call", output_to_operand_aliasing={{}: (0, {})} | custom-call | flops 1073741824 | bytes 4194304 | tf_op jit(solution)/shard_map/pallas_call | solution.py:295
Async XLA Ops:
  0.0 7.2 %copy-start.7 = (bf16[1,256,1024]{2,1,0:T(8,128)(2,1)S(1)}, bf16[1,256,1024]{2,1,0:T(8,128)(2,1)}, u32[]{:S(2)}) copy-start(bf16[1,256,1024]{2,1,0:T(8,128)(2,1)} %image.1) | copy-start | bytes 1572868
  0.0 7.2 %copy-start.2 = (bf16[1,256,1024]{2,1,0:T(8,128)(2,1)S(1)}, bf16[1,256,1024]{2,1,0:T(8,128)(2,1)}, u32[]{:S(2)}) copy-start(bf16[1,256,1024]{2,1,0:T(8,128)(2,1)} %weight_ref.3) | copy-start | bytes 1572868
  0.0 7.2 %copy-start.10 = (f32[1,1,25]{2,1,0:T(1,128)S(1)}, f32[1,1,25]{2,1,0:T(1,128)}, u32[]{:S(2)}) copy-start(f32[1,1,25]{2,1,0:T(1,128)} %taps_ref.1) | copy-start | bytes 304
  0.0 8.7 %copy-start.11 = (s32[1,1,16]{2,1,0:T(1,128)S(1)}, s32[1,1,16]{2,1,0:T(1,128)}, u32[]{:S(2)}) copy-start(s32[1,1,16]{2,1,0:T(1,128)} %counts.1) | copy-start | bytes 196
  0.0 8.7 %copy-start.8 = (s32[1,1,16,2]{2,3,1,0:T(2,128)S(1)}, s32[1,1,16,2]{2,3,1,0:T(2,128)}, u32[]{:S(2)}) copy-start(s32[1,1,16,2]{2,3,1,0:T(2,128)} %param.15) | copy-start | bytes 388
  1.0 7.7 %collective-permute-start.1 = (bf16[32,1024]{1,0:T(8,128)(2,1)S(1)}, bf16[32,1024]{1,0:T(8,128)(2,1)S(1)}, u32[]{:S(2)}, u32[]{:S(2)}) collective-permute-start(bf16[32,1024]{1,0:T(8,128)(2,1)S(1)} %get-tuple-element.17), channel_id=1, source_target_pairs={{1,2},{2,1},{3,4},{4,3},{5,6},{6,5},{7,8},{8,7},{9,10},{10,9},{11,... | collective-permute-start | bytes 196616 | tf_op jit(solution)/shard_map/ppermute | solution.py:330
  5.3 3.2 %collective-permute-start = (bf16[16,1024]{1,0:T(8,128)(2,1)S(1)}, bf16[16,1024]{1,0:T(8,128)(2,1)S(1)}, u32[]{:S(2)}, u32[]{:S(2)}) collective-permute-start(bf16[16,1024]{1,0:T(8,128)(2,1)S(1)} %get-tuple-element.16), channel_id=1, source_target_pairs={{0,1},{1,0},{2,3},{3,2},{4,5},{5,4},{6,7},{7,6},{8,9},{9,8},{10,11... | collective-permute-start | bytes 98312 | tf_op jit(solution)/shard_map/ppermute | solution.py:331
  8.7 20.6 %copy-start.9 = (s32[1,16,1,2]{1,3,2,0:T(2,128)S(1)}, s32[1,16,1,2]{1,3,2,0:T(2,128)}, u32[]{:S(2)}) copy-start(s32[1,16,1,2]{1,3,2,0:T(2,128)} %param.16) | copy-start | bytes 388
  9.7 24.3 %copy-start.1 = (bf16[16,128,128]{2,1,0:T(8,128)(2,1)S(1)}, bf16[16,128,128]{2,1,0:T(8,128)(2,1)}, u32[]{:S(2)}) copy-start(bf16[16,128,128]{2,1,0:T(8,128)(2,1)} %anchor_ref.5) | copy-start | bytes 1572868
  9.7 36.8 %copy-start = (bf16[1408,128]{1,0:T(8,128)(2,1)S(1)}, bf16[1408,128]{1,0:T(8,128)(2,1)}, u32[]{:S(2)}) copy-start(bf16[1408,128]{1,0:T(8,128)(2,1)} %constant.12.clone.refs_2_) | copy-start | bytes 1081348
  9.7 36.8 %copy-start.3 = (bf16[256,256]{1,0:T(8,128)(2,1)S(1)}, bf16[256,256]{1,0:T(8,128)(2,1)}, u32[]{:S(2)}) copy-start(bf16[256,256]{1,0:T(8,128)(2,1)} %constant.11.clone.refs_1_) | copy-start | bytes 393220
  9.7 36.8 %copy-start.4 = (bf16[256,256]{1,0:T(8,128)(2,1)S(1)}, bf16[256,256]{1,0:T(8,128)(2,1)}, u32[]{:S(2)}) copy-start(bf16[256,256]{1,0:T(8,128)(2,1)} %constant.10.clone.refs_0_) | copy-start | bytes 393220
  30.1 21.3 %collective-permute-start.2 = (bf16[11,128,128]{2,1,0:T(8,128)(2,1)S(1)}, bf16[11,128,128]{2,1,0:T(8,128)(2,1)S(1)}, u32[]{:S(2)}, u32[]{:S(2)}) collective-permute-start(bf16[11,128,128]{2,1,0:T(8,128)(2,1)S(1)} %get-tuple-element.20.a_ref), channel_id=1, source_target_pairs={{0,16},{16,32},{32,48},{48,64},{64,80},{80,96},{96,112},{112,128},... | collective-permute-start | bytes 1081352 | tf_op jit(solution)/shard_map/ppermute | solution.py:380
  34.0 17.4 %copy-start.5 = (bf16[256,256]{1,0:T(8,128)(2,1)S(1)}, bf16[256,256]{1,0:T(8,128)(2,1)}, u32[]{:S(2)}) copy-start(bf16[256,256]{1,0:T(8,128)(2,1)} %constant.14.clone.refs_4_) | copy-start | bytes 393220
  34.0 17.4 %copy-start.6 = (bf16[256,256]{1,0:T(8,128)(2,1)S(1)}, bf16[256,256]{1,0:T(8,128)(2,1)}, u32[]{:S(2)}) copy-start(bf16[256,256]{1,0:T(8,128)(2,1)} %constant.13.clone.refs_3_) | copy-start | bytes 393220
  34.1 20.6 %collective-permute-start.4 = (bf16[5,128,128]{2,1,0:T(8,128)(2,1)S(1)}, bf16[5,128,128]{2,1,0:T(8,128)(2,1)S(1)}, u32[]{:S(2)}, u32[]{:S(2)}) collective-permute-start(bf16[5,128,128]{2,1,0:T(8,128)(2,1)S(1)} %get-tuple-element.22.b_ref), channel_id=1, source_target_pairs={{0,16},{16,32},{32,48},{48,64},{64,80},{80,96},{96,112},{112,128},... | collective-permute-start | bytes 491528 | tf_op jit(solution)/shard_map/ppermute | solution.py:381
  38.0 9.4 %collective-permute-start.3 = (bf16[64,128]{1,0:T(8,128)(2,1)S(1)}, bf16[64,128]{1,0:T(8,128)(2,1)S(1)}, u32[]{:S(2)}, u32[]{:S(2)}) collective-permute-start(bf16[64,128]{1,0:T(8,128)(2,1)S(1)} %get-tuple-element.23), channel_id=1, source_target_pairs={{1,0},{2,1},{3,2},{4,3},{5,4},{6,5},{7,6},{8,7},{9,8},{10,9},{11,1... | collective-permute-start | bytes 49160 | tf_op jit(solution)/shard_map/ppermute | solution.py:382
  40.8 13.2 %collective-permute-start.6 = (bf16[64,128]{1,0:T(8,128)(2,1)S(1)}, bf16[64,128]{1,0:T(8,128)(2,1)S(1)}, u32[]{:S(2)}, u32[]{:S(2)}) collective-permute-start(bf16[64,128]{1,0:T(8,128)(2,1)S(1)} %get-tuple-element.24), channel_id=1, source_target_pairs={{1,0},{2,1},{3,2},{4,3},{5,4},{6,5},{7,6},{8,7},{9,8},{10,9},{11,1... | collective-permute-start | bytes 49160 | tf_op jit(solution)/shard_map/ppermute | solution.py:385
  43.2 11.0 %collective-permute-start.5 = (bf16[64,128]{1,0:T(8,128)(2,1)S(1)}, bf16[64,128]{1,0:T(8,128)(2,1)S(1)}, u32[]{:S(2)}, u32[]{:S(2)}) collective-permute-start(bf16[64,128]{1,0:T(8,128)(2,1)S(1)} %get-tuple-element.23), channel_id=1, source_target_pairs={{1,16},{2,17},{3,18},{4,19},{5,20},{6,21},{7,22},{8,23},{9,24},{10... | collective-permute-start | bytes 49160 | tf_op jit(solution)/shard_map/ppermute | solution.py:384
